TPU v7x, 128 devices: a whole 4x4x4 slice. The times are simulated.
128 devices in a mesh: rep: 8 (over z, x_lo), tp: 16 (over y, x_hi, core).
Axes of the slice: x: 4 (x_hi: 2, x_lo: 2; x = x_hi * 2 + x_lo), y: 4, z: 4, core: 2. Of those that a mesh axis runs over, the one named last changes fastest.
Arguments:
- tokens: bfloat16 [1024, 4, 8192], P('rep', None, 'tp'), may hold values from -6 to 6
- query_weight_matrix: bfloat16 [8192, 8192], P(None, 'tp'), may hold values from -0.0625 to 0.0625
- key_value_weight: bfloat16 [8192, 2048], P(None, 'tp'), may hold values from -0.0625 to 0.0625
- adapter_down_factors: bfloat16 [64, 8192, 128], P('rep', 'tp'), may hold values from -0.0625 to 0.0625
- adapter_up_query: bfloat16 [64, 64, 8192], P('rep', None, 'tp'), may hold values from -0.375 to 0.375
- adapter_up_key_value: bfloat16 [64, 64, 2048], P('rep', None, 'tp'), may hold values from -0.375 to 0.375
- storage_slot_adapter: int32 [64], replicated, may hold values from 0 to 63, as said below
- slot_request_adapter: int32 [1024], replicated, may hold values from 0 to 63, as said below
- migration: int32 [1024], replicated, may hold values from 0 to 1023, as said below
- lengths: int32 [1024], P('rep'), may hold values from 1 to 124
- previous_block_table: int32 [1024, 8], P('rep'), may hold values from 0 to 1023, as said below
- moved_block_table: int32 [1024, 8], P('rep'), may hold values from 0 to 1023, as said below
- paged_cache_pool: bfloat16 [8192, 16, 2048], P('rep', None, 'tp'), may hold values from -900 to 900
Outputs:
- attention: bfloat16 [1024, 4, 8192], P('rep', None, 'tp')
- new_pool: bfloat16 [8192, 16, 2048], P('rep', None, 'tp')
Inputs may be any that keep to these rules, and one draw needn't show every extreme that they name: `storage_slot_adapter`: a permutation of all adapters. `slot_request_adapter`: the requests in the new slots of one group name exactly 8 distinct adapters, and at most one of them is stored (slots g * 8 to g * 8 + 7 of storage_slot_adapter for group g) in any one other group. `migration`: a permutation of all requests; at most 8 requests move from one group to any one other group. `previous_block_table`: the rows of the 128 requests of one group name every block 0 to 1023 exactly once. `moved_block_table`: the rows of the 128 new slots of one group name every block 0 to 1023 exactly once.
All inputs are finite; a program needn't handle non-finite values.
Results may differ from a plain program's by a relative error of at most 0.018.
The roundings to bfloat16 on the way count: a program that leaves them out, or rounds other values in their place, can miss the bound.
Values may be sent and summed in bfloat16 or wider, within the bound.
No kernel may reach another device: no remote copies, remote signals or barrier semaphores. Data moves between devices by JAX's collectives and lax.ppermute only.
A program may use at most 128 MiB of HBM per device.

v0:
```python
import math

import jax
import jax.numpy as jnp
from jax import lax
from jax.sharding import PartitionSpec as P

HEAD_SIZE = 128


THETA = 500000.0


def swapped(array, axis, stride):
    return lax.ppermute(array, axis, [(i, i ^ 1 << stride) for i in range(lax.axis_size(axis))])


def rotate(values, positions):
    head_width = values.shape[-1]
    half_width = head_width // 2
    frequency = THETA ** (-(jnp.arange(half_width, dtype=jnp.float32) * 2.0 / head_width))
    angles = positions.astype(jnp.float32)[..., None] * frequency
    cosine = jnp.cos(angles)
    sine_part = jnp.sin(angles)
    lower_half = values[..., :half_width]
    upper_half = values[..., half_width:]
    return jnp.concatenate(
        [
            lower_half * cosine - upper_half * sine_part,
            upper_half * cosine + lower_half * sine_part,
        ],
        axis=-1,
    )


def compact(arrays, cand_ids, wanted, keep_count):
    needed = jnp.any(cand_ids[:, None] == wanted[None, :], axis=1) & (cand_ids >= 0)
    ranking = jnp.cumsum(needed.astype(jnp.int32)) - 1
    chooser = (ranking[None, :] == jnp.arange(keep_count, dtype=jnp.int32)[:, None]) & needed[
        None, :
    ]
    where_from = jnp.sum(
        jnp.where(chooser, jnp.arange(cand_ids.shape[0], dtype=jnp.int32)[None, :], 0), axis=1
    )
    picked_ids = jnp.sum(jnp.where(chooser, cand_ids[None, :], 0), axis=1)
    picked_ids = jnp.where(jnp.any(chooser, axis=1), picked_ids, -1)
    picked = tuple((jnp.take(member, where_from, axis=0) for member in arrays))
    return (picked, picked_ids)


def softmax_rows(scores, visible):
    scores = jnp.where(visible, scores, -1e30)
    top_score = jnp.max(scores, axis=-1, keepdims=True)
    weights = jnp.where(visible, jnp.exp(scores - top_score), 0.0)
    return (weights / jnp.sum(weights, axis=-1, keepdims=True)).astype(jnp.bfloat16)


def body(
    tokens,
    query_weight_matrix,
    key_value_weight,
    adapter_down_factors,
    adapter_up_query,
    adapter_up_key_value,
    storage_slot_adapter,
    slot_request_adapter,
    migration,
    lengths,
    previous_block_table,
    moved_block_table,
    paged_cache_pool,
):
    group_count = lax.axis_size("rep")
    my_group = lax.axis_index("rep")
    my_shard = lax.axis_index("tp")
    local_requests, step_count, local_features = tokens.shape
    capacity = local_requests // (2 * group_count)
    request_count = migration.shape[0]
    resident_adapters = adapter_down_factors.shape[0]
    columns = paged_cache_pool.shape[2]
    page_rows = paged_cache_pool.shape[1]
    block_slots = previous_block_table.shape[1]
    cache_span = block_slots * page_rows
    row_count = local_requests * step_count
    place = jnp.arange(local_requests, dtype=jnp.int32)
    cache_rows = jnp.arange(cache_span, dtype=jnp.int32)
    destination = (
        jnp.zeros((request_count,), jnp.int32)
        .at[migration]
        .set(jnp.arange(request_count, dtype=jnp.int32))
    )
    dest_slot = destination[my_group * local_requests + place]
    dest_group = dest_slot // local_requests
    leaving = dest_group != my_group
    same_dest = (dest_group[:, None] == dest_group[None, :]) & (
        dest_slot[None, :] < dest_slot[:, None]
    )
    out_rank = jnp.sum(same_dest.astype(jnp.int32), axis=1)
    out_slot = dest_group * capacity + out_rank
    buffer_index = jnp.arange(group_count * capacity, dtype=jnp.int32)
    matches = leaving[None, :] & (out_slot[None, :] == buffer_index[:, None])
    filled = jnp.any(matches, axis=1)
    source_row = jnp.sum(jnp.where(matches, place[None, :], 0), axis=1)
    pages = paged_cache_pool[previous_block_table].reshape(local_requests, cache_span, columns)
    dense = jnp.where(
        (cache_rows[None, :] < lengths[:, None])[:, :, None], pages, jnp.zeros((), pages.dtype)
    )
    send_tokens = jnp.where(filled[:, None, None], tokens[source_row], jnp.zeros((), tokens.dtype))
    send_cache = jnp.where(filled[:, None, None], dense[source_row], jnp.zeros((), dense.dtype))
    send_length = jnp.where(filled, lengths[source_row], 0)
    got_tokens, got_cache, got_length = (
        lax.all_to_all(send_tokens, "rep", split_axis=0, concat_axis=0, tiled=True),
        lax.all_to_all(send_cache, "rep", split_axis=0, concat_axis=0, tiled=True),
        lax.all_to_all(send_length, "rep", split_axis=0, concat_axis=0, tiled=True),
    )
    source = migration[my_group * local_requests + place]
    source_group = source // local_requests
    source_local = source % local_requests
    staying = source_group == my_group
    same_source = (source_group[:, None] == source_group[None, :]) & (
        place[None, :] < place[:, None]
    )
    in_rank = jnp.sum(same_source.astype(jnp.int32), axis=1)
    in_slot = jnp.where(staying, 0, source_group * capacity + in_rank)
    moved = jnp.where(staying[:, None, None], tokens[source_local], got_tokens[in_slot])
    cache_now = jnp.where(staying[:, None, None], dense[source_local], got_cache[in_slot])
    length_now = jnp.where(staying, lengths[source_local], got_length[in_slot])
    flat_tokens = moved.reshape(row_count, local_features)
    shard_piece = lax.all_gather(flat_tokens, "tp", axis=1, tiled=True)
    base_q = jnp.dot(shard_piece, query_weight_matrix, preferred_element_type=jnp.float32)
    base_kv = jnp.dot(shard_piece, key_value_weight, preferred_element_type=jnp.float32)
    wanted = lax.dynamic_slice_in_dim(
        slot_request_adapter, my_group * local_requests, local_requests
    )
    every_one = (
        lax.all_gather(adapter_down_factors, "rep", axis=0, tiled=True),
        lax.all_gather(adapter_up_query, "rep", axis=0, tiled=True),
        lax.all_gather(adapter_up_key_value, "rep", axis=0, tiled=True),
    )
    picked, picked_ids = compact(every_one, storage_slot_adapter, wanted, resident_adapters)
    row_adapter = jnp.repeat(wanted, step_count)
    selector = row_adapter[:, None] == picked_ids[None, :]
    spread = jnp.einsum("rd,adk->rak", flat_tokens, picked[0], preferred_element_type=jnp.float32)
    partial_down = jnp.sum(jnp.where(selector[:, :, None], spread, 0.0), axis=1)
    down_factor_rows = lax.psum(partial_down, "tp").astype(jnp.bfloat16)
    rank_size = picked[1].shape[1]
    selector_bf = selector.astype(jnp.bfloat16)
    spread_q = (selector_bf[:, :, None] * down_factor_rows[:, None, :rank_size]).reshape(
        row_count, resident_adapters * rank_size
    )
    spread_kv = (selector_bf[:, :, None] * down_factor_rows[:, None, rank_size:]).reshape(
        row_count, resident_adapters * rank_size
    )
    query_raw = base_q + jnp.dot(
        spread_q,
        picked[1].reshape(resident_adapters * rank_size, -1),
        preferred_element_type=jnp.float32,
    )
    kv_raw = base_kv + jnp.dot(
        spread_kv,
        picked[2].reshape(resident_adapters * rank_size, -1),
        preferred_element_type=jnp.float32,
    )
    positions = length_now[:, None] + jnp.arange(step_count, dtype=jnp.int32)[None, :]
    q_heads = query_raw.shape[1] // HEAD_SIZE
    query = rotate(
        query_raw.reshape(local_requests, step_count, q_heads, HEAD_SIZE), positions[:, :, None]
    ).astype(jnp.bfloat16)
    kv_blocks = columns // HEAD_SIZE
    kv_view = kv_raw.reshape(local_requests, step_count, kv_blocks, HEAD_SIZE)
    block_kind = (my_shard * kv_blocks + jnp.arange(kv_blocks, dtype=jnp.int32)) % 2
    turned = rotate(kv_view, positions[:, :, None])
    fresh = (
        jnp.where((block_kind == 0)[None, None, :, None], turned, kv_view)
        .astype(jnp.bfloat16)
        .reshape(local_requests, step_count, columns)
    )
    for step_at in range(step_count):
        landing = (cache_rows[None, :] == (length_now + step_at)[:, None])[:, :, None]
        cache_now = jnp.where(landing, fresh[:, step_at][:, None, :], cache_now)
    visible_rows = cache_rows[None, None, :] <= positions[:, :, None]
    holds_keys = my_shard % 2 == 0
    partner = swapped(cache_now, "tp", 0)
    key_rows = jnp.where(holds_keys, cache_now, partner)[:, :, None, :]
    value_rows = jnp.where(holds_keys, partner, cache_now)[:, :, None, :]
    kv_heads = key_rows.shape[2]
    grouped = query.reshape(local_requests, step_count, kv_heads, q_heads // kv_heads, HEAD_SIZE)
    scores = jnp.einsum(
        "rsjgd,rpjd->rsjgp", grouped, key_rows, preferred_element_type=jnp.float32
    ) / math.sqrt(HEAD_SIZE)
    probability = softmax_rows(scores, visible_rows[:, :, None, None, :])
    mixed_out = jnp.einsum(
        "rsjgp,rpjd->rsjgd", probability, value_rows, preferred_element_type=jnp.float32
    )
    attention = mixed_out.astype(jnp.bfloat16).reshape(
        local_requests, step_count, q_heads * HEAD_SIZE
    )
    written = (
        jnp.zeros_like(paged_cache_pool)
        .at[moved_block_table.reshape(-1)]
        .set(cache_now.reshape(local_requests * block_slots, page_rows, columns))
    )
    return (attention, written)


def solution(mesh):
    in_specs = (
        P("rep", None, "tp"),
        P(None, "tp"),
        P(None, "tp"),
        P("rep", "tp", None),
        P("rep", None, "tp"),
        P("rep", None, "tp"),
        P(),
        P(),
        P(),
        P("rep"),
        P("rep", None),
        P("rep", None),
        P("rep", None, "tp"),
    )
    out_specs = (P("rep", None, "tp"), P("rep", None, "tp"))
    return jax.shard_map(body, mesh=mesh, in_specs=in_specs, out_specs=out_specs, check_vma=False)
```

profile of v0, /device:TPU:1, one launch (start us, length us, event | category | flops | bytes accessed | tf_op | source)
XLA Modules:
  0.0 579.1 jit_solution(580144888924186052)
XLA Ops:
  9.4 4.3 scatter_custom_fusion
  17.3 6.8 %all-to-all-start = ((s32[8,8,1]{1,2,0:T(1,128)}), s32[8,8,1]{1,2,0:T(1,128)S(1)}, u32[]{:S(2)}, u32[]{:S(2)}) async-start(s32[8,8,1]{1,2,0:T(1,128)} %bitcast.5), calls=%async_computation | async-start | bytes 8192 | tf_op jit(solution)/shard_map/all_to_all | solution.py:114
  24.1 1.6 gather_fusion
  25.7 1.8 gather_fusion.6
  29.0 4.8 all-to-all-start.1
  39.1 4.3 all-to-all-done.1
  43.4 1.8 gather_fusion.7
  47.5 10.5 %gather_fusion.10 = bf16[1024,16,128]{2,1,0:T(8,128)(2,1)} fusion(bf16[1024,16,128]{2,1,0:T(8,128)(2,1)} %param.25, s32[1024]{0:T(1024)S(1)} %broadcast_clamp_fusion), kind=kCustom, calls=%fused_computation.10 | custom fusion | bytes 8392704 | tf_op jit(solution)/shard_map/gather | solution.py:104
  58.1 7.7 %bitcast_select_fusion = bf16[128,128,128]{2,1,0:T(8,128)(2,1)} fusion(pred[128,128]{1,0:T(8,128)(4,1)S(1)} %iota_compare_fusion.1, bf16[128,128,128]{2,1,0:T(8,128)(2,1)} %bitcast.132), kind=kLoop, calls=%fused_computation.21 | loop fusion | flops 2097152 | bytes 8404992 | tf_op jit(solution)/shard_map/jit(_where)/select_n | solution.py:105
  65.8 4.3 gather_fusion.12
  70.2 3.1 broadcast_select_fusion
  73.3 4.4 all-to-all-start.2
  80.9 5.2 gather_fusion.11
  91.4 35.5 %all-to-all-done.2 = bf16[64,128,128]{2,1,0:T(8,128)(2,1)} async-done(((bf16[64,128,128]{2,1,0:T(8,128)(2,1)}), bf16[64,128,128]{2,1,0:T(8,128)(2,1)}, u32[]{:S(2)}, u32[]{:S(2)}) %all-to-all-start.2) | async-done | bytes 2097184 | tf_op jit(solution)/shard_map/all_to_all | solution.py:113
  126.8 4.8 gather_fusion.13
  131.7 2.4 gather_fusion.9
  134.1 111.7 %all-gather.7.cloned.1.call-done = bf16[64,512,128]{2,1,0:T(8,128)(2,1)} async-done(((bf16[8,512,128]{2,1,0:T(8,128)(2,1)}), bf16[64,512,128]{2,1,0:T(8,128)(2,1)}) %all-gather.7.cloned.1.call-update) | async-done | bytes 8388624 | tf_op jit(solution)/shard_map/all_gather | solution.py:136
  245.8 5.1 gather_fusion.8
  250.9 2.4 select_reduce_fusion
  253.3 68.8 %all-reduce.1 = bf16[512,128]{1,0:T(8,128)(2,1)S(1)} all-reduce(f32[512,128]{1,0:T(8,128)S(1)} %select_reduce_fusion), channel_id=1, replica_groups=mesh['rep'=8,'tp'=16] {'tp'}, use_global_device_ids=true, to_apply=%region_11.12 | all-reduce | flops 65536 | bytes 393216 | tf_op jit(solution)/shard_map/psum | solution.py:145
  322.3 7.4 %all-gather.5.cloned.1.call-done = bf16[512,8192]{1,0:T(8,128)(2,1)} async-done(((bf16[512,512]{1,0:T(8,128)(2,1)}), bf16[512,8192]{1,0:T(8,128)(2,1)}) %all-gather.5.cloned.1.call-update) | async-done | bytes 8388624 | tf_op jit(solution)/shard_map/all_gather | solution.py:129
  329.8 5.9 %fusion.79 = f32[512,128]{1,0:T(8,128)S(1)} fusion(bf16[512,8192]{1,0:T(8,128)(2,1)} %all-gather.5.cloned.1.call-done, bf16[8192,128]{1,0:T(8,128)(2,1)S(1)} %copy-done), kind=kOutput, calls=%fused_computation.179 | convolution fusion | flops 1073741824 | bytes 10747904 | tf_op jit(solution)/shard_map/dot_general | solution.py:131
  337.6 11.0 %select_select_fusion.1 = bf16[128,128,128]{2,1,0:T(8,128)(2,1)} fusion(bf16[128,128,128]{2,1,0:T(8,128)(2,1)S(1)} %copy-done.3, bf16[128,128,128]{2,1,0:T(8,128)(2,1)S(1)} %copy-done.4, pred[128]{0:T(512)(128)(4,1)S(1)} %get-tuple-element.8, pred[128,128]{1,0:T(8,128)(4,1)S(1)} %get-tuple-element.39, pred[128,128]{1,0:T(8,128)(4,1)S(1)} %get-tuple-element.41, ...), kind=kLoop, calls=%fused_computation.25 | loop fusion | flops 10485760 | bytes 12779648 | tf_op jit(solution)/shard_map/jit(_where)/select_n | solution.py:180
  349.1 2.2 multiply_cosine_fusion.1
  351.3 68.2 %all-gather.11.cloned.1.call-done = bf16[64,64,512]{2,1,0:T(8,128)(2,1)} async-done(((bf16[8,64,512]{2,1,0:T(8,128)(2,1)}), bf16[64,64,512]{2,1,0:T(8,128)(2,1)}) %all-gather.11.cloned.1.call-update) | async-done | bytes 4194320 | tf_op jit(solution)/shard_map/all_gather | solution.py:137
  419.5 2.9 gather_fusion.14
  423.0 9.5 %convolution_add_fusion = f32[512,512]{1,0:T(8,128)S(1)} fusion(f32[512,512]{1,0:T(8,128)S(1)} %convolution_bitcast_fusion, bf16[512,8192]{1,0:T(8,128)(2,1)} %all-gather.5.cloned.1.call-done, bf16[8192,512]{1,0:T(8,128)(2,1)} %param.14), kind=kOutput, calls=%fused_computation.35 | convolution fusion | flops 4295229440 | bytes 18874368 | tf_op jit(solution)/shard_map/dot_general | solution.py:130
  433.1 14.6 %select_select_fusion = bf16[1024,16,128]{2,1,0:T(8,128)(2,1)} fusion(bf16[1024,16,128]{2,1,0:T(8,128)(2,1)} %bitcast.130, bf16[1024,16,128]{2,1,0:T(8,128)(2,1)} %bitcast.131, pred[1024]{0:T(1024)(128)(4,1)S(1)} %copy-done.14, pred[1024,16]{1,0:T(8,128)(4,1)S(1)} %get-tuple-element.26, pred[1024,16]{1,0:T(8,128)(4,1)S(1)} %get-tuple-element.27, ...), kind=kLoop, calls=%fused_computation.22 | loop fusion | flops 10485760 | bytes 13698048 | tf_op jit(solution)/shard_map/jit(_where)/select_n | solution.py:180
  447.7 2.6 broadcast_in_dim.384
  450.3 110.4 %scatter_fusion = bf16[1024,16,128]{2,1,0:T(8,128)(2,1)} fusion(bf16[1024,16,128]{2,1,0:T(8,128)(2,1)} %broadcast_in_dim.384, s32[1024]{0:T(1024)S(1)} %bitcast.135, bf16[1024,16,128]{2,1,0:T(8,128)(2,1)} %select_select_fusion), kind=kCustom, calls=%fused_computation.16 | custom fusion | bytes 12587008 | tf_op jit(solution)/shard_map/scatter | solution.py:201
  561.5 4.9 fusion.78
  567.8 3.8 fusion.17
  (147 shorter events, 29.9 us)
Async XLA Ops:
  7.2 322.6 %copy-start = (bf16[8192,128]{1,0:T(8,128)(2,1)S(1)}, bf16[8192,128]{1,0:T(8,128)(2,1)}, u32[]{:S(2)}) copy-start(bf16[8192,128]{1,0:T(8,128)(2,1)} %param.15) | copy-start | bytes 6291460
  7.2 26.7 %copy-start.2 = (s32[128]{0:T(128)S(1)}, s32[128]{0:T(128)}, u32[]{:S(2)}) copy-start(s32[128]{0:T(128)} %param.22) | copy-start | bytes 1540
  7.2 28.0 %copy-start.6 = (bf16[128,4,512]{2,1,0:T(4,128)(2,1)S(1)}, bf16[128,4,512]{2,1,0:T(4,128)(2,1)}, u32[]{:S(2)}) copy-start(bf16[128,4,512]{2,1,0:T(4,128)(2,1)} %param.13) | copy-start | bytes 1572868
  7.2 124.4 %all-gather.9.cloned.1.call-start = ((), (), s32[]{:S(2)}) async-start(), calls=%async_computation.5 | async-start | bytes 1179648 | tf_op jit(solution)/shard_map/all_gather | solution.py:138
  7.9 237.8 %all-gather.7.cloned.1.call-start = ((), (), s32[]{:S(2)}) async-start(), calls=%async_computation.4 | async-start | bytes 9437184 | tf_op jit(solution)/shard_map/all_gather | solution.py:136
  17.3 11.7 %all-to-all-start = ((s32[8,8,1]{1,2,0:T(1,128)}), s32[8,8,1]{1,2,0:T(1,128)S(1)}, u32[]{:S(2)}, u32[]{:S(2)}) async-start(s32[8,8,1]{1,2,0:T(1,128)} %bitcast.5), calls=%async_computation | async-start | bytes 8192 | tf_op jit(solution)/shard_map/all_to_all | solution.py:114
  27.8 19.6 %copy-start.16 = (s32[128,8]{0,1:T(8,128)S(1)}, s32[128,8]{0,1:T(8,128)}, u32[]{:S(2)}) copy-start(s32[128,8]{0,1:T(8,128)} %param.23) | copy-start | bytes 12292
  28.7 29.3 %copy-start.12 = (s32[1024]{0:T(1024)}, s32[1024]{0:T(1024)S(1)}, u32[]{:S(2)}) copy-start(s32[1024]{0:T(1024)S(1)} %pad_clamp_fusion.1) | copy-start | bytes 12292
  29.0 14.4 %all-to-all-start.1 = ((bf16[64,4,512]{2,1,0:T(4,128)(2,1)}), bf16[64,4,512]{2,1,0:T(4,128)(2,1)S(1)}, u32[]{:S(2)}, u32[]{:S(2)}) async-start(bf16[64,4,512]{2,1,0:T(4,128)(2,1)} %broadcast_select_fusion.2), calls=%async_computation.1 | async-start | bytes 524288 | tf_op jit(solution)/shard_map/all_to_all | solution.py:112
  33.9 295.9 %all-gather.5.cloned.1.call-start = ((), (), s32[]{:S(2)}) async-start(), calls=%async_computation.3 | async-start | bytes 8912896 | tf_op jit(solution)/shard_map/all_gather | solution.py:129
  38.9 49.3 %copy-start.13 = (s32[128]{0:T(128)}, s32[128]{0:T(128)S(1)}, u32[]{:S(2)}) copy-start(s32[128]{0:T(128)S(1)} %get-tuple-element.6) | copy-start | bytes 1540
  70.2 8.9 %copy-start.18 = (s32[64]{0:T(128)S(1)}, s32[64]{0:T(128)}, u32[]{:S(2)}) copy-start(s32[64]{0:T(128)} %param.19) | copy-start | bytes 772
  73.3 53.5 %all-to-all-start.2 = ((bf16[64,128,128]{2,1,0:T(8,128)(2,1)}), bf16[64,128,128]{2,1,0:T(8,128)(2,1)}, u32[]{:S(2)}, u32[]{:S(2)}) async-start(bf16[64,128,128]{2,1,0:T(8,128)(2,1)} %broadcast_select_fusion), calls=%async_computation.2 | async-start | bytes 4194304 | tf_op jit(solution)/shard_map/all_to_all | solution.py:113
  77.7 341.8 %all-gather.11.cloned.1.call-start = ((), (), s32[]{:S(2)}) async-start(), calls=%async_computation.6 | async-start | bytes 4718592 | tf_op jit(solution)/shard_map/all_gather | solution.py:137
  79.7 166.1 %copy-start.11 = (s32[1024]{0:T(1024)}, s32[1024]{0:T(1024)S(1)}, u32[]{:S(2)}) copy-start(s32[1024]{0:T(1024)S(1)} %pad_clamp_fusion) | copy-start | bytes 12292
  80.9 5.4 copy-start.15
  91.3 159.6 %copy-start.5 = (bf16[512,512]{1,0:T(8,128)(2,1)S(1)}, bf16[512,512]{1,0:T(8,128)(2,1)}, u32[]{:S(2)}) copy-start(bf16[512,512]{1,0:T(8,128)(2,1)} %broadcast_select_fusion.1) | copy-start | bytes 1572868
  91.3 159.5 %copy-start.17 = (pred[512,8]{0,1:T(8,128)(4,1)S(1)}, pred[512,8]{0,1:T(8,128)(4,1)}, u32[]{:S(2)}) copy-start(pred[512,8]{0,1:T(8,128)(4,1)} %get-tuple-element.30) | copy-start | bytes 12292
  322.3 13.4 %copy-start.8 = (bf16[8,64,128]{2,1,0:T(8,128)(2,1)S(1)}, bf16[8,64,128]{2,1,0:T(8,128)(2,1)}, u32[]{:S(2)}) copy-start(bf16[8,64,128]{2,1,0:T(8,128)(2,1)} %gather_fusion.9) | copy-start | bytes 393220
  322.3 13.4 %copy-start.9 = (bf16[512,8]{0,1:T(8,128)(2,1)S(1)}, bf16[512,8]{0,1:T(8,128)(2,1)}, u32[]{:S(2)}) copy-start(bf16[512,8]{0,1:T(8,128)(2,1)} %get-tuple-element.29) | copy-start | bytes 24580
  322.3 13.4 %copy-start.20 = (pred[8]{0:T(512)(128)(4,1)S(1)}, pred[8]{0:T(512)(128)(4,1)}, u32[]{:S(2)}) copy-start(pred[8]{0:T(512)(128)(4,1)} %compare_and_fusion) | copy-start | bytes 28
  322.3 13.9 %copy-start.19 = (f32[64]{0:T(128)S(1)}, f32[64]{0:T(128)}, u32[]{:S(2)}) copy-start(f32[64]{0:T(128)} %negate_power_fusion) | copy-start | bytes 772
  329.8 7.8 %copy-start.3 = (bf16[128,128,128]{2,1,0:T(8,128)(2,1)S(1)}, bf16[128,128,128]{2,1,0:T(8,128)(2,1)}, u32[]{:S(2)}) copy-start(bf16[128,128,128]{2,1,0:T(8,128)(2,1)} %gather_fusion.11) | copy-start | bytes 12582916
  329.8 7.8 %copy-start.4 = (bf16[128,128,128]{2,1,0:T(8,128)(2,1)S(1)}, bf16[128,128,128]{2,1,0:T(8,128)(2,1)}, u32[]{:S(2)}) copy-start(bf16[128,128,128]{2,1,0:T(8,128)(2,1)} %gather_fusion.13) | copy-start | bytes 12582916
  337.6 11.5 %copy-start.7 = (f32[128,4]{1,0:T(8,128)S(1)}, f32[128,4]{1,0:T(8,128)}, u32[]{:S(2)}) copy-start(f32[128,4]{1,0:T(8,128)} %copy.44) | copy-start | bytes 6148
  337.6 84.9 %copy-start.10 = (bf16[512,8]{0,1:T(8,128)(2,1)S(1)}, bf16[512,8]{0,1:T(8,128)(2,1)}, u32[]{:S(2)}) copy-start(bf16[512,8]{0,1:T(8,128)(2,1)} %get-tuple-element.29) | copy-start | bytes 24580
  337.6 84.9 %copy-start.21 = (pred[8]{0:T(512)(128)(4,1)S(1)}, pred[8]{0:T(512)(128)(4,1)}, u32[]{:S(2)}) copy-start(pred[8]{0:T(512)(128)(4,1)} %compare_and_fusion) | copy-start | bytes 28
  348.6 212.9 %collective-permute-start = (bf16[128,128,128]{2,1,0:T(8,128)(2,1)}, bf16[128,128,128]{2,1,0:T(8,128)(2,1)}, u32[]{:S(2)}, u32[]{:S(2)}) collective-permute-start(bf16[128,128,128]{2,1,0:T(8,128)(2,1)} %select_select_fusion.1), channel_id=1, source_target_pairs={{0,1},{1,0},{2,3},{3,2},{4,5},{5,4},{6,7},{7,6},{8,9},{9,8},{10,11... | collective-permute-start | bytes 12582920 | tf_op jit(solution)/shard_map/ppermute | solution.py:15
  423.0 10.1 %copy-start.14 = (pred[1024]{0:T(1024)(128)(4,1)S(1)}, pred[1024]{0:T(1024)(128)(4,1)}, u32[]{:S(2)}) copy-start(pred[1024]{0:T(1024)(128)(4,1)} %broadcast_in_dim.402) | copy-start | bytes 3076
  567.8 4.8 copy-start.1
Sparse Core Ops, SparseCore 0:
  9.7 40.6 all-gather.8
  52.0 193.7 all-gather.6
  248.7 81.0 all-gather.4
  331.3 88.1 all-gather.10
where the time goes:
time: 584 us; the launch traced here: 579 us
  waiting for transfers between devices  229 us (39%)
  local copies, waits for them, and re-layouts  172 us (29%)
  blocking collectives  68.8 us (12%)
  other arithmetic  50.5 us (9%)
  matrix products  27.3 us (5%)
  starting transfers between devices  16.4 us (3%)
  between operations  14.5 us (2%)
    all_gather x1, waiting for transfers between devices, body(): lax.all_gather(adapter_down_factors, 'rep', axis=0, tiled=True)  112 us
    scatter x1, local copies, waits for them, and re-layouts, body(): written = jnp.zeros_like(paged_cache_pool).at[moved_block_table.reshape(-...  110 us
    psum x1, blocking collectives, body(): down_factor_rows = lax.psum(partial_down, 'tp').astype(jnp.bfloat16)  68.8 us
    all_gather x1, waiting for transfers between devices, body(): lax.all_gather(adapter_up_query, 'rep', axis=0, tiled=True)  68.2 us
    all_to_all x1, waiting for transfers between devices, body(): lax.all_to_all(send_cache, 'rep', split_axis=0, concat_axis=0, tiled=True)  35.5 us
    select_n x2, other arithmetic, body(): cache_now = jnp.where(landing, fresh[:, step_at][:, None, :], cache_now)  25.6 us
  transfers between devices with their start and end apart: 8, of which 6 were waited for; matrix products, arithmetic and copies ran while one was open for 41% of the time, Pallas kernels for 0%

commit v1 on v0

v1 whole, which is shorter than its diff:
```python
import functools
import math

import jax
import jax.numpy as jnp
from jax import lax
from jax.experimental import pallas as pl
from jax.experimental.pallas import tpu as pltpu
from jax.sharding import PartitionSpec as P

HEAD = 128
THETA = 500000.0
MIB = 1 << 20

F32 = jnp.float32
BF16 = jnp.bfloat16
I32 = jnp.int32


def iota(shape, axis):
    return lax.broadcasted_iota(I32, shape, axis)


def col_to_row(col):
    n = col.shape[0]
    return jnp.sum(jnp.where(iota((n, n), 0) == iota((n, n), 1), col, 0), axis=0, keepdims=True)


def row_to_col(row, n, stretch=1):
    w = row.shape[1]
    return jnp.sum(
        jnp.where(iota((n, w), 1) == iota((n, w), 0) // stretch, row, 0), axis=1, keepdims=True
    )


def below(mask):
    n = mask.shape[1]
    tri = (iota((n, n), 0) < iota((n, n), 1)).astype(BF16)
    return jnp.dot(mask.astype(BF16), tri, preferred_element_type=F32).astype(I32)


def plan_kernel(me_ref, mig_ref, sra_ref, ssa_ref, len_ref, tok_ref, send_ref, own_ref, cand_ref, meta_ref):
    r = me_ref[0]
    groups, per = mig_ref.shape
    half = per // 2
    mig = mig_ref[...]
    grp, loc = mig // per, mig % per
    drow = iota((groups, per), 0)
    out_mask = ((grp == r) & (drow != r)).astype(I32)
    mine = jnp.sum(jnp.where(drow == r, mig, 0), axis=0, keepdims=True)
    g_in, loc_in = mine // per, mine % per
    in_mask = (g_in == drow).astype(I32)
    ranks = below(jnp.concatenate([out_mask, in_mask], axis=0))
    out_rank, in_ranks = ranks[:groups], ranks[groups:]
    in_rank = jnp.sum(in_mask * in_ranks, axis=0, keepdims=True)
    stay = g_in == r

    parts = []
    for d in range(groups):
        hit = (out_mask[d : d + 1] == 1) & (out_rank[d : d + 1] == iota((groups, per), 0))
        parts.append(jnp.sum(jnp.where(hit, loc[d : d + 1] + 1, 0), axis=1, keepdims=True))
    src_col = jnp.concatenate(parts, axis=0) - 1
    src_row = col_to_row(src_col)

    count = jnp.sum(jnp.where(drow == r, 0, in_mask), axis=1, keepdims=True)
    lane_u = iota((groups, half), 1)
    count_u = jnp.sum(jnp.where(iota((groups, half), 0) == lane_u // groups, count, 0), axis=0, keepdims=True)
    free = (lane_u[:1] % groups >= count_u).astype(I32)
    free_rank = jnp.where(free == 1, below(free), -1)
    free_col = row_to_col(free_rank, half)
    extra = jnp.sum(
        jnp.where(free_col == in_rank - half, iota((half, per), 0), 0), axis=0, keepdims=True
    )
    place = jnp.where(
        stay, jnp.where(in_rank < half, in_rank, half + extra), half + groups * g_in + in_rank
    )
    sel = place == iota((per, per), 0)

    def placed(row):
        return jnp.sum(jnp.where(sel, row, 0), axis=1, keepdims=True)

    slot_row = col_to_row(placed(iota((1, per), 1)))
    loc_row = col_to_row(placed(jnp.where(stay, loc_in, -1)))

    drow_sra = iota(sra_ref.shape, 0)
    sra = sra_ref[...]
    wanted = jnp.sum(jnp.where(drow_sra == r, sra, 0), axis=0, keepdims=True)
    ssa_col = row_to_col(ssa_ref[...], half)
    store = jnp.sum(jnp.where(ssa_col == wanted, iota((half, per), 0), 0), axis=0, keepdims=True)
    cand = jnp.where(store // groups == r, store % groups, groups + store // groups)
    cand_row = col_to_row(placed(cand))
    rows = per * 4
    cand_ref[...] = jnp.broadcast_to(row_to_col(cand_row, rows, 4), (rows, HEAD)).astype(BF16)
    picks = jnp.zeros((groups, 1), I32)
    for i in range(groups):
        mine_id = jnp.sum(jnp.where(iota((1, half), 1) == r * groups + i, ssa_ref[...], 0))
        used = jnp.max((sra == mine_id).astype(I32), axis=1, keepdims=True)
        picks = jnp.maximum(picks, used * i)
    pick_row = jnp.sum(
        jnp.where(iota((groups, per), 0) == iota((groups, per), 1), picks, 0), axis=0, keepdims=True
    )

    len_col = jnp.broadcast_to(row_to_col(len_ref[...], rows, 4), (rows, HEAD))
    tok = jnp.concatenate([tok_ref[...], len_col.astype(F32).astype(BF16)], axis=1)

    def rows_of(row, n):
        base = row_to_col(row, n, 4)
        at = 4 * base + iota((n, 1), 0) % 4
        pick = (jnp.broadcast_to(at, (n, rows)) == iota((n, rows), 1)) & (base >= 0)
        return jnp.dot(
            jnp.where(pick, 1.0, 0.0).astype(BF16), tok, preferred_element_type=F32
        ).astype(BF16)

    send_ref[...] = rows_of(src_row, rows // 2)
    own_ref[...] = rows_of(loc_row, rows)
    src_wide = jnp.sum(
        jnp.where(iota((half, per), 0) == iota((half, per), 1), src_col, 0), axis=0, keepdims=True
    )
    zero = jnp.zeros((groups - 4, per), I32)
    meta_ref[...] = jnp.concatenate([slot_row, loc_row, src_wide, pick_row, zero], axis=0)


def vspec():
    return pl.BlockSpec(memory_space=pltpu.VMEM)


def sspec():
    return pl.BlockSpec(memory_space=pltpu.SMEM)


def params(mib):
    return pltpu.CompilerParams(vmem_limit_bytes=mib * MIB)


def sds(shape, dtype):
    return jax.ShapeDtypeStruct(shape, dtype)


def plan(me, mig, sra, ssa, lengths, tok):
    rows = tok.shape[0]
    return pl.pallas_call(
        plan_kernel,
        out_shape=(
            sds((rows // 2, 640), BF16),
            sds((rows, 640), BF16),
            sds((rows, HEAD), BF16),
            sds((8, HEAD), I32),
        ),
        in_specs=[sspec()] + [vspec()] * 5,
        out_specs=(vspec(),) * 4,
        compiler_params=params(24),
        name="plan",
    )(me, mig, sra, ssa, lengths, tok)


def pack_adapters_kernel(meta_ref, *refs):
    n = len(refs) // 2
    for src, dst in zip(refs[:n], refs[n:]):
        dst[...] = src[...]


def pack_adapters(meta, down, up_q, up_kv, up_kv_other):
    arrays = (down, up_q, up_kv, up_kv_other)

    def spec_in(a):
        return pl.BlockSpec((1,) + a.shape[1:], lambda d, meta: (meta[3, d], 0, 0))

    def spec_out(a):
        return pl.BlockSpec((1,) + a.shape[1:], lambda d, meta: (d, 0, 0))

    return pl.pallas_call(
        pack_adapters_kernel,
        grid_spec=pltpu.PrefetchScalarGridSpec(
            num_scalar_prefetch=1,
            grid=(8,),
            in_specs=[spec_in(a) for a in arrays],
            out_specs=tuple(spec_out(a) for a in arrays),
        ),
        out_shape=tuple(sds(a.shape, a.dtype) for a in arrays),
        name="pack_adapters",
    )(meta, *arrays)


def pack_cache_kernel(meta_ref, table_ref, pool_ref, out_ref):
    def one(u, _):
        src = jnp.maximum(meta_ref[2, u], 0)
        for b in range(8):
            out_ref[u * 8 + b] = pool_ref[table_ref[src, b]]
        return 0

    lax.fori_loop(0, 64, one, 0)


def pack_cache(meta, table, pool):
    return pl.pallas_call(
        pack_cache_kernel,
        out_shape=sds((512, 16, HEAD), BF16),
        in_specs=[sspec(), sspec(), vspec()],
        out_specs=vspec(),
        compiler_params=params(16),
        name="pack_cache",
    )(meta, table, pool)


def join_kernel(own_ref, got_ref, x_ref, len_ref, lens_ref):
    rows = x_ref.shape[0]
    x_ref[: rows // 2] = own_ref[: rows // 2, :512]
    x_ref[rows // 2 :] = own_ref[rows // 2 :, :512] + got_ref[:, :512]
    length = jnp.concatenate(
        [own_ref[: rows // 2, 512:], own_ref[rows // 2 :, 512:] + got_ref[:, 512:]], axis=0
    ).astype(F32)
    len_ref[...] = length
    row = jnp.sum(
        jnp.where(iota((rows, HEAD), 0) == 4 * iota((rows, HEAD), 1), length, 0.0),
        axis=0,
        keepdims=True,
    ).astype(I32)
    lens_ref[...] = jnp.broadcast_to(row, (8, HEAD))


def join(own, got):
    rows = own.shape[0]
    return pl.pallas_call(
        join_kernel,
        out_shape=(sds((rows, 512), BF16), sds((rows, HEAD), F32), sds((8, HEAD), I32)),
        in_specs=[vspec()] * 2,
        out_specs=(vspec(),) * 3,
        compiler_params=params(16),
        name="join",
    )(own, got)


def matmul_kernel(n, halves, js_ref, *refs):
    xs = refs[:n]
    i = n
    ws = [refs[i + 4 * k : i + 4 * k + 4] for k in range(len(halves))]
    i += 4 * len(halves)
    first = len(refs) - i == 2
    own_ref, far_ref = refs[-2:]
    own = far = None
    at = 0
    for k, parts in enumerate(halves):
        block = [x[...] for x in xs[at : at + parts]]
        at += parts
        x = block[0] if parts == 1 else jnp.concatenate(block, axis=0)
        wq, wk, vq, vk = ws[k]
        a = jnp.dot(x, wq[...], preferred_element_type=F32)
        b = jnp.concatenate(
            [
                jnp.dot(x, vq[...], preferred_element_type=F32),
                jnp.dot(
                    x, jnp.concatenate([wk[...], vk[...]], axis=1), preferred_element_type=F32
                ),
            ],
            axis=1,
        )
        own = a if own is None else own + a
        far = b if far is None else far + b
    if not first:
        own = own + refs[i][...]
        far = far + refs[i + 1][...]
    own_ref[...] = own
    far_ref[...] = far


def matmul(js, blocks, wq, wk, vq, vk, acc=None):
    nb = len(blocks)
    halves = [len(b) for b in blocks]
    xs = [x for b in blocks for x in b]
    specs = [pl.BlockSpec(x.shape, lambda s, js: (0, 0)) for x in xs]
    args = list(xs)
    for k in range(nb):
        for w, kind in ((wq, 0), (wk, 0), (vq, 1), (vk, 1)):
            specs.append(
                pl.BlockSpec((512, w.shape[1]), lambda s, js, k=k, kind=kind: (js[kind * nb + k], 0))
            )
            args.append(w)
    outs = [(512, 512), (512, 768)]
    if acc is not None:
        for a in acc:
            specs.append(pl.BlockSpec(a.shape, lambda s, js: (0, 0)))
            args.append(a)
    return pl.pallas_call(
        functools.partial(matmul_kernel, len(xs), halves),
        grid_spec=pltpu.PrefetchScalarGridSpec(
            num_scalar_prefetch=1,
            grid=(1,),
            in_specs=specs,
            out_specs=tuple(pl.BlockSpec(o, lambda s, js: (0, 0)) for o in outs),
        ),
        out_shape=tuple(sds(o, F32) for o in outs),
        compiler_params=params(48),
        name="matmul%d" % nb,
    )(js, *args)


def down_kernel(x_ref, here_ref, far_ref, cand_ref, out_ref):
    x = x_ref[...]
    cand = cand_ref[...].astype(F32)
    acc = None
    for a in range(16):
        ref = here_ref if a < 8 else far_ref
        y = jnp.dot(x, ref[a % 8], preferred_element_type=F32)
        y = jnp.where(cand == float(a), y, 0.0)
        acc = y if acc is None else acc + y
    out_ref[...] = acc


def down_product(x, here, far, cand):
    return pl.pallas_call(
        down_kernel,
        out_shape=sds((x.shape[0], HEAD), F32),
        in_specs=[vspec()] * 4,
        out_specs=vspec(),
        compiler_params=params(24),
        name="down_product",
    )(x, here, far, cand)


def down_sum_kernel(x_ref, out_ref):
    n = x_ref.shape[0]
    total = x_ref[0]
    for i in range(1, n):
        total = total + x_ref[i]
    total = total.astype(BF16)
    for i in range(n):
        out_ref[i] = total


def down_sum(x):
    return pl.pallas_call(
        down_sum_kernel,
        out_shape=sds(x.shape, BF16),
        in_specs=[vspec()],
        out_specs=vspec(),
        name="down_sum",
    )(x)


def up_kernel(down_ref, cand_ref, q_here, k_here, o_here, q_far, k_far, o_far, out_ref):
    down = down_ref[...].astype(F32)
    cand = cand_ref[...].astype(F32)
    rows = down.shape[0]
    lane = iota((rows, HEAD), 1)
    upper = lane >= HEAD // 2
    other = pltpu.roll(down, HEAD // 2, 1)
    down_q = jnp.where(upper, other, down)
    down_k = jnp.where(upper, down, other)
    shift = jnp.where(upper, 1.0, 0.0)

    def spread(v):
        return jnp.concatenate(
            [jnp.where(cand == shift + float(2 * i), v, 0.0).astype(BF16) for i in range(8)], axis=1
        )

    sq, sk = spread(down_q), spread(down_k)

    def both(here, far):
        h, f = here[...], far[...]
        return jnp.concatenate([h.reshape(-1, h.shape[2]), f.reshape(-1, f.shape[2])], axis=0)

    out_ref[:, :512] = jnp.dot(sq, both(q_here, q_far), preferred_element_type=F32)
    out_ref[:, 512:640] = jnp.dot(sk, both(k_here, k_far), preferred_element_type=F32)
    out_ref[:, 640:] = jnp.dot(sk, both(o_here, o_far), preferred_element_type=F32)


def up_product(down, cand, here, far):
    return pl.pallas_call(
        up_kernel,
        out_shape=sds((down.shape[0], 768), F32),
        in_specs=[vspec()] * 8,
        out_specs=vspec(),
        compiler_params=params(24),
        name="up_product",
    )(down, cand, *here, *far)


def attend_kernel(
    par_ref, meta_ref, lens_ref, prev_ref, moved_ref,
    own_ref, far_ref, rx_ref, delta_ref, cos_ref, sin_ref,
    pool_ref, pool2_ref, got_ref, got2_ref,
    out_ref, new_ref,
    q_scr, f_scr, kv_scr,
):
    odd = par_ref[0]
    cos, sin = cos_ref[...], sin_ref[...]

    def turn(v):
        return v * cos + pltpu.roll(v, HEAD // 2, 1) * sin

    for h in range(4):
        at = slice(h * HEAD, (h + 1) * HEAD)
        q_scr[:, at] = turn(own_ref[:, at] + rx_ref[:, at] + delta_ref[:, at])
    kv_own = far_ref[:, 512:640] + rx_ref[:, 640:768] + delta_ref[:, 512:640]
    kv_oth = far_ref[:, 640:768] + rx_ref[:, 512:640] + delta_ref[:, 640:768]
    key = turn(jnp.where(odd == 0, kv_own, kv_oth))
    value = jnp.where(odd == 0, kv_oth, kv_own)
    f_scr[:, :HEAD] = key
    f_scr[:, HEAD:] = value

    t = iota((256, 8), 0)
    c = iota((256, 8), 1)
    t_wide = iota((HEAD, HEAD), 0)
    row2 = (iota((32, 256), 0) % 8) // 4
    step = iota((32, 256), 0) % 4
    col = iota((32, 256), 1)

    def pair(i, arrivals):
        lengths, slots = [], []
        for e in range(2):
            p = 2 * i + e
            n = meta_ref[0, p]
            lengths.append(lens_ref[0, p])
            slots.append(n)
            src = meta_ref[1, p]
            local = jnp.maximum(src, 0)
            for b in range(8):
                page = prev_ref[local, b]
                mine, other = pool_ref[page], pool2_ref[page]
                if arrivals:
                    at = (p - 64) * 8 + b
                    mine = jnp.where(src < 0, got_ref[at], mine)
                    other = jnp.where(src < 0, got2_ref[at], other)
                rows = pl.ds(e * HEAD + b * 16, 16)
                kv_scr[0, rows, :] = mine
                kv_scr[1, rows, :] = other
        fresh = f_scr[pl.ds(pl.multiple_of(8 * i, 8), 8), :].astype(BF16)
        land = (t % HEAD == jnp.where(c < 4, lengths[0], lengths[1]) + c % 4) & (t // HEAD == c // 4)
        spread = jnp.dot(
            jnp.where(land, 1.0, 0.0).astype(BF16), fresh, preferred_element_type=F32
        )
        old = jnp.concatenate(
            [t_wide < lengths[0], t_wide < lengths[1]], axis=0
        )
        keys = jnp.where(old, kv_scr[odd].astype(F32), spread[:, :HEAD]).astype(BF16)
        values = jnp.where(old, kv_scr[1 - odd].astype(F32), spread[:, HEAD:]).astype(BF16)
        kept = jnp.where(odd == 0, keys, values)
        for e in range(2):
            for b in range(8):
                lo = e * HEAD + b * 16
                new_ref[moved_ref[slots[e], b]] = kept[lo : lo + 16]
        q = q_scr[pl.ds(pl.multiple_of(8 * i, 8), 8), :]
        q = jnp.concatenate([q[:, h * HEAD : (h + 1) * HEAD] for h in range(4)], axis=0)
        scores = lax.dot_general(
            q.astype(BF16), keys, (((1,), (1,)), ((), ())), preferred_element_type=F32
        ) / math.sqrt(HEAD)
        limit = jnp.where(row2 == 0, lengths[0], lengths[1] + HEAD) + step
        seen = (col <= limit) & (col >= row2 * HEAD)
        scores = jnp.where(seen, scores, -1e30)
        top = jnp.max(scores, axis=1, keepdims=True)
        weight = jnp.where(seen, jnp.exp(scores - top), 0.0)
        prob = (weight / jnp.sum(weight, axis=1, keepdims=True)).astype(BF16)
        mixed = jnp.dot(prob, values, preferred_element_type=F32)
        for e in range(2):
            for h in range(4):
                lo = h * 8 + e * 4
                out_ref[slots[e], :, h * HEAD : (h + 1) * HEAD] = mixed[lo : lo + 4].astype(BF16)

    def first(i, _):
        pair(i, False)
        return 0

    def second(i, _):
        pair(i, True)
        return 0

    lax.fori_loop(0, 32, first, 0)
    lax.fori_loop(32, 64, second, 0)


def attend(parity, meta, lens, prev, moved, own, far, rx, delta, cos, sin, pool, pool2, got, got2):
    return pl.pallas_call(
        attend_kernel,
        out_shape=(sds((128, 4, 512), BF16), sds((1024, 16, HEAD), BF16)),
        in_specs=[sspec()] * 5 + [vspec()] * 10,
        out_specs=(vspec(), vspec()),
        scratch_shapes=[
            pltpu.VMEM((512, 512), F32),
            pltpu.VMEM((512, 256), F32),
            pltpu.VMEM((2, 256, HEAD), BF16),
        ],
        compiler_params=params(40),
        name="attend",
    )(parity, meta, lens, prev, moved, own, far, rx, delta, cos, sin, pool, pool2, got, got2)


def body(
    tokens,
    query_weight_matrix,
    key_value_weight,
    adapter_down_factors,
    adapter_up_query,
    adapter_up_key_value,
    storage_slot_adapter,
    slot_request_adapter,
    migration,
    lengths,
    previous_block_table,
    moved_block_table,
    paged_cache_pool,
):
    r = lax.axis_index("rep").astype(I32)
    t = lax.axis_index("tp").astype(I32)
    core = t % 2

    def other_core(a):
        return lax.ppermute(a, "tp", [(i, i ^ 1) for i in range(16)])

    def other_x(a):
        return lax.ppermute(a, "tp", [(i, i ^ 2) for i in range(16)])

    def along_y(a, d):
        return lax.ppermute(a, "tp", [(i, (i + 4 * d) % 16) for i in range(16)])

    def swap_rep(a):
        return lax.all_to_all(a, "rep", split_axis=0, concat_axis=0, tiled=True)

    send, own, cand, meta = plan(
        r.reshape(1),
        migration.reshape(8, 128),
        slot_request_adapter.reshape(8, 128),
        storage_slot_adapter.reshape(1, 64),
        lengths.reshape(1, 128),
        tokens.reshape(512, 512),
    )
    x, length, lens = join(own, swap_rep(send))

    pool2 = other_core(paged_cache_pool)
    far_core = 1 - core
    vq = other_core(
        lax.dynamic_index_in_dim(query_weight_matrix.reshape(8, 2, 512, 512), far_core, 1, False)
    ).reshape(4096, 512)
    vk = other_core(
        lax.dynamic_index_in_dim(key_value_weight.reshape(8, 2, 512, HEAD), far_core, 1, False)
    ).reshape(4096, HEAD)
    up_kv_other = other_core(adapter_up_key_value)

    here = (adapter_up_query, adapter_up_key_value, up_kv_other)
    packed = pack_adapters(meta, adapter_down_factors, *here)
    far_down = swap_rep(packed[0])
    far_up = tuple(swap_rep(a) for a in packed[1:])
    got = swap_rep(pack_cache(meta, previous_block_table, paged_cache_pool))
    got2 = other_core(got)

    hi = (t // 2) % 2
    y = t // 4

    def rows(dy, dx):
        at = ((y + dy) % 4) * 2 + (hi ^ dx)
        return at * 2 + core, at

    def js(*blocks):
        pairs = [rows(*b) for b in blocks]
        return jnp.stack([p[0] for p in pairs] + [p[1] for p in pairs]).astype(I32)

    weights = (query_weight_matrix, key_value_weight, vq, vk)
    xh = other_x(x)
    yp = along_y(x, 1)
    ym = along_y(x, -1)
    xyp = along_y(xh, 1)
    xym = along_y(xh, -1)
    y2 = (along_y(yp[:256], 1), along_y(ym[256:], -1))
    acc = matmul(js((0, 0), (0, 1), (3, 0), (1, 0)), [(x,), (xh,), (yp,), (ym,)], *weights)
    xy2 = (along_y(xyp[:256], 1), along_y(xym[256:], -1))
    acc = matmul(js((3, 1), (1, 1), (2, 0)), [(xyp,), (xym,), y2], *weights, acc=acc)
    acc_own, acc_far = matmul(js((2, 1)), [xy2], *weights, acc=acc)
    rx = other_core(acc_far)

    partial = down_product(x, adapter_down_factors, far_down, cand)
    pieces = lax.all_to_all(partial, "tp", split_axis=0, concat_axis=0, tiled=True)
    down = lax.all_to_all(
        down_sum(pieces.reshape(16, 32, HEAD)).reshape(512, HEAD),
        "tp", split_axis=0, concat_axis=0, tiled=True,
    )
    delta = up_product(down, cand, here, far_up)

    positions = length + (jnp.arange(512, dtype=I32) % 4).astype(F32)[:, None]
    frequency = THETA ** (-(jnp.arange(HEAD // 2, dtype=F32) * 2.0 / HEAD))
    angles = positions[:, : HEAD // 2] * frequency
    cos, sin = jnp.cos(angles), jnp.sin(angles)
    cos = jnp.concatenate([cos, cos], axis=1)
    sin = jnp.concatenate([-sin, sin], axis=1)
    return attend(
        core.reshape(1), meta, lens, previous_block_table, moved_block_table,
        acc_own, acc_far, rx, delta, cos, sin, paged_cache_pool, pool2, got, got2,
    )


def solution(mesh):
    in_specs = (
        P("rep", None, "tp"),
        P(None, "tp"),
        P(None, "tp"),
        P("rep", "tp", None),
        P("rep", None, "tp"),
        P("rep", None, "tp"),
        P(),
        P(),
        P(),
        P("rep"),
        P("rep", None),
        P("rep", None),
        P("rep", None, "tp"),
    )
    out_specs = (P("rep", None, "tp"), P("rep", None, "tp"))
    return jax.shard_map(body, mesh=mesh, in_specs=in_specs, out_specs=out_specs, check_vma=False)
```

time: 584 us -> 250 us (0.43)
  waiting for transfers between devices: 229 us -> 61.8 us
  local copies, waits for them, and re-layouts: 172 us -> 30.7 us
  Pallas kernels: 0 us -> 82.9 us
  blocking collectives: 68.8 us -> 10.2 us
  other arithmetic: 50.5 us -> 4.95 us
  starting transfers between devices: 16.4 us -> 56.5 us
  matrix products: 27.3 us -> 0 us
  between operations: 14.5 us -> 1.01 us
    all_gather x4 -> x0, waiting for transfers between devices: 187 us -> none  [the longest x1 112 us: body(): lax.all_gather(adapter_down_factors, 'rep', axis=0, tiled=True)]
    scatter x2 -> x0, local copies, waits for them, and re-layouts: 115 us -> none  [the longest x1 110 us: body(): written = jnp.zeros_like(paged_cache_pool).at[moved_block_table.reshape(-...]
    pallas_call x0 -> x11, Pallas kernels: none -> 82.9 us  [the longest x1 46.4 us: attend(): pl.pallas_call(attend_kernel, out_shape=(sds((128, 4, 512), BF16), sds((1...]
    psum x1 -> x0, blocking collectives: 68.8 us -> none  [body(): down_factor_rows = lax.psum(partial_down, 'tp').astype(jnp.bfloat16)]
    gather x17 -> x0, local copies, waits for them, and re-layouts: 47.7 us -> none  [the longest x1 10.5 us: body(): paged_cache_pool[previous_block_table]]
    ppermute x1 -> x15, waiting for transfers between devices: 0.01 us -> 42.1 us  [the longest x1 31.6 us: other_x(): return lax.ppermute(a, 'tp', [(i, i ^ 2) for i in range(16)])]
    select_n x16 -> x0, other arithmetic: 39.1 us -> none  [the longest x2 25.6 us: body(): cache_now = jnp.where(landing, fresh[:, step_at][:, None, :], cache_now)]
    dot_general x7 -> x0, matrix products: 27.3 us -> none  [the longest x1 9.51 us: body(): jnp.dot(shard_piece, query_weight_matrix, preferred_element_type=jnp.floa...]
  transfers between devices with their start and end apart: 8 -> 22, of which waited for: 6 -> 6; matrix products, arithmetic and copies ran while one was open for 41% -> 5% of each run, Pallas kernels for 0% -> 15%
where the time goes in v1:
time: 250 us; the launch traced here: 248 us
  Pallas kernels  82.9 us (33%)
  waiting for transfers between devices  61.8 us (25%)
  starting transfers between devices  56.5 us (23%)
  local copies, waits for them, and re-layouts  30.7 us (12%)
  blocking collectives  10.2 us (4%)
  other arithmetic  4.95 us (2%)
    pallas_call x1, Pallas kernels, attend(): pl.pallas_call(attend_kernel, out_shape=(sds((128, 4, 512), BF16), sds((1...  46.4 us
    ppermute x1, waiting for transfers between devices, other_x(): return lax.ppermute(a, 'tp', [(i, i ^ 2) for i in range(16)])  31.6 us
    all_to_all x5, starting transfers between devices, swap_rep(): return lax.all_to_all(a, 'rep', split_axis=0, concat_axis=0, tiled=True)  25.5 us
    unnamed x82, local copies, waits for them, and re-layouts  18.9 us
    pallas_call x3, Pallas kernels, matmul(): pl.pallas_call(functools.partial(matmul_kernel, len(xs), halves), grid_sp...  16.9 us
    ppermute x8, starting transfers between devices, along_y(): return lax.ppermute(a, 'tp', [(i, (i + 4 * d) % 16) for i in range(16)])  11.9 us
    ppermute x8, waiting for transfers between devices, along_y(): return lax.ppermute(a, 'tp', [(i, (i + 4 * d) % 16) for i in range(16)])  10.5 us
    all_to_all x1, blocking collectives, swap_rep(): return lax.all_to_all(a, 'rep', split_axis=0, concat_axis=0, tiled=True)  10.2 us
  transfers between devices with their start and end apart: 22, of which 6 were waited for; matrix products, arithmetic and copies ran while one was open for 5% of the time, Pallas kernels for 15%

profile of v1, /device:TPU:1, one launch (start us, length us, event | category | flops | bytes accessed | tf_op | source)
XLA Modules:
  0.0 248.1 jit_solution(2436955457110982600)
XLA Ops:
  0.7 4.5 %dynamic-slice_bitcast_fusion = bf16[8,512,512]{2,1,0:T(8,128)(2,1)} fusion(bf16[8,2,512,512]{3,2,1,0:T(8,128)(2,1)} %bitcast.47, s32[]{:T(128)S(6)} %select_n.63), kind=kLoop, calls=%fused_computation | loop fusion | bytes 8388612 | tf_op jit(solution)/shard_map/jit(dynamic_index_in_dim)/squeeze | solution.py:531
  6.8 2.1 plan.1
  9.6 6.0 %all-to-all-start = ((bf16[8,32,640]{2,1,0:T(8,128)(2,1)}), bf16[8,32,640]{2,1,0:T(8,128)(2,1)S(1)}, u32[]{:S(2)}, u32[]{:S(2)}) async-start(bf16[8,32,640]{2,1,0:T(8,128)(2,1)} %bitcast.6), calls=%async_computation | async-start | bytes 655360 | tf_op jit(solution)/shard_map/all_to_all | solution.py:516
  16.0 2.2 copy-done
  18.2 3.0 %pack_cache.1 = bf16[512,16,128]{2,1,0:T(8,128)(2,1)S(1)} custom-call(s32[8,128]{1,0:T(8,128)S(1)} %get-tuple-element.19.meta_ref, s32[128,8]{1,0:T(8,128)S(1)} %copy.16.table_ref.prev_ref, bf16[1024,16,128]{2,1,0:T(8,128)(2,1)S(1)} %copy-done), custom_call_target="tpu_custom_call" | custom-call | tf_op jit(solution)/shard_map/pack_cache/pallas_call | solution.py:195
  23.4 4.7 %all-to-all-start.7 = ((bf16[512,16,128]{2,1,0:T(8,128)(2,1)}), bf16[512,16,128]{2,1,0:T(8,128)(2,1)S(1)}, u32[]{:S(2)}, u32[]{:S(2)}) async-start(bf16[512,16,128]{2,1,0:T(8,128)(2,1)} %copy-done.1), calls=%async_computation.7 | async-start | bytes 4194304 | tf_op jit(solution)/shard_map/all_to_all | solution.py:516
  28.2 2.5 %collective-permute-start = (bf16[512,512]{1,0:T(8,128)(2,1)S(1)}, bf16[512,512]{1,0:T(8,128)(2,1)}, u32[]{:S(2)}, u32[]{:S(2)}) collective-permute-start(bf16[512,512]{1,0:T(8,128)(2,1)S(1)} %get-tuple-element.23.refs_0_.x_ref), channel_id=1, source_target_pairs={{0,2},{1,3},{2,0},{3,1},{4,6},{5,7},{6,4},{7,5},{8,10},{9,11},{10,... | collective-permute-start | bytes 1572872 | tf_op jit(solution)/shard_map/ppermute | solution.py:510
  34.1 31.6 %collective-permute-done.refs_1_ = bf16[512,512]{1,0:T(8,128)(2,1)} collective-permute-done((bf16[512,512]{1,0:T(8,128)(2,1)S(1)}, bf16[512,512]{1,0:T(8,128)(2,1)}, u32[]{:S(2)}, u32[]{:S(2)}) %collective-permute-start) | collective-permute-done | bytes 524320 | tf_op jit(solution)/shard_map/ppermute | solution.py:510
  65.7 2.7 %collective-permute-start.9 = (bf16[512,512]{1,0:T(8,128)(2,1)S(1)}, bf16[512,512]{1,0:T(8,128)(2,1)S(1)}, u32[]{:S(2)}, u32[]{:S(2)}) collective-permute-start(bf16[512,512]{1,0:T(8,128)(2,1)S(1)} %get-tuple-element.23.refs_0_.x_ref), channel_id=1, source_target_pairs={{0,12},{1,13},{2,14},{3,15},{4,0},{5,1},{6,2},{7,3},{8,4},{9,5},{1... | collective-permute-start | bytes 1572872 | tf_op jit(solution)/shard_map/ppermute | solution.py:513
  68.4 10.4 %collective-permute-done.9.refs_3_ = bf16[512,512]{1,0:T(8,128)(2,1)S(1)} collective-permute-done((bf16[512,512]{1,0:T(8,128)(2,1)S(1)}, bf16[512,512]{1,0:T(8,128)(2,1)S(1)}, u32[]{:S(2)}, u32[]{:S(2)}) %collective-permute-start.9) | collective-permute-done | bytes 524320 | tf_op jit(solution)/shard_map/ppermute | solution.py:513
  78.9 3.4 %collective-permute-start.3 = (bf16[512,512]{1,0:T(8,128)(2,1)}, bf16[512,512]{1,0:T(8,128)(2,1)}, u32[]{:S(2)}, u32[]{:S(2)}) collective-permute-start(bf16[512,512]{1,0:T(8,128)(2,1)} %collective-permute-done.refs_1_), channel_id=1, source_target_pairs={{0,12},{1,13},{2,14},{3,15},{4,0},{5,1},{6,2},{7,3},{8,4},{9,5},{1... | collective-permute-start | bytes 1572872 | tf_op jit(solution)/shard_map/ppermute | solution.py:513
  83.1 2.0 collective-permute-start.14
  85.2 6.3 %pack_adapters.1 = (bf16[8,512,128]{2,1,0:T(8,128)(2,1)}, bf16[8,64,512]{2,1,0:T(8,128)(2,1)}, bf16[8,64,128]{2,1,0:T(8,128)(2,1)}, bf16[8,64,128]{2,1,0:T(8,128)(2,1)}) custom-call(s32[8,128]{1,0:T(8,128)} %copy-done.30, bf16[8,512,128]{2,1,0:T(8,128)(2,1)} %here_ref.1, bf16[8,64,512]{2,1,0:T(8,128)(2,1)} %q_here.1, bf16[8,64,128]{2,1,0:T(8,128)(2,1)} %k_here.1, ...), custom_call_target="tpu_custom_call" | custom-call | tf_op jit(solution)/shard_map/pack_adapters/pallas_call | solution.py:171
  91.5 10.2 %all_to_all.53.k_far = bf16[8,64,128]{2,1,0:T(8,128)(2,1)} all-to-all(bf16[8,64,128]{2,1,0:T(8,128)(2,1)} %get-tuple-element.33), channel_id=1, replica_groups=mesh['rep'=8,'tp'=16] {'rep'}, dimensions={0} | all-to-all | bytes 262144 | tf_op jit(solution)/shard_map/all_to_all | solution.py:516
  101.8 4.2 %all-to-all-start.1 = ((bf16[8,512,128]{2,1,0:T(8,128)(2,1)}), bf16[8,512,128]{2,1,0:T(8,128)(2,1)}, u32[]{:S(2)}, u32[]{:S(2)}) async-start(bf16[8,512,128]{2,1,0:T(8,128)(2,1)} %get-tuple-element.30), calls=%async_computation.1 | async-start | bytes 2097152 | tf_op jit(solution)/shard_map/all_to_all | solution.py:516
  112.7 2.7 %collective-permute-start.4 = (bf16[256,512]{1,0:T(8,128)(2,1)}, bf16[256,512]{1,0:T(8,128)(2,1)}, u32[]{:S(2)}, u32[]{:S(2)}) collective-permute-start(bf16[256,512]{1,0:T(8,128)(2,1)} %slice.21), channel_id=1, source_target_pairs={{0,12},{1,13},{2,14},{3,15},{4,0},{5,1},{6,2},{7,3},{8,4},{9,5},{1... | collective-permute-start | bytes 786440 | tf_op jit(solution)/shard_map/ppermute | solution.py:513
  118.7 5.9 %matmul4.1 = (f32[512,512]{1,0:T(8,128)S(1)}, f32[512,768]{1,0:T(8,128)S(1)}) custom-call(s32[8]{0:T(128)S(1)} %stack.75.js_ref, bf16[512,512]{1,0:T(8,128)(2,1)S(1)} %copy-done.4, bf16[512,512]{1,0:T(8,128)(2,1)} %collective-permute-done.refs_1_, bf16[512,512]{1,0:T(8,128)(2,1)S(1)} %copy-done.9, bf16[512,512]{1,0:T(8,128)(2,1)S(1)} %copy-done.11, ...), custom_call_target="tpu_custom_call" | custom-call | tf_op jit(solution)/shard_map/matmul4/pallas_call | solution.py:283
  125.8 6.9 %matmul3.1 = (f32[512,512]{1,0:T(8,128)S(1)}, f32[512,768]{1,0:T(8,128)}) custom-call(s32[6]{0:T(128)S(1)} %stack.66.js_ref, bf16[512,512]{1,0:T(8,128)(2,1)} %collective-permute-done.1.refs_0_, bf16[512,512]{1,0:T(8,128)(2,1)} %collective-permute-done.3.refs_1_, bf16[256,512]{1,0:T(8,128)(2,1)} %collective-permute-done.8.refs_2_, ...), custom_call_target="tpu_custom_call" | custom-call | tf_op jit(solution)/shard_map/matmul3/pallas_call | solution.py:283
  134.3 4.2 %matmul1.1 = (f32[512,512]{1,0:T(8,128)S(1)}, f32[512,768]{1,0:T(8,128)}) custom-call(s32[2]{0:T(128)S(1)} %pad_add_fusion.js_ref, bf16[256,512]{1,0:T(8,128)(2,1)S(1)} %copy-done.28, bf16[256,512]{1,0:T(8,128)(2,1)} %collective-permute-done.4.refs_1_, bf16[8192,512]{1,0:T(8,128)(2,1)} %refs_2_.2, bf16[8192,128]{1,0:T(8,128)(2,1)} %refs_3_.1, ...), custom_call_target="tpu_custom_call" | custom-call | tf_op jit(solution)/shard_map/matmul1/pallas_call | solution.py:283
  139.5 2.3 collective-permute-start.11
  141.7 5.3 %all-to-all-start.6 = ((bf16[8,64,128]{2,1,0:T(8,128)(2,1)}), bf16[8,64,128]{2,1,0:T(8,128)(2,1)S(1)}, u32[]{:S(2)}, u32[]{:S(2)}) async-start(bf16[8,64,128]{2,1,0:T(8,128)(2,1)} %get-tuple-element.34), calls=%async_computation.6 | async-start | bytes 262144 | tf_op jit(solution)/shard_map/all_to_all | solution.py:516
  149.3 4.3 %down_product.1 = f32[512,128]{1,0:T(8,128)} custom-call(bf16[512,512]{1,0:T(8,128)(2,1)S(1)} %copy-done.5, bf16[8,512,128]{2,1,0:T(8,128)(2,1)S(1)} %copy-done.2, bf16[8,512,128]{2,1,0:T(8,128)(2,1)} %all-to-all-done.1.far_ref, bf16[512,128]{1,0:T(8,128)(2,1)S(1)} %copy-done.22), custom_call_target="tpu_custom_call" | custom-call | tf_op jit(solution)/shard_map/down_product/pallas_call | solution.py:310
  153.6 3.8 %all-to-all-start.2 = ((f32[16,32,128]{2,1,0:T(8,128)}), f32[16,32,128]{2,1,0:T(8,128)S(1)}, u32[]{:S(2)}, u32[]{:S(2)}) async-start(f32[16,32,128]{2,1,0:T(8,128)} %bitcast.30), calls=%async_computation.2 | async-start | bytes 524288 | tf_op jit(solution)/shard_map/all_to_all | solution.py:570
  157.5 8.6 %all-to-all-done.2.x_ref = f32[16,32,128]{2,1,0:T(8,128)S(1)} async-done(((f32[16,32,128]{2,1,0:T(8,128)}), f32[16,32,128]{2,1,0:T(8,128)S(1)}, u32[]{:S(2)}, u32[]{:S(2)}) %all-to-all-start.2) | async-done | bytes 262176 | tf_op jit(solution)/shard_map/all_to_all | solution.py:570
  166.8 5.3 %all-to-all-start.4 = ((bf16[8,64,512]{2,1,0:T(8,128)(2,1)}), bf16[8,64,512]{2,1,0:T(8,128)(2,1)S(1)}, u32[]{:S(2)}, u32[]{:S(2)}) async-start(bf16[8,64,512]{2,1,0:T(8,128)(2,1)} %get-tuple-element.32), calls=%async_computation.4 | async-start | bytes 1048576 | tf_op jit(solution)/shard_map/all_to_all | solution.py:516
  172.1 2.8 %fusion.7 = (f32[512,64]{1,0:T(8,128)}, f32[512,64]{1,0:T(8,128)}, f32[512,64]{1,0:T(8,128)}) fusion(f32[64]{0:T(128)S(1)} %negate_power_fusion, f32[512]{0:T(512)S(1)} %fusion.3, f32[512,128]{1,0:T(8,128)} %copy-done.29), kind=kLoop, calls=%fused_computation.16 | loop fusion | flops 98304 | bytes 526592 | tf_op jit(solution)/shard_map/neg | solution.py:582
  176.5 4.4 %all-to-all-done.4.q_far = bf16[8,64,512]{2,1,0:T(8,128)(2,1)S(1)} async-done(((bf16[8,64,512]{2,1,0:T(8,128)(2,1)}), bf16[8,64,512]{2,1,0:T(8,128)(2,1)S(1)}, u32[]{:S(2)}, u32[]{:S(2)}) %all-to-all-start.4) | async-done | bytes 524320 | tf_op jit(solution)/shard_map/all_to_all | solution.py:516
  180.9 6.1 %all-to-all-start.3 = ((bf16[16,32,128]{2,1,0:T(8,128)(2,1)}), bf16[16,32,128]{2,1,0:T(8,128)(2,1)}, u32[]{:S(2)}, u32[]{:S(2)}) async-start(bf16[16,32,128]{2,1,0:T(8,128)(2,1)} %down_sum.1), calls=%async_computation.3 | async-start | bytes 262144 | tf_op jit(solution)/shard_map/all_to_all | solution.py:571
  187.0 2.1 pad_maximum_fusion
  189.1 5.7 %all-to-all-done.3 = bf16[16,32,128]{2,1,0:T(8,128)(2,1)} async-done(((bf16[16,32,128]{2,1,0:T(8,128)(2,1)}), bf16[16,32,128]{2,1,0:T(8,128)(2,1)}, u32[]{:S(2)}, u32[]{:S(2)}) %all-to-all-start.3) | async-done | bytes 131104 | tf_op jit(solution)/shard_map/all_to_all | solution.py:571
  199.5 2.2 up_product.1.delta_ref
  201.7 46.4 %attend.1 = (bf16[128,4,512]{2,1,0:T(4,128)(2,1)}, bf16[1024,16,128]{2,1,0:T(8,128)(2,1)}) custom-call(s32[1]{0:T(128)} %bitcast.par_ref, s32[8,128]{1,0:T(8,128)S(1)} %copy-done.31, s32[8,128]{1,0:T(8,128)S(1)} %get-tuple-element.22.lens_ref, s32[128,8]{1,0:T(8,128)S(1)} %copy.16.table_ref.prev_ref, s32[128,8]{1,0:T(8,128)S(1)} %copy.17.moved_ref, ...), custom_call_target="tpu_custom_call" | custom-call | tf_op jit(solution)/shard_map/attend/pallas_call | solution.py:472
  (120 shorter events, 32.3 us)
Async XLA Ops:
  5.2 10.7 %copy-start.38 = (s32[128,8]{0,1:T(8,128)S(1)}, s32[128,8]{0,1:T(8,128)}, u32[]{:S(2)}) copy-start(s32[128,8]{0,1:T(8,128)} %param.23) | copy-start | bytes 12292
  5.2 107.5 %collective-permute-start.5 = (bf16[8,512,512]{2,1,0:T(8,128)(2,1)}, bf16[8,512,512]{2,1,0:T(8,128)(2,1)}, u32[]{:S(2)}, u32[]{:S(2)}) collective-permute-start(bf16[8,512,512]{2,1,0:T(8,128)(2,1)} %dynamic-slice_bitcast_fusion), channel_id=1, source_target_pairs={{0,1},{1,0},{2,3},{3,2},{4,5},{5,4},{6,7},{7,6},{8,9},{9,8},{10,11... | collective-permute-start | bytes 12582920 | tf_op jit(solution)/shard_map/ppermute | solution.py:507
  9.6 11.6 %copy-start.30 = (s32[8,128]{1,0:T(8,128)}, s32[8,128]{1,0:T(8,128)S(1)}, u32[]{:S(2)}) copy-start(s32[8,128]{1,0:T(8,128)S(1)} %get-tuple-element.19.meta_ref) | copy-start | bytes 12292
  9.6 13.8 %all-to-all-start = ((bf16[8,32,640]{2,1,0:T(8,128)(2,1)}), bf16[8,32,640]{2,1,0:T(8,128)(2,1)S(1)}, u32[]{:S(2)}, u32[]{:S(2)}) async-start(bf16[8,32,640]{2,1,0:T(8,128)(2,1)} %bitcast.6), calls=%async_computation | async-start | bytes 655360 | tf_op jit(solution)/shard_map/all_to_all | solution.py:516
  15.6 186.1 %collective-permute-start.13 = (bf16[1024,16,128]{2,1,0:T(8,128)(2,1)}, bf16[1024,16,128]{2,1,0:T(8,128)(2,1)}, u32[]{:S(2)}, u32[]{:S(2)}) collective-permute-start(bf16[1024,16,128]{2,1,0:T(8,128)(2,1)} %pool_ref.3), channel_id=1, source_target_pairs={{0,1},{1,0},{2,3},{3,2},{4,5},{5,4},{6,7},{7,6},{8,9},{9,8},{10,11... | collective-permute-start | bytes 12582920 | tf_op jit(solution)/shard_map/ppermute | solution.py:507
  23.4 59.7 %all-to-all-start.7 = ((bf16[512,16,128]{2,1,0:T(8,128)(2,1)}), bf16[512,16,128]{2,1,0:T(8,128)(2,1)S(1)}, u32[]{:S(2)}, u32[]{:S(2)}) async-start(bf16[512,16,128]{2,1,0:T(8,128)(2,1)} %copy-done.1), calls=%async_computation.7 | async-start | bytes 4194304 | tf_op jit(solution)/shard_map/all_to_all | solution.py:516
  28.2 54.9 %copy-start.3 = (bf16[512,512]{1,0:T(8,128)(2,1)}, bf16[512,512]{1,0:T(8,128)(2,1)S(1)}, u32[]{:S(2)}) copy-start(bf16[512,512]{1,0:T(8,128)(2,1)S(1)} %get-tuple-element.23.refs_0_.x_ref) | copy-start | bytes 1572868
  28.2 54.9 %copy-start.29 = (f32[512,128]{1,0:T(8,128)}, f32[512,128]{1,0:T(8,128)S(1)}, u32[]{:S(2)}) copy-start(f32[512,128]{1,0:T(8,128)S(1)} %get-tuple-element.35) | copy-start | bytes 786436
  28.2 37.5 %collective-permute-start = (bf16[512,512]{1,0:T(8,128)(2,1)S(1)}, bf16[512,512]{1,0:T(8,128)(2,1)}, u32[]{:S(2)}, u32[]{:S(2)}) collective-permute-start(bf16[512,512]{1,0:T(8,128)(2,1)S(1)} %get-tuple-element.23.refs_0_.x_ref), channel_id=1, source_target_pairs={{0,2},{1,3},{2,0},{3,1},{4,6},{5,7},{6,4},{7,5},{8,10},{9,11},{10,... | collective-permute-start | bytes 1572872 | tf_op jit(solution)/shard_map/ppermute | solution.py:510
  30.7 2.0 collective-permute-start.12
  32.6 50.5 %collective-permute-start.6 = (bf16[8,512,128]{2,1,0:T(8,128)(2,1)S(1)}, bf16[8,512,128]{2,1,0:T(8,128)(2,1)S(1)}, u32[]{:S(2)}, u32[]{:S(2)}) collective-permute-start(bf16[8,512,128]{2,1,0:T(8,128)(2,1)S(1)} %dynamic-slice_bitcast_fusion.1), channel_id=1, source_target_pairs={{0,1},{1,0},{2,3},{3,2},{4,5},{5,4},{6,7},{7,6},{8,9},{9,8},{10,11... | collective-permute-start | bytes 3145736 | tf_op jit(solution)/shard_map/ppermute | solution.py:507
  32.7 52.5 %copy-start.19 = (bf16[8,64,128]{2,1,0:T(8,128)(2,1)}, bf16[8,64,128]{2,1,0:T(8,128)(2,1)S(1)}, u32[]{:S(2)}) copy-start(bf16[8,64,128]{2,1,0:T(8,128)(2,1)S(1)} %collective-permute-done.12.refs_3_.o_here) | copy-start | bytes 393220
  32.7 35.7 %collective-permute-start.7 = (bf16[512,512]{1,0:T(8,128)(2,1)S(1)}, bf16[512,512]{1,0:T(8,128)(2,1)S(1)}, u32[]{:S(2)}, u32[]{:S(2)}) collective-permute-start(bf16[512,512]{1,0:T(8,128)(2,1)S(1)} %get-tuple-element.23.refs_0_.x_ref), channel_id=1, source_target_pairs={{0,4},{1,5},{2,6},{3,7},{4,8},{5,9},{6,10},{7,11},{8,12},{9,13},{1... | collective-permute-start | bytes 1572872 | tf_op jit(solution)/shard_map/ppermute | solution.py:513
  65.7 13.2 %collective-permute-start.9 = (bf16[512,512]{1,0:T(8,128)(2,1)S(1)}, bf16[512,512]{1,0:T(8,128)(2,1)S(1)}, u32[]{:S(2)}, u32[]{:S(2)}) collective-permute-start(bf16[512,512]{1,0:T(8,128)(2,1)S(1)} %get-tuple-element.23.refs_0_.x_ref), channel_id=1, source_target_pairs={{0,12},{1,13},{2,14},{3,15},{4,0},{5,1},{6,2},{7,3},{8,4},{9,5},{1... | collective-permute-start | bytes 1572872 | tf_op jit(solution)/shard_map/ppermute | solution.py:513
  68.4 14.7 %collective-permute-start.1 = (bf16[512,512]{1,0:T(8,128)(2,1)}, bf16[512,512]{1,0:T(8,128)(2,1)}, u32[]{:S(2)}, u32[]{:S(2)}) collective-permute-start(bf16[512,512]{1,0:T(8,128)(2,1)} %collective-permute-done.refs_1_), channel_id=1, source_target_pairs={{0,4},{1,5},{2,6},{3,7},{4,8},{5,9},{6,10},{7,11},{8,12},{9,13},{1... | collective-permute-start | bytes 1572872 | tf_op jit(solution)/shard_map/ppermute | solution.py:513
  78.9 30.5 %collective-permute-start.3 = (bf16[512,512]{1,0:T(8,128)(2,1)}, bf16[512,512]{1,0:T(8,128)(2,1)}, u32[]{:S(2)}, u32[]{:S(2)}) collective-permute-start(bf16[512,512]{1,0:T(8,128)(2,1)} %collective-permute-done.refs_1_), channel_id=1, source_target_pairs={{0,12},{1,13},{2,14},{3,15},{4,0},{5,1},{6,2},{7,3},{8,4},{9,5},{1... | collective-permute-start | bytes 1572872 | tf_op jit(solution)/shard_map/ppermute | solution.py:513
  83.0 29.6 %collective-permute-start.10 = (bf16[256,512]{1,0:T(8,128)(2,1)}, bf16[256,512]{1,0:T(8,128)(2,1)}, u32[]{:S(2)}, u32[]{:S(2)}) collective-permute-start(bf16[256,512]{1,0:T(8,128)(2,1)} %slice.23), channel_id=1, source_target_pairs={{0,12},{1,13},{2,14},{3,15},{4,0},{5,1},{6,2},{7,3},{8,4},{9,5},{1... | collective-permute-start | bytes 786440 | tf_op jit(solution)/shard_map/ppermute | solution.py:513
  83.1 118.5 %collective-permute-start.14 = (bf16[512,16,128]{2,1,0:T(8,128)(2,1)S(1)}, bf16[512,16,128]{2,1,0:T(8,128)(2,1)}, u32[]{:S(2)}, u32[]{:S(2)}) collective-permute-start(bf16[512,16,128]{2,1,0:T(8,128)(2,1)S(1)} %all-to-all-done.7.got_ref), channel_id=1, source_target_pairs={{0,1},{1,0},{2,3},{3,2},{4,5},{5,4},{6,7},{7,6},{8,9},{9,8},{10,11... | collective-permute-start | bytes 6291464 | tf_op jit(solution)/shard_map/ppermute | solution.py:507
  101.8 40.0 %all-to-all-start.1 = ((bf16[8,512,128]{2,1,0:T(8,128)(2,1)}), bf16[8,512,128]{2,1,0:T(8,128)(2,1)}, u32[]{:S(2)}, u32[]{:S(2)}) async-start(bf16[8,512,128]{2,1,0:T(8,128)(2,1)} %get-tuple-element.30), calls=%async_computation.1 | async-start | bytes 2097152 | tf_op jit(solution)/shard_map/all_to_all | solution.py:516
  109.4 16.4 %collective-permute-start.8 = (bf16[256,512]{1,0:T(8,128)(2,1)}, bf16[256,512]{1,0:T(8,128)(2,1)}, u32[]{:S(2)}, u32[]{:S(2)}) collective-permute-start(bf16[256,512]{1,0:T(8,128)(2,1)} %slice.22), channel_id=1, source_target_pairs={{0,4},{1,5},{2,6},{3,7},{4,8},{5,9},{6,10},{7,11},{8,12},{9,13},{1... | collective-permute-start | bytes 786440 | tf_op jit(solution)/shard_map/ppermute | solution.py:513
  112.7 20.0 %collective-permute-start.2 = (bf16[256,512]{1,0:T(8,128)(2,1)}, bf16[256,512]{1,0:T(8,128)(2,1)S(1)}, u32[]{:S(2)}, u32[]{:S(2)}) collective-permute-start(bf16[256,512]{1,0:T(8,128)(2,1)} %slice.20), channel_id=1, source_target_pairs={{0,4},{1,5},{2,6},{3,7},{4,8},{5,9},{6,10},{7,11},{8,12},{9,13},{1... | collective-permute-start | bytes 786440 | tf_op jit(solution)/shard_map/ppermute | solution.py:513
  112.7 20.7 %collective-permute-start.4 = (bf16[256,512]{1,0:T(8,128)(2,1)}, bf16[256,512]{1,0:T(8,128)(2,1)}, u32[]{:S(2)}, u32[]{:S(2)}) collective-permute-start(bf16[256,512]{1,0:T(8,128)(2,1)} %slice.21), channel_id=1, source_target_pairs={{0,12},{1,13},{2,14},{3,15},{4,0},{5,1},{6,2},{7,3},{8,4},{9,5},{1... | collective-permute-start | bytes 786440 | tf_op jit(solution)/shard_map/ppermute | solution.py:513
  134.3 12.7 %copy-start.22 = (bf16[512,128]{1,0:T(8,128)(2,1)S(1)}, bf16[512,128]{1,0:T(8,128)(2,1)}, u32[]{:S(2)}) copy-start(bf16[512,128]{1,0:T(8,128)(2,1)} %copy-done.21) | copy-start | bytes 393220
  139.5 17.9 %copy-start.39 = (s32[128,8]{0,1:T(8,128)S(1)}, s32[128,8]{0,1:T(8,128)}, u32[]{:S(2)}) copy-start(s32[128,8]{0,1:T(8,128)} %param.24) | copy-start | bytes 12292
  139.5 62.2 %collective-permute-start.11 = (f32[512,768]{1,0:T(8,128)}, f32[512,768]{1,0:T(8,128)}, u32[]{:S(2)}, u32[]{:S(2)}) collective-permute-start(f32[512,768]{1,0:T(8,128)} %get-tuple-element.29.far_ref), channel_id=1, source_target_pairs={{0,1},{1,0},{2,3},{3,2},{4,5},{5,4},{6,7},{7,6},{8,9},{9,8},{10,11... | collective-permute-start | bytes 4718600 | tf_op jit(solution)/shard_map/ppermute | solution.py:507
  141.7 11.9 %all-to-all-start.6 = ((bf16[8,64,128]{2,1,0:T(8,128)(2,1)}), bf16[8,64,128]{2,1,0:T(8,128)(2,1)S(1)}, u32[]{:S(2)}, u32[]{:S(2)}) async-start(bf16[8,64,128]{2,1,0:T(8,128)(2,1)} %get-tuple-element.34), calls=%async_computation.6 | async-start | bytes 262144 | tf_op jit(solution)/shard_map/all_to_all | solution.py:516
  153.6 33.4 %copy-start.25 = (bf16[8,64,128]{2,1,0:T(8,128)(2,1)}, bf16[8,64,128]{2,1,0:T(8,128)(2,1)S(1)}, u32[]{:S(2)}) copy-start(bf16[8,64,128]{2,1,0:T(8,128)(2,1)S(1)} %all-to-all-done.6.o_far) | copy-start | bytes 393220
  153.6 12.5 %all-to-all-start.2 = ((f32[16,32,128]{2,1,0:T(8,128)}), f32[16,32,128]{2,1,0:T(8,128)S(1)}, u32[]{:S(2)}, u32[]{:S(2)}) async-start(f32[16,32,128]{2,1,0:T(8,128)} %bitcast.30), calls=%async_computation.2 | async-start | bytes 524288 | tf_op jit(solution)/shard_map/all_to_all | solution.py:570
  157.4 37.5 %copy-start.6 = (bf16[8,64,512]{2,1,0:T(8,128)(2,1)S(1)}, bf16[8,64,512]{2,1,0:T(8,128)(2,1)}, u32[]{:S(2)}) copy-start(bf16[8,64,512]{2,1,0:T(8,128)(2,1)} %q_here.1) | copy-start | bytes 1572868
  166.8 14.1 %all-to-all-start.4 = ((bf16[8,64,512]{2,1,0:T(8,128)(2,1)}), bf16[8,64,512]{2,1,0:T(8,128)(2,1)S(1)}, u32[]{:S(2)}, u32[]{:S(2)}) async-start(bf16[8,64,512]{2,1,0:T(8,128)(2,1)} %get-tuple-element.32), calls=%async_computation.4 | async-start | bytes 1048576 | tf_op jit(solution)/shard_map/all_to_all | solution.py:516
  180.9 13.9 %all-to-all-start.3 = ((bf16[16,32,128]{2,1,0:T(8,128)(2,1)}), bf16[16,32,128]{2,1,0:T(8,128)(2,1)}, u32[]{:S(2)}, u32[]{:S(2)}) async-start(bf16[16,32,128]{2,1,0:T(8,128)(2,1)} %down_sum.1), calls=%async_computation.3 | async-start | bytes 262144 | tf_op jit(solution)/shard_map/all_to_all | solution.py:571
  187.0 14.7 %copy-start.31 = (s32[8,128]{1,0:T(8,128)S(1)}, s32[8,128]{1,0:T(8,128)}, u32[]{:S(2)}) copy-start(s32[8,128]{1,0:T(8,128)} %copy-done.30) | copy-start | bytes 12292
  (30 other events, 97.9 us)

commit v2 on v1

v2 whole, which is shorter than its diff:
```python
import functools
import math

import jax
import jax.numpy as jnp
import ml_dtypes
import numpy as np
from jax import lax
from jax.experimental import pallas as pl
from jax.experimental.pallas import tpu as pltpu
from jax.sharding import PartitionSpec as P

HEAD = 128
THETA = 500000.0
MIB = 1 << 20
VMEM_MIB = 60
POOL = 1024
ZERO_PAGE = POOL + 512

SLOT, PICK, SOURCE, TARGET, LEAVE = 0, 3, 8, 16, 24
KEPT, LENGTH, FROM = 0, 8, 16

F32 = jnp.float32
BF16 = jnp.bfloat16
I32 = jnp.int32


def iota(shape, axis):
    return lax.broadcasted_iota(I32, shape, axis)


def col_to_row(col):
    n = col.shape[0]
    return jnp.sum(jnp.where(iota((n, n), 0) == iota((n, n), 1), col, 0), axis=0, keepdims=True)


def row_to_col(row, n, stretch=1):
    w = row.shape[1]
    return jnp.sum(
        jnp.where(iota((n, w), 1) == iota((n, w), 0) // stretch, row, 0), axis=1, keepdims=True
    )


def below(mask):
    n = mask.shape[1]
    tri = (iota((n, n), 0) < iota((n, n), 1)).astype(BF16)
    return jnp.dot(mask.astype(BF16), tri, preferred_element_type=F32).astype(I32)


def plan_kernel(
    me_ref, mig_hbm, sra_hbm, ssa_hbm, len_hbm, prev_hbm, moved_hbm, tok_hbm,
    send_hbm, own_hbm, cand_hbm, meta_hbm,
    mig_ref, sra_ref, ssa_ref, len_ref, prev_ref, moved_ref, tok_ref, send_ref, own_ref, cand_ref, meta_ref, sem,
):
    loads = fetch(
        (
            (mig_hbm, mig_ref), (sra_hbm, sra_ref), (ssa_hbm, ssa_ref), (len_hbm, len_ref),
            (prev_hbm, prev_ref), (moved_hbm, moved_ref), (tok_hbm, tok_ref),
        ),
        sem,
    )
    settle(loads[:6])
    r = me_ref[0]
    groups, per = mig_ref.shape
    half = per // 2
    mig = mig_ref[...]
    grp, loc = mig // per, mig % per
    drow = iota((groups, per), 0)
    out_mask = ((grp == r) & (drow != r)).astype(I32)
    mine = jnp.sum(jnp.where(drow == r, mig, 0), axis=0, keepdims=True)
    g_in, loc_in = mine // per, mine % per
    in_mask = (g_in == drow).astype(I32)
    ranks = below(jnp.concatenate([out_mask, in_mask], axis=0))
    out_rank, in_ranks = ranks[:groups], ranks[groups:]
    in_rank = jnp.sum(in_mask * in_ranks, axis=0, keepdims=True)
    stay = g_in == r

    parts = []
    for d in range(groups):
        hit = (out_mask[d : d + 1] == 1) & (out_rank[d : d + 1] == iota((groups, per), 0))
        parts.append(jnp.sum(jnp.where(hit, loc[d : d + 1] + 1, 0), axis=1, keepdims=True))
    src_col = jnp.concatenate(parts, axis=0) - 1
    src_row = col_to_row(src_col)

    count = jnp.sum(jnp.where(drow == r, 0, in_mask), axis=1, keepdims=True)
    lane_u = iota((groups, half), 1)
    count_u = jnp.sum(jnp.where(iota((groups, half), 0) == lane_u // groups, count, 0), axis=0, keepdims=True)
    free = (lane_u[:1] % groups >= count_u).astype(I32)
    free_rank = jnp.where(free == 1, below(free), -1)
    free_col = row_to_col(free_rank, half)
    extra = jnp.sum(
        jnp.where(free_col == in_rank - half, iota((half, per), 0), 0), axis=0, keepdims=True
    )
    place = jnp.where(
        stay, jnp.where(in_rank < half, in_rank, half + extra), half + groups * g_in + in_rank
    )
    sel = place == iota((per, per), 0)

    def placed(row):
        return jnp.sum(jnp.where(sel, row, 0), axis=1, keepdims=True)

    slot_row = col_to_row(placed(iota((1, per), 1)))
    loc_row = col_to_row(placed(jnp.where(stay, loc_in, -1)))

    drow_sra = iota(sra_ref.shape, 0)
    sra = sra_ref[...]
    wanted = jnp.sum(jnp.where(drow_sra == r, sra, 0), axis=0, keepdims=True)
    ssa_col = row_to_col(ssa_ref[...], half)
    store = jnp.sum(jnp.where(ssa_col == wanted, iota((half, per), 0), 0), axis=0, keepdims=True)
    cand = jnp.where(store // groups == r, store % groups, groups + store // groups)
    cand_row = col_to_row(placed(cand))
    rows = per * 4
    cand_ref[...] = jnp.broadcast_to(row_to_col(cand_row, rows, 4), (rows, HEAD)).astype(BF16)
    picks = jnp.zeros((groups, 1), I32)
    lane_s = iota((1, half), 1)
    for i in range(groups):
        name = jnp.sum(jnp.where(lane_s == r * groups + i, ssa_ref[...], 0), axis=1, keepdims=True)
        used = jnp.max((sra == name).astype(I32), axis=1, keepdims=True)
        picks = jnp.maximum(picks, used * i)
    pick_row = jnp.sum(
        jnp.where(iota((groups, per), 0) == iota((groups, per), 1), picks, 0), axis=0, keepdims=True
    )

    len_col = jnp.broadcast_to(row_to_col(len_ref[...], rows, 4), (rows, HEAD))
    settle(loads[6:])
    tok = jnp.concatenate([tok_ref[...], len_col.astype(F32).astype(BF16)], axis=1)

    def rows_of(row, n):
        base = row_to_col(row, n, 4)
        at = 4 * base + iota((n, 1), 0) % 4
        pick = (jnp.broadcast_to(at, (n, rows)) == iota((n, rows), 1)) & (base >= 0)
        return jnp.dot(
            jnp.where(pick, 1.0, 0.0).astype(BF16), tok, preferred_element_type=F32
        ).astype(BF16)

    send_ref[...] = rows_of(src_row, rows // 2)
    stores = fetch(((send_ref, send_hbm),), sem)
    own_ref[...] = rows_of(loc_row, rows)
    stores += fetch(((own_ref, own_hbm),), sem, 1)
    src_wide = jnp.sum(
        jnp.where(iota((half, per), 0) == iota((half, per), 1), src_col, 0), axis=0, keepdims=True
    )
    def looked_up(table, row):
        pick = jnp.where(row == iota((per, per), 0), 1.0, 0.0).astype(BF16)
        parts = jnp.concatenate([table // 32, table % 32], axis=0).astype(F32).astype(BF16)
        found = jnp.dot(parts, pick, preferred_element_type=F32).astype(I32)
        return found[:8] * 32 + found[8:]

    prev, moved = prev_ref[...], moved_ref[...]
    lane8, row8 = iota((8, per), 1), iota((8, per), 0)
    source = jnp.where(loc_row >= 0, looked_up(prev, loc_row), POOL + (lane8 - half) * 8 + row8)
    target = looked_up(moved, slot_row)
    leave = looked_up(prev, src_wide)
    zero = jnp.zeros((groups - 4, per), I32)
    meta_ref[...] = jnp.concatenate(
        [slot_row, loc_row, src_wide, pick_row, zero, source, target, leave], axis=0
    )
    stores += fetch(((cand_ref, cand_hbm), (meta_ref, meta_hbm)), sem, 2)
    settle(stores)


def hspec():
    return pl.BlockSpec(memory_space=pltpu.HBM)


def fetch(pairs, sem, at=0):
    copies = [pltpu.make_async_copy(a, b, sem.at[at + n]) for n, (a, b) in enumerate(pairs)]
    for c in copies:
        c.start()
    return copies


def settle(copies):
    for c in copies:
        c.wait()


def sspec():
    return pl.BlockSpec(memory_space=pltpu.SMEM)


def params():
    return pltpu.CompilerParams(vmem_limit_bytes=VMEM_MIB * MIB)


def sds(shape, dtype):
    return jax.ShapeDtypeStruct(shape, dtype)


def plan(me, mig, sra, ssa, lengths, prev, moved, tok):
    rows = tok.shape[0]
    ins = (mig, sra, ssa, lengths, prev, moved, tok)
    outs = (
        sds((rows // 2, 640), BF16),
        sds((rows, 640), BF16),
        sds((rows, HEAD), BF16),
        sds((32, HEAD), I32),
    )
    return pl.pallas_call(
        plan_kernel,
        out_shape=outs,
        in_specs=[sspec()] + [hspec()] * 7,
        out_specs=(hspec(),) * 4,
        scratch_shapes=[pltpu.VMEM(a.shape, a.dtype) for a in ins + outs]
        + [pltpu.SemaphoreType.DMA((7,))],
        compiler_params=params(),
        name="plan",
    )(me, *ins)


def pack_adapters_kernel(meta_ref, down_hbm, q_hbm, k_hbm, out_hbm, q_ref, out_ref, sem):
    pairs = []
    for d in range(8):
        i = meta_ref[PICK, d]
        pairs.append((q_hbm.at[i], q_ref.at[d]))
        pairs.append((k_hbm.at[i], out_ref.at[d, 768:]))
        pairs.append((down_hbm.at[i], out_ref.at[d, :512]))
    loads = fetch(pairs, sem)
    for d in range(8):
        loads[3 * d].wait()
        q = q_ref[d]
        for h in range(4):
            out_ref[d, 512 + 64 * h : 576 + 64 * h] = q[:, h * HEAD : (h + 1) * HEAD]
        loads[3 * d + 1].wait()
        loads[3 * d + 2].wait()
    settle(fetch(((out_ref, out_hbm),), sem))


def pack_adapters(meta, down, up_q, up_kv):
    return pl.pallas_call(
        pack_adapters_kernel,
        out_shape=sds((8, 832, HEAD), BF16),
        in_specs=[sspec()] + [hspec()] * 3,
        out_specs=hspec(),
        scratch_shapes=[
            pltpu.VMEM(up_q.shape, BF16),
            pltpu.VMEM((8, 832, HEAD), BF16),
            pltpu.SemaphoreType.DMA((24,)),
        ],
        compiler_params=params(),
        name="pack_adapters",
    )(meta, down, up_q, up_kv)


def pack_cache_kernel(meta_ref, pool_hbm, cache_hbm, pool_ref, cache_ref, sem):
    settle(fetch(((pool_hbm, pool_ref),), sem))

    def some(g, _):
        pages = [pool_ref[meta_ref[LEAVE + b, 4 * g + e]] for e in range(4) for b in range(8)]
        for n, page in enumerate(pages):
            cache_ref[g * 32 + n] = page
        return 0

    lax.fori_loop(0, 16, some, 0)
    settle(fetch(((cache_ref, cache_hbm),), sem))


def pack_cache(meta, pool):
    return pl.pallas_call(
        pack_cache_kernel,
        out_shape=sds((512, 16, HEAD), BF16),
        in_specs=[sspec(), hspec()],
        out_specs=hspec(),
        scratch_shapes=[
            pltpu.VMEM(pool.shape, BF16),
            pltpu.VMEM((512, 16, HEAD), BF16),
            pltpu.SemaphoreType.DMA((1,)),
        ],
        compiler_params=params(),
        name="pack_cache",
    )(meta, pool)


def join_kernel(
    own_hbm, got_hbm, meta_hbm, after_ref, after2_ref, after3_ref, x_hbm, len_hbm, lens_hbm,
    own_ref, got_ref, meta_ref, x_ref, len_ref, lens_ref, sem,
):
    settle(fetch(((own_hbm, own_ref), (got_hbm, got_ref), (meta_hbm, meta_ref)), sem))
    rows = x_ref.shape[0]
    x_ref[: rows // 2] = own_ref[: rows // 2, :512]
    x_ref[rows // 2 :] = own_ref[rows // 2 :, :512] + got_ref[:, :512]
    store = fetch(((x_ref, x_hbm),), sem)
    length = jnp.concatenate(
        [own_ref[: rows // 2, 512:], own_ref[rows // 2 :, 512:] + got_ref[:, 512:]], axis=0
    ).astype(F32)
    len_ref[...] = length
    row = jnp.sum(
        jnp.where(iota((rows, HEAD), 0) == 4 * iota((rows, HEAD), 1), length, 0.0),
        axis=0,
        keepdims=True,
    ).astype(I32)
    kept = jnp.clip(row - 16 * iota((8, HEAD), 0), 0, 16)
    lens_ref[KEPT : KEPT + 8] = kept
    lens_ref[LENGTH : LENGTH + 8] = jnp.broadcast_to(row, (8, HEAD))
    lens_ref[FROM : FROM + 8] = jnp.where(kept > 0, meta_ref[SOURCE : SOURCE + 8], ZERO_PAGE)
    settle(store + fetch(((len_ref, len_hbm), (lens_ref, lens_hbm)), sem, 1))


def join(own, got, meta, *after):
    rows = own.shape[0]
    return pl.pallas_call(
        join_kernel,
        out_shape=(sds((rows, 512), BF16), sds((rows, HEAD), F32), sds((24, HEAD), I32)),
        in_specs=[hspec()] * 6,
        out_specs=(hspec(),) * 3,
        scratch_shapes=[
            pltpu.VMEM(own.shape, BF16),
            pltpu.VMEM(got.shape, BF16),
            pltpu.VMEM(meta.shape, I32),
            pltpu.VMEM((rows, 512), BF16),
            pltpu.VMEM((rows, HEAD), F32),
            pltpu.VMEM((24, HEAD), I32),
            pltpu.SemaphoreType.DMA((3,)),
        ],
        compiler_params=params(),
        name="join",
    )(own, got, meta, *after)


def slices_kernel(moves, n, *refs):
    outs = len({m[2] for m in moves})
    ins, dst = refs[:n], refs[-1 - 2 * outs : -1 - outs]
    tmp, sem = refs[-1 - outs : -1], refs[-1]
    loads = fetch(
        [(ins[i].at[lo:hi], tmp[o].at[at : at + hi - lo]) for i, (lo, hi), o, at in moves], sem
    )
    settle(loads)
    settle(fetch([(t, d) for t, d in zip(tmp, dst)], sem))


def slices(moves, rows, arrays, after):
    shapes = [(n, 512) for n in rows]
    return pl.pallas_call(
        functools.partial(slices_kernel, moves, len(arrays)),
        out_shape=tuple(sds(s, BF16) for s in shapes),
        in_specs=[hspec()] * (len(arrays) + len(after)),
        out_specs=(hspec(),) * len(rows),
        scratch_shapes=[pltpu.VMEM(s, BF16) for s in shapes]
        + [pltpu.SemaphoreType.DMA((len(moves),))],
        compiler_params=params(),
        name="slices",
    )(*arrays, *after)


def matmul_kernel(blocks, n, extra, js_ref, *refs):
    xs, refs = refs[:n], refs[n:]
    weights, refs = refs[:4], refs[4:]
    accs, refs = refs[:extra], refs[extra:]
    own_hbm, far_hbm, refs = refs[0], refs[1], refs[2:]
    bufs, refs = refs[:4], refs[4:]
    held, refs = refs[:n], refs[n:]
    acc, refs = refs[:extra], refs[extra:]
    own_ref, far_ref, x_sem, sem, acc_sem = refs
    nb = len(blocks)
    loads = fetch(list(zip(xs, held)), x_sem)
    copies = []
    for k in range(nb):
        at = pl.ds(pl.multiple_of(js_ref[k] * 512, 512), 512)
        copies.append(
            [
                pltpu.make_async_copy(
                    weights[w].at[at], bufs[w].at[k * 512 : (k + 1) * 512], sem.at[k, w]
                )
                for w in range(4)
            ]
        )
    for w in (2, 1, 3, 0):
        for k in range(nb):
            copies[k][w].start()
    acc_loads = fetch(list(zip(accs, acc)), acc_sem)
    settle(loads)
    x = []
    for parts in blocks:
        pieces = [held[i][lo:hi] for i, lo, hi in parts]
        x.append(pieces[0] if len(pieces) == 1 else jnp.concatenate(pieces, axis=0))
    x = jnp.concatenate(x, axis=1) if nb > 1 else x[0]

    def product(*which):
        for k in range(nb):
            for w in which:
                copies[k][w].wait()
        w = [bufs[w][...] for w in which]
        w = w[0] if len(w) == 1 else jnp.concatenate(w, axis=1)
        return jnp.dot(x, w, preferred_element_type=F32)

    far_q = product(2)
    settle(acc_loads)
    if extra:
        far_q = far_q + acc[1][:, :512]
    far_ref[:, :512] = far_q
    far_k = product(1, 3)
    if extra:
        far_k = far_k + acc[1][:, 512:]
    if extra == 3:
        far_k = far_k + jnp.concatenate([acc[2][:, 512:], jnp.zeros((512, HEAD), F32)], axis=1)
    far_ref[:, 512:] = far_k
    stores = fetch(((far_ref, far_hbm),), acc_sem, extra)
    own = product(0)
    if extra:
        own = own + acc[0][...]
    if extra == 3:
        own = own + acc[2][:, :512]
    own_ref[...] = own
    settle(stores + fetch(((own_ref, own_hbm),), acc_sem, extra + 1))


def matmul(js, blocks, xs, weights, accs=()):
    nb = len(blocks)
    outs = (sds((512, 512), F32), sds((512, 768), F32))
    return pl.pallas_call(
        functools.partial(matmul_kernel, blocks, len(xs), len(accs)),
        out_shape=outs,
        in_specs=[sspec()] + [hspec()] * (len(xs) + 4 + len(accs)),
        out_specs=(hspec(), hspec()),
        scratch_shapes=[pltpu.VMEM((nb * 512, w.shape[1]), BF16) for w in weights]
        + [pltpu.VMEM(a.shape, a.dtype) for a in (*xs, *accs, *outs)]
        + [
            pltpu.SemaphoreType.DMA((len(xs),)),
            pltpu.SemaphoreType.DMA((nb, 4)),
            pltpu.SemaphoreType.DMA((len(accs) + 2,)),
        ],
        compiler_params=params(),
        name="matmul%d" % nb,
    )(js, *xs, *weights, *accs)


def down_kernel(
    core_ref, x_hbm, here_hbm, far_hbm, cand_hbm, keep_hbm, give_hbm,
    x_ref, here_ref, far_ref, cand_ref, out_ref, sem,
):
    loads = fetch(
        ((x_hbm, x_ref), (here_hbm, here_ref), (cand_hbm, cand_ref), (far_hbm.at[:, :512], far_ref)),
        sem,
    )
    settle(loads[:3])
    x = x_ref[...]
    cand = cand_ref[...].astype(F32)
    acc = None
    for a in range(0, 16, 2):
        if a == 8:
            settle(loads[3:])
        ref = here_ref if a < 8 else far_ref
        b = a % 8
        w = jnp.concatenate([ref[b], ref[b + 1]], axis=1)
        y = jnp.dot(x, w, preferred_element_type=F32)
        y = jnp.where(cand == float(a), y[:, :HEAD], jnp.where(cand == float(a + 1), y[:, HEAD:], 0.0))
        acc = y if acc is None else acc + y
    out_ref[...] = acc
    half = out_ref.shape[0] // 2
    mine = pl.ds(pl.multiple_of(core_ref[0] * half, half), half)
    other = pl.ds(pl.multiple_of((1 - core_ref[0]) * half, half), half)
    settle(fetch(((out_ref.at[mine], keep_hbm), (out_ref.at[other], give_hbm)), sem))


def down_product(core, x, here, far, cand):
    rows = x.shape[0]
    return pl.pallas_call(
        down_kernel,
        out_shape=(sds((rows // 2, HEAD), F32),) * 2,
        in_specs=[sspec()] + [hspec()] * 4,
        out_specs=(hspec(), hspec()),
        scratch_shapes=[
            pltpu.VMEM(x.shape, BF16),
            pltpu.VMEM(here.shape, BF16),
            pltpu.VMEM(here.shape, BF16),
            pltpu.VMEM(cand.shape, BF16),
            pltpu.VMEM((rows, HEAD), F32),
            pltpu.SemaphoreType.DMA((4,)),
        ],
        compiler_params=params(),
        name="down_product",
    )(core, x, here, far, cand)


def turn_table():
    frequency = np.float32(THETA) ** (-(np.arange(HEAD // 2, dtype=np.float32) * 2.0 / HEAD))
    angles = np.arange(HEAD, dtype=np.float32)[:, None] * frequency.astype(np.float32)
    cos, sin = np.cos(angles.astype(np.float64)), np.sin(angles.astype(np.float64))
    rest = np.concatenate([cos, cos, -sin, sin], axis=1).astype(np.float32)
    terms = []
    for _ in range(3):
        terms.append(rest.astype(ml_dtypes.bfloat16))
        rest = rest - terms[-1].astype(np.float32)
    return np.concatenate(terms, axis=1)


def up_kernel(
    core_ref, mine_hbm, other_hbm, far_hbm, cand_hbm, q_hbm, k_hbm, len_hbm, table_hbm, after_ref,
    out_hbm, cos_hbm, sin_hbm,
    down_ref, far, cand_ref, q_here, k_here, len_ref, table_ref, out_ref, cos_ref, sin_ref, sem,
):
    half = mine_hbm.shape[0]
    mine = pl.ds(pl.multiple_of(core_ref[0] * half, half), half)
    other = pl.ds(pl.multiple_of((1 - core_ref[0]) * half, half), half)
    settle(
        fetch(
            (
                (mine_hbm, down_ref.at[mine]), (other_hbm, down_ref.at[other]),
                (far_hbm.at[:, 512:], far), (cand_hbm, cand_ref), (q_hbm, q_here),
                (k_hbm, k_here), (len_hbm, len_ref), (table_hbm, table_ref),
            ),
            sem,
        )
    )
    down = down_ref[...].astype(F32)
    cand = cand_ref[...].astype(F32)
    rows = down.shape[0]
    lane = iota((rows, HEAD), 1)
    upper = lane >= HEAD // 2
    other = pltpu.roll(down, HEAD // 2, 1)
    down_q = jnp.where(upper, other, down)
    down_k = jnp.where(upper, down, other)
    shift = jnp.where(upper, 1.0, 0.0)

    def spread(v):
        return jnp.concatenate(
            [jnp.where(cand == shift + float(2 * i), v, 0.0).astype(BF16) for i in range(8)], axis=1
        )

    sq, sk = spread(down_q), spread(down_k)
    q_all, k_all = q_here[...].reshape(512, 512), k_here[...].reshape(512, HEAD)

    def far_part(lo):
        return jnp.concatenate([far[a, lo : lo + 64] for a in range(8)], axis=0)

    w = [
        jnp.concatenate([q_all[:, h * HEAD : (h + 1) * HEAD], far_part(64 * h)], axis=0)
        for h in range(4)
    ]
    for h in (0, 2):
        out_ref[:, h * HEAD : (h + 2) * HEAD] = jnp.dot(
            sq, jnp.concatenate([w[h], w[h + 1]], axis=1), preferred_element_type=F32
        )
    out_ref[:, 512:] = jnp.dot(
        sk, jnp.concatenate([k_all, far_part(256)], axis=0), preferred_element_type=F32
    )
    position = len_ref[...].astype(I32) + iota((rows, HEAD), 0) % 4
    pick = jnp.where(position == lane, 1.0, 0.0).astype(BF16)
    turns = jnp.dot(pick, table_ref[...], preferred_element_type=F32)
    turns = turns[:, :256] + turns[:, 256:512] + turns[:, 512:]
    cos_ref[...] = turns[:, :HEAD]
    sin_ref[...] = turns[:, HEAD:]
    settle(fetch(((out_ref, out_hbm), (cos_ref, cos_hbm), (sin_ref, sin_hbm)), sem))


def up_product(core, mine, other, far, cand, up_q, up_kv, length, after):
    rows = cand.shape[0]
    ins = (cand, up_q, up_kv, length, jnp.asarray(turn_table()))
    outs = (sds((rows, 640), F32), sds((rows, HEAD), F32), sds((rows, HEAD), F32))
    return pl.pallas_call(
        up_kernel,
        out_shape=outs,
        in_specs=[sspec()] + [hspec()] * 9,
        out_specs=(hspec(),) * 3,
        scratch_shapes=[pltpu.VMEM((rows, HEAD), BF16), pltpu.VMEM((8, 320, HEAD), BF16)]
        + [pltpu.VMEM(a.shape, a.dtype) for a in ins + outs]
        + [pltpu.SemaphoreType.DMA((8,))],
        compiler_params=params(),
        name="up_product",
    )(core, mine, other, far, *ins, after)


GROUP = 4


def page_masks(mask_scr):
    for d in range(17):
        mask_scr[d] = jnp.where(iota((16, HEAD), 0) < d, 1.0, 0.0).astype(BF16)


def attend_kernel(
    par_ref, meta_ref, lens_ref,
    own_hbm, far_hbm, rx_hbm, cos_hbm, sin_hbm,
    pool_hbm, pool2_hbm, got_hbm, got2_hbm,
    out_hbm, new_hbm,
    own_ref, far_ref, rx_ref, cos_ref, sin_ref, out_ref, new_ref,
    q_scr, f_scr, page_scr, mask_scr, sem,
):
    odd = par_ref[0]
    copies = fetch(
        (
            (pool_hbm, page_scr.at[0, :POOL]), (got_hbm, page_scr.at[0, POOL:ZERO_PAGE]),
            (own_hbm, own_ref), (far_hbm, far_ref), (rx_hbm, rx_ref),
            (cos_hbm, cos_ref), (sin_hbm, sin_ref),
            (pool2_hbm, page_scr.at[1, :POOL]), (got2_hbm, page_scr.at[1, POOL:ZERO_PAGE]),
        ),
        sem,
    )
    page_masks(mask_scr)
    page_scr[0, ZERO_PAGE] = jnp.zeros((16, HEAD), BF16)
    settle(copies[:2])

    def keep(g, _):
        kept = []
        for e in range(4):
            for b in range(8):
                p = 4 * g + e
                kept.append((meta_ref[TARGET + b, p], page_scr[0, lens_ref[FROM + b, p]]))
        for at, page in kept:
            new_ref[at] = page
        return 0

    lax.fori_loop(0, 32, keep, 0)
    settle(copies[2:7])
    cos, sin = cos_ref[...], sin_ref[...]

    def turn(v):
        return v * cos + pltpu.roll(v, HEAD // 2, 1) * sin

    for h in range(4):
        at = slice(h * HEAD, (h + 1) * HEAD)
        q_scr[:, at] = turn(own_ref[:, at] + rx_ref[:, at])
    kv_own = far_ref[:, 512:640] + rx_ref[:, 640:768]
    kv_oth = far_ref[:, 640:768] + rx_ref[:, 512:640]
    key = turn(jnp.where(odd == 0, kv_own, kv_oth))
    value = jnp.where(odd == 0, kv_oth, kv_own)
    f_scr[:, :HEAD] = key
    f_scr[:, HEAD : 2 * HEAD] = value
    f_scr[:, 2 * HEAD :] = jnp.where(odd == 0, key, value)

    gap = jnp.where(
        iota((256, 32), 0) // 32 == iota((256, 32), 1) // 4,
        iota((256, 32), 0) % 32 - iota((256, 32), 1) % 4,
        -1,
    )
    c32 = iota((1, 32), 1) // 4

    def edge(g, _):
        at = [8 * g + e for e in range(8)]
        lengths = [lens_ref[LENGTH, p] for p in at]
        first = [jnp.minimum(n // 16, 6) for n in lengths]
        fresh = f_scr[pl.ds(pl.multiple_of(32 * g, 32), 32), 2 * HEAD :].astype(BF16)
        start = jnp.zeros((1, 32), I32)
        for e in range(8):
            start = jnp.where(c32 == e, lengths[e] - 16 * first[e], start)
        land = jnp.where(gap == start, 1.0, 0.0).astype(BF16)
        placed = jnp.dot(land, fresh, preferred_element_type=F32).astype(BF16)
        done = []
        for e, p in enumerate(at):
            for k in range(2):
                b = first[e] + k
                lo = e * 32 + k * 16
                page = page_scr[0, meta_ref[SOURCE + b, p]] * mask_scr[lens_ref[KEPT + b, p]]
                done.append((meta_ref[TARGET + b, p], page + placed[lo : lo + 16]))
        for to, page in done:
            new_ref[to] = page
        return 0

    scale = 1.0 / math.sqrt(HEAD)
    row2 = (iota((32, HEAD), 0) % 8) // 4
    lane32 = iota((32, HEAD), 1)
    col_a = jnp.where(row2 == 0, lane32, HEAD)
    col_b = jnp.where(row2 == 1, lane32, HEAD)
    row = iota((HEAD, HEAD), 0)
    col_new = iota((HEAD, HEAD), 1) - (row // 32) * 8 - (row % 8) // 4 * 4
    contract = (((1,), (1,)), ((), ()))

    def mix(g, _):
        q32 = q_scr[pl.ds(pl.multiple_of(32 * g, 32), 32), :]
        q = jnp.concatenate(
            [
                q32[8 * k : 8 * k + 8, h * HEAD : (h + 1) * HEAD]
                for k in range(GROUP)
                for h in range(4)
            ],
            axis=0,
        ).astype(BF16)
        block = pl.ds(pl.multiple_of((g // 4) * HEAD, HEAD), HEAD)
        fresh_k = f_scr[block, :HEAD].astype(BF16)
        fresh_v = f_scr[block, HEAD : 2 * HEAD].astype(BF16)
        new = lax.dot_general(q, fresh_k, contract, preferred_element_type=F32)
        rel = col_new - 32 * (g % 4)
        new = jnp.where((rel >= 0) & (rel <= row % 4), new, -1e30)
        lengths = [lens_ref[LENGTH, 8 * g + e] for e in range(8)]
        index = [meta_ref[SOURCE + b, 8 * g + e] for e in range(8) for b in range(8)]
        old_a, old_b = [], []
        for k in range(GROUP):
            keys = jnp.concatenate([page_scr[odd, j] for j in index[16 * k : 16 * k + 16]], axis=0)
            old = lax.dot_general(
                q[32 * k : 32 * k + 32], keys, contract, preferred_element_type=F32
            )
            old_a.append(jnp.where(col_a < lengths[2 * k], old[:, :HEAD], -1e30))
            old_b.append(jnp.where(col_b < lengths[2 * k + 1], old[:, HEAD:], -1e30))
        old_a, old_b = jnp.concatenate(old_a, axis=0), jnp.concatenate(old_b, axis=0)
        top = jnp.max(jnp.maximum(jnp.maximum(old_a, old_b), new), axis=1, keepdims=True)
        old_a, old_b, new = (jnp.exp((v - top) * scale) for v in (old_a, old_b, new))
        part = 1.0 / jnp.sum(old_a + old_b + new, axis=1, keepdims=True)
        old = jnp.concatenate([old_a * part, old_b * part], axis=1).astype(BF16)
        mixed = jnp.dot((new * part).astype(BF16), fresh_v, preferred_element_type=F32)
        old_mixed = []
        for k in range(GROUP):
            values = jnp.concatenate(
                [page_scr[1 - odd, j] for j in index[16 * k : 16 * k + 16]], axis=0
            )
            old_mixed.append(
                jnp.dot(old[32 * k : 32 * k + 32], values, preferred_element_type=F32)
            )
        mixed = (mixed + jnp.concatenate(old_mixed, axis=0)).astype(BF16)
        for k in range(GROUP):
            for e in range(2):
                slot = meta_ref[SLOT, 8 * g + 2 * k + e]
                for h in range(4):
                    lo = k * 32 + h * 8 + e * 4
                    out_ref[slot, :, h * HEAD : (h + 1) * HEAD] = mixed[lo : lo + 4]
        return 0

    lax.fori_loop(0, 16, edge, 0)
    stores = fetch(((new_ref, new_hbm),), sem)
    settle(copies[7:])
    lax.fori_loop(0, 16, mix, 0)
    settle(stores + fetch(((out_ref, out_hbm),), sem, 1))


def attend(parity, meta, lens, own, far, rx, cos, sin, pool, pool2, got, got2):
    outs = (sds((128, 4, 512), BF16), sds(pool.shape, BF16))
    return pl.pallas_call(
        attend_kernel,
        out_shape=outs,
        in_specs=[sspec()] * 3 + [hspec()] * 9,
        out_specs=(hspec(), hspec()),
        scratch_shapes=[pltpu.VMEM(a.shape, a.dtype) for a in (own, far, rx, cos, sin, *outs)]
        + [
            pltpu.VMEM((512, 512), F32),
            pltpu.VMEM((512, 3 * HEAD), F32),
            pltpu.VMEM((2, ZERO_PAGE + 1, 16, HEAD), BF16),
            pltpu.VMEM((17, 16, HEAD), BF16),
            pltpu.SemaphoreType.DMA((9,)),
        ],
        compiler_params=params(),
        name="attend",
    )(parity, meta, lens, own, far, rx, cos, sin, pool, pool2, got, got2)


def body(
    tokens,
    query_weight_matrix,
    key_value_weight,
    adapter_down_factors,
    adapter_up_query,
    adapter_up_key_value,
    storage_slot_adapter,
    slot_request_adapter,
    migration,
    lengths,
    previous_block_table,
    moved_block_table,
    paged_cache_pool,
):
    r = lax.axis_index("rep").astype(I32)
    t = lax.axis_index("tp").astype(I32)
    core = t % 2

    def other_core(a):
        return lax.ppermute(a, "tp", [(i, i ^ 1) for i in range(16)])

    def other_x(a):
        return lax.ppermute(a, "tp", [(i, i ^ 2) for i in range(16)])

    def along_y(a, d):
        return lax.ppermute(a, "tp", [(i, (i + 4 * d) % 16) for i in range(16)])

    def swap_rep(a):
        return lax.all_to_all(a, "rep", split_axis=0, concat_axis=0, tiled=True)

    send, own, cand, meta = plan(
        r.reshape(1), migration.reshape(8, 128), slot_request_adapter.reshape(8, 128),
        storage_slot_adapter.reshape(1, 64), lengths.reshape(1, 128),
        previous_block_table.T, moved_block_table.T, tokens.reshape(512, 512),
    )
    packed = pack_adapters(meta, adapter_down_factors, adapter_up_query, adapter_up_key_value)
    pool2 = other_core(paged_cache_pool)
    vq, vk = other_core(query_weight_matrix), other_core(key_value_weight)
    leaving = pack_cache(meta, paged_cache_pool)
    x, length, lens = join(own, swap_rep(send), meta, packed, leaving, pool2)
    far = swap_rep(packed)

    hi = (t // 2) % 2
    y = t // 4

    def js(*blocks):
        at = [(((y + dy) % 4) * 2 + (hi ^ dx)) * 2 + core for dy, dx in blocks]
        return jnp.stack(at).astype(I32)

    weights = (query_weight_matrix, key_value_weight, vq, vk)
    one = core.reshape(1)
    xh = other_x(x)
    yp = along_y(x, 1)
    ym = along_y(x, -1)
    full = (0, 512)
    up, dn = slices(
        ((0, (0, 512), 0, 0), (1, (0, 256), 0, 512), (0, (0, 512), 1, 0), (2, (256, 512), 1, 512)),
        (768, 768), (xh, yp, ym), (vq, vk),
    )
    leaving, far, _ = lax.optimization_barrier((leaving, far, up))
    got = swap_rep(leaving)
    got2 = other_core(got)
    up, dn = along_y(up, 1), along_y(dn, -1)
    acc = matmul(
        js((0, 0), (0, 1), (3, 0), (1, 0)),
        tuple(((i, *full),) for i in range(4)),
        (x, xh, yp, ym), weights,
    )
    keep, give = down_product(one, x, adapter_down_factors, far, cand)
    up2, dn2 = slices(
        ((0, (0, 256), 0, 0), (1, (256, 512), 1, 0)), (256, 256), (up, dn), (acc[0], keep)
    )
    last = (along_y(up2, 1), along_y(dn2, -1))
    total = keep + other_core(give)
    total = total + other_x(total)
    total = (total + along_y(total, 2)) + (along_y(total, 1) + along_y(total, -1))
    total = total.astype(BF16)
    delta, cos, sin = up_product(
        one, total, other_core(total), far, cand, adapter_up_query, adapter_up_key_value, length,
        acc[0],
    )
    acc_own, acc_far = matmul(
        js((3, 1), (1, 1), (2, 0), (2, 1)),
        (
            ((0, *full),), ((1, *full),), ((0, 512, 768), (1, 512, 768)),
            ((2, 0, 256), (3, 0, 256)),
        ),
        (up, dn, *last), weights, (*acc, delta),
    )
    rx = other_core(acc_far)
    return attend(
        one, meta, lens, acc_own, acc_far, rx, cos, sin, paged_cache_pool, pool2, got, got2
    )


def solution(mesh):
    in_specs = (
        P("rep", None, "tp"),
        P(None, "tp"),
        P(None, "tp"),
        P("rep", "tp", None),
        P("rep", None, "tp"),
        P("rep", None, "tp"),
        P(),
        P(),
        P(),
        P("rep"),
        P("rep", None),
        P("rep", None),
        P("rep", None, "tp"),
    )
    out_specs = (P("rep", None, "tp"), P("rep", None, "tp"))
    return jax.shard_map(body, mesh=mesh, in_specs=in_specs, out_specs=out_specs, check_vma=False)
```

time: 250 us -> 161 us (0.64)
  local copies, waits for them, and re-layouts: 30.7 us -> 5.34 us
  waiting for transfers between devices: 61.8 us -> 39.3 us
  Pallas kernels: 82.9 us -> 68.1 us
  starting transfers between devices: 56.5 us -> 43.9 us
  blocking collectives: 10.2 us -> 0 us
  other arithmetic: 4.95 us -> 2.15 us
    ppermute x1 -> x2, waiting for transfers between devices: 31.6 us -> 8.31 us  [other_x(): return lax.ppermute(a, 'tp', [(i, i ^ 2) for i in range(16)])]
    pallas_call x9, Pallas kernels: 79.8 us -> 60.7 us  [the longest x1 21.6 us: attend(): pl.pallas_call(attend_kernel, out_shape=outs, in_specs=[sspec()] * 3 + [h...]
    unnamed x82 -> x24, local copies, waits for them, and re-layouts: 18.9 us -> 3.38 us
    all_to_all x2 -> x0, waiting for transfers between devices: 14.3 us -> none  [the longest x1 8.61 us: body(): lax.all_to_all(partial, 'tp', split_axis=0, concat_axis=0, tiled=True)]
    all_to_all x5 -> x3, starting transfers between devices: 25.5 us -> 15 us  [swap_rep(): return lax.all_to_all(a, 'rep', split_axis=0, concat_axis=0, tiled=True)]
    all_to_all x1 -> x0, blocking collectives: 10.2 us -> none  [swap_rep(): return lax.all_to_all(a, 'rep', split_axis=0, concat_axis=0, tiled=True)]
    all_to_all x2 -> x0, starting transfers between devices: 9.87 us -> none  [the longest x1 6.1 us: body(): lax.all_to_all(down_sum(pieces.reshape(16, 32, HEAD)).reshape(512, HEAD),...]
    all_to_all x5 -> x3, waiting for transfers between devices: 5.32 us -> 15.2 us  [swap_rep(): return lax.all_to_all(a, 'rep', split_axis=0, concat_axis=0, tiled=True)]
  transfers between devices with their start and end apart: 22 -> 21, of which waited for: 6 -> 8; matrix products, arithmetic and copies ran while one was open for 5% -> 3% of each run, Pallas kernels for 15% -> 29%
where the time goes in v2:
time: 161 us; the launch traced here: 160 us
  Pallas kernels  68.1 us (42%)
  starting transfers between devices  43.9 us (27%)
  waiting for transfers between devices  39.3 us (24%)
  local copies, waits for them, and re-layouts  5.34 us (3%)
  other arithmetic  2.15 us (1%)
    pallas_call x1, Pallas kernels, attend(): pl.pallas_call(attend_kernel, out_shape=outs, in_specs=[sspec()] * 3 + [h...  21.6 us
    pallas_call x2, Pallas kernels, matmul(): pl.pallas_call(functools.partial(matmul_kernel, blocks, len(xs), len(accs...  19.7 us
    all_to_all x3, waiting for transfers between devices, swap_rep(): return lax.all_to_all(a, 'rep', split_axis=0, concat_axis=0, tiled=True)  15.2 us
    all_to_all x3, starting transfers between devices, swap_rep(): return lax.all_to_all(a, 'rep', split_axis=0, concat_axis=0, tiled=True)  15 us
    ppermute x9, starting transfers between devices, along_y(): return lax.ppermute(a, 'tp', [(i, (i + 4 * d) % 16) for i in range(16)])  12.7 us
    ppermute x7, starting transfers between devices, other_core(): return lax.ppermute(a, 'tp', [(i, i ^ 1) for i in range(16)])  12 us
    ppermute x9, waiting for transfers between devices, along_y(): return lax.ppermute(a, 'tp', [(i, (i + 4 * d) % 16) for i in range(16)])  11 us
    ppermute x2, waiting for transfers between devices, other_x(): return lax.ppermute(a, 'tp', [(i, i ^ 2) for i in range(16)])  8.31 us
  transfers between devices with their start and end apart: 21, of which 8 were waited for; matrix products, arithmetic and copies ran while one was open for 3% of the time, Pallas kernels for 29%

profile of v2, /device:TPU:1, one launch (start us, length us, event | category | flops | bytes accessed | tf_op | source)
XLA Modules:
  0.0 159.8 jit_solution(11455336446826567360)
XLA Ops:
  0.6 1.5 collective-permute-start.4
  2.6 2.0 %reshape.33.tok_hbm = bf16[512,512]{1,0:T(8,128)(2,1)} reshape(bf16[128,4,512]{2,1,0:T(4,128)(2,1)} %param.14) | data formatting | bytes 1048576 | tf_op jit(solution)/shard_map/reshape | solution.py:768
  4.6 3.5 %plan.1 = (bf16[256,640]{1,0:T(8,128)(2,1)}, bf16[512,640]{1,0:T(8,128)(2,1)}, bf16[512,128]{1,0:T(8,128)(2,1)}, s32[32,128]{1,0:T(8,128)}) custom-call(s32[1]{0:T(128)} %bitcast.1.me_ref, s32[8,128]{1,0:T(8,128)} %bitcast.20, s32[8,128]{1,0:T(8,128)} %bitcast.21, s32[1,64]{1,0:T(1,128)} %bitcast.24, s32[1,128]{1,0:T(1,128)} %bitcast.25, s32[8,128]{1,0:T(8,128)} %bitcast.22, ...), custom_call_target="tpu_custom_call" | custom-call | tf_op jit(solution)/shard_map/plan/pallas_call | solution.py:199
  8.1 6.1 %all-to-all-start = ((bf16[8,32,640]{2,1,0:T(8,128)(2,1)}), bf16[8,32,640]{2,1,0:T(8,128)(2,1)S(1)}, u32[]{:S(2)}, u32[]{:S(2)}) async-start(bf16[8,32,640]{2,1,0:T(8,128)(2,1)} %bitcast.19), calls=%async_computation | async-start | bytes 655360 | tf_op jit(solution)/shard_map/all_to_all | solution.py:763
  14.2 3.9 %pack_adapters.1.after_ref = bf16[8,832,128]{2,1,0:T(8,128)(2,1)} custom-call(s32[32,128]{1,0:T(8,128)} %get-tuple-element.24.meta_ref.meta_hbm, bf16[8,512,128]{2,1,0:T(8,128)(2,1)} %here_hbm.1, bf16[8,64,512]{2,1,0:T(8,128)(2,1)} %q_hbm.3, bf16[8,64,128]{2,1,0:T(8,128)(2,1)} %k_hbm.3), custom_call_target="tpu_custom_call" | custom-call | tf_op jit(solution)/shard_map/pack_adapters/pallas_call | solution.py:230
  18.1 3.8 %all-to-all-done = bf16[8,32,640]{2,1,0:T(8,128)(2,1)S(1)} async-done(((bf16[8,32,640]{2,1,0:T(8,128)(2,1)}), bf16[8,32,640]{2,1,0:T(8,128)(2,1)S(1)}, u32[]{:S(2)}, u32[]{:S(2)}) %all-to-all-start) | async-done | bytes 327712 | tf_op jit(solution)/shard_map/all_to_all | solution.py:763
  21.9 4.3 %all-to-all-start.1 = ((bf16[8,832,128]{2,1,0:T(8,128)(2,1)}), bf16[8,832,128]{2,1,0:T(8,128)(2,1)}, u32[]{:S(2)}, u32[]{:S(2)}) async-start(bf16[8,832,128]{2,1,0:T(8,128)(2,1)} %pack_adapters.1.after_ref), calls=%async_computation.1 | async-start | bytes 3407872 | tf_op jit(solution)/shard_map/all_to_all | solution.py:763
  26.2 5.2 %pack_cache.1.after2_ref = bf16[512,16,128]{2,1,0:T(8,128)(2,1)} custom-call(s32[32,128]{1,0:T(8,128)} %get-tuple-element.24.meta_ref.meta_hbm, bf16[1024,16,128]{2,1,0:T(8,128)(2,1)} %pool_hbm.3), custom_call_target="tpu_custom_call" | custom-call | tf_op jit(solution)/shard_map/pack_cache/pallas_call | solution.py:259
  31.5 2.1 %join.1 = (bf16[512,512]{1,0:T(8,128)(2,1)}, f32[512,128]{1,0:T(8,128)}, s32[24,128]{1,0:T(8,128)}) custom-call(bf16[512,640]{1,0:T(8,128)(2,1)} %get-tuple-element.25.own_hbm, bf16[256,640]{1,0:T(8,128)(2,1)} %bitcast.18, s32[32,128]{1,0:T(8,128)} %get-tuple-element.24.meta_ref.meta_hbm, bf16[8,832,128]{2,1,0:T(8,128)(2,1)} %pack_adapters.1.after_ref, ...), custom_call_target="tpu_custom_call" | custom-call | tf_op jit(solution)/shard_map/join/pallas_call | solution.py:301
  33.7 2.8 %collective-permute-start.3 = (bf16[512,512]{1,0:T(8,128)(2,1)}, bf16[512,512]{1,0:T(8,128)(2,1)S(1)}, u32[]{:S(2)}, u32[]{:S(2)}) collective-permute-start(bf16[512,512]{1,0:T(8,128)(2,1)} %get-tuple-element.28.refs_0_.x_hbm), channel_id=1, source_target_pairs={{0,12},{1,13},{2,14},{3,15},{4,0},{5,1},{6,2},{7,3},{8,4},{9,5},{1... | collective-permute-start | bytes 1572872 | tf_op jit(solution)/shard_map/ppermute | solution.py:760
  36.5 2.5 %collective-permute-start.1 = (bf16[512,512]{1,0:T(8,128)(2,1)}, bf16[512,512]{1,0:T(8,128)(2,1)S(1)}, u32[]{:S(2)}, u32[]{:S(2)}) collective-permute-start(bf16[512,512]{1,0:T(8,128)(2,1)} %get-tuple-element.28.refs_0_.x_hbm), channel_id=1, source_target_pairs={{0,2},{1,3},{2,0},{3,1},{4,6},{5,7},{6,4},{7,5},{8,10},{9,11},{10,... | collective-permute-start | bytes 1572872 | tf_op jit(solution)/shard_map/ppermute | solution.py:757
  38.9 7.9 %collective-permute-done.3.refs_2_.refs_3_ = bf16[512,512]{1,0:T(8,128)(2,1)S(1)} collective-permute-done((bf16[512,512]{1,0:T(8,128)(2,1)}, bf16[512,512]{1,0:T(8,128)(2,1)S(1)}, u32[]{:S(2)}, u32[]{:S(2)}) %collective-permute-start.3) | collective-permute-done | bytes 524320 | tf_op jit(solution)/shard_map/ppermute | solution.py:760
  46.8 3.1 %collective-permute-done.2.refs_1_.refs_2_ = bf16[512,512]{1,0:T(8,128)(2,1)S(1)} collective-permute-done((bf16[512,512]{1,0:T(8,128)(2,1)}, bf16[512,512]{1,0:T(8,128)(2,1)S(1)}, u32[]{:S(2)}, u32[]{:S(2)}) %collective-permute-start.2) | collective-permute-done | bytes 524320 | tf_op jit(solution)/shard_map/ppermute | solution.py:760
  49.9 8.3 %collective-permute-done.1.refs_0_.refs_1_ = bf16[512,512]{1,0:T(8,128)(2,1)S(1)} collective-permute-done((bf16[512,512]{1,0:T(8,128)(2,1)}, bf16[512,512]{1,0:T(8,128)(2,1)S(1)}, u32[]{:S(2)}, u32[]{:S(2)}) %collective-permute-start.1) | collective-permute-done | bytes 524320 | tf_op jit(solution)/shard_map/ppermute | solution.py:757
  59.1 2.7 %slices.2 = (bf16[768,512]{1,0:T(8,128)(2,1)}, bf16[768,512]{1,0:T(8,128)(2,1)}) custom-call(bf16[512,512]{1,0:T(8,128)(2,1)} %copy-done.5, bf16[512,512]{1,0:T(8,128)(2,1)} %copy-done.4, bf16[512,512]{1,0:T(8,128)(2,1)} %copy-done.3, bf16[8192,512]{1,0:T(8,128)(2,1)} %collective-permute-done.4.refs_3_.refs_6_, bf16[8192,128]{1,0:T(8,128)(2,1)} %copy-done), custom_call_target="tpu_custom_call" | custom-call | tf_op jit(solution)/shard_map/slices/pallas_call | solution.py:333
  61.8 4.6 %all-to-all-start.2 = ((bf16[512,16,128]{2,1,0:T(8,128)(2,1)}), bf16[512,16,128]{2,1,0:T(8,128)(2,1)S(1)}, u32[]{:S(2)}, u32[]{:S(2)}) async-start(bf16[512,16,128]{2,1,0:T(8,128)(2,1)} %pack_cache.1.after2_ref), calls=%async_computation.2 | async-start | bytes 4194304 | tf_op jit(solution)/shard_map/all_to_all | solution.py:763
  66.3 2.7 %collective-permute-start.7 = (bf16[768,512]{1,0:T(8,128)(2,1)}, bf16[768,512]{1,0:T(8,128)(2,1)S(1)}, u32[]{:S(2)}, u32[]{:S(2)}) collective-permute-start(bf16[768,512]{1,0:T(8,128)(2,1)} %get-tuple-element.30), channel_id=1, source_target_pairs={{0,12},{1,13},{2,14},{3,15},{4,0},{5,1},{6,2},{7,3},{8,4},{9,5},{1... | collective-permute-start | bytes 2359304 | tf_op jit(solution)/shard_map/ppermute | solution.py:760
  69.1 3.6 %down_product.1 = (f32[256,128]{1,0:T(8,128)}, f32[256,128]{1,0:T(8,128)}) custom-call(s32[1]{0:T(128)} %bitcast.core_ref.par_ref, bf16[512,512]{1,0:T(8,128)(2,1)} %get-tuple-element.28.refs_0_.x_hbm, bf16[8,512,128]{2,1,0:T(8,128)(2,1)} %here_hbm.1, bf16[8,832,128]{2,1,0:T(8,128)(2,1)} %all-to-all-done.1.far_hbm, bf16[512,128]{1,0:T(8,128)(2,1)} %get-tuple-element.33.cand_hbm), custom_call_target="tpu_custom_call" | custom-call | tf_op jit(solution)/shard_map/down_product/pallas_call | solution.py:457
  72.6 2.8 %collective-permute-start.10 = (f32[256,128]{1,0:T(8,128)}, f32[256,128]{1,0:T(8,128)S(1)}, u32[]{:S(2)}, u32[]{:S(2)}) collective-permute-start(f32[256,128]{1,0:T(8,128)} %get-tuple-element.38), channel_id=1, source_target_pairs={{0,1},{1,0},{2,3},{3,2},{4,5},{5,4},{6,7},{7,6},{8,9},{9,8},{10,11... | collective-permute-start | bytes 393224 | tf_op jit(solution)/shard_map/ppermute | solution.py:754
  77.5 1.8 %collective-permute-start.11 = (f32[256,128]{1,0:T(8,128)S(1)}, f32[256,128]{1,0:T(8,128)S(1)}, u32[]{:S(2)}, u32[]{:S(2)}) collective-permute-start(f32[256,128]{1,0:T(8,128)S(1)} %add.125), channel_id=1, source_target_pairs={{0,2},{1,3},{2,0},{3,1},{4,6},{5,7},{6,4},{7,5},{8,10},{9,11},{10,... | collective-permute-start | bytes 393224 | tf_op jit(solution)/shard_map/ppermute | solution.py:757
  79.3 11.3 %all-to-all-done.2.got_hbm = bf16[512,16,128]{2,1,0:T(8,128)(2,1)S(1)} async-done(((bf16[512,16,128]{2,1,0:T(8,128)(2,1)}), bf16[512,16,128]{2,1,0:T(8,128)(2,1)S(1)}, u32[]{:S(2)}, u32[]{:S(2)}) %all-to-all-start.2) | async-done | bytes 2097184 | tf_op jit(solution)/shard_map/all_to_all | solution.py:763
  90.6 5.0 %collective-permute-start.17 = (bf16[512,16,128]{2,1,0:T(8,128)(2,1)S(1)}, bf16[512,16,128]{2,1,0:T(8,128)(2,1)}, u32[]{:S(2)}, u32[]{:S(2)}) collective-permute-start(bf16[512,16,128]{2,1,0:T(8,128)(2,1)S(1)} %all-to-all-done.2.got_hbm), channel_id=1, source_target_pairs={{0,1},{1,0},{2,3},{3,2},{4,5},{5,4},{6,7},{7,6},{8,9},{9,8},{10,11... | collective-permute-start | bytes 6291464 | tf_op jit(solution)/shard_map/ppermute | solution.py:754
  95.7 2.8 %collective-permute-start.14 = (f32[256,128]{1,0:T(8,128)S(1)}, f32[256,128]{1,0:T(8,128)S(1)}, u32[]{:S(2)}, u32[]{:S(2)}) collective-permute-start(f32[256,128]{1,0:T(8,128)S(1)} %add.126), channel_id=1, source_target_pairs={{0,12},{1,13},{2,14},{3,15},{4,0},{5,1},{6,2},{7,3},{8,4},{9,5},{1... | collective-permute-start | bytes 393224 | tf_op jit(solution)/shard_map/ppermute | solution.py:760
  98.5 1.6 %collective-permute-start.12 = (f32[256,128]{1,0:T(8,128)S(1)}, f32[256,128]{1,0:T(8,128)S(1)}, u32[]{:S(2)}, u32[]{:S(2)}) collective-permute-start(f32[256,128]{1,0:T(8,128)S(1)} %add.126), channel_id=1, source_target_pairs={{0,8},{1,9},{2,10},{3,11},{4,12},{5,13},{6,14},{7,15},{8,0},{9,1},... | collective-permute-start | bytes 393224 | tf_op jit(solution)/shard_map/ppermute | solution.py:760
  100.7 9.2 %matmul4.2 = (f32[512,512]{1,0:T(8,128)}, f32[512,768]{1,0:T(8,128)}) custom-call(s32[4]{0:T(128)} %pad_add_fusion.1.js_ref, bf16[512,512]{1,0:T(8,128)(2,1)} %get-tuple-element.28.refs_0_.x_hbm, bf16[512,512]{1,0:T(8,128)(2,1)} %copy-done.5, bf16[512,512]{1,0:T(8,128)(2,1)} %copy-done.4, bf16[512,512]{1,0:T(8,128)(2,1)} %copy-done.3, ...), custom_call_target="tpu_custom_call" | custom-call | tf_op jit(solution)/shard_map/matmul4/pallas_call | solution.py:410
  109.9 1.8 %slices.3 = (bf16[256,512]{1,0:T(8,128)(2,1)}, bf16[256,512]{1,0:T(8,128)(2,1)}) custom-call(bf16[768,512]{1,0:T(8,128)(2,1)} %collective-permute-done.6.refs_0_, bf16[768,512]{1,0:T(8,128)(2,1)} %copy-done.2, f32[512,512]{1,0:T(8,128)} %get-tuple-element.31.refs_2_.after_ref.refs_8_, f32[256,128]{1,0:T(8,128)} %get-tuple-element.34.refs_3_), custom_call_target="tpu_custom_call" | custom-call | tf_op jit(solution)/shard_map/slices/pallas_call | solution.py:333
  111.8 1.7 %collective-permute-start.8 = (bf16[256,512]{1,0:T(8,128)(2,1)}, bf16[256,512]{1,0:T(8,128)(2,1)S(1)}, u32[]{:S(2)}, u32[]{:S(2)}) collective-permute-start(bf16[256,512]{1,0:T(8,128)(2,1)} %get-tuple-element.35), channel_id=1, source_target_pairs={{0,4},{1,5},{2,6},{3,7},{4,8},{5,9},{6,10},{7,11},{8,12},{9,13},{1... | collective-permute-start | bytes 786440 | tf_op jit(solution)/shard_map/ppermute | solution.py:760
  114.6 1.7 %collective-permute-start.15 = (bf16[256,128]{1,0:T(8,128)(2,1)S(1)}, bf16[256,128]{1,0:T(8,128)(2,1)S(1)}, u32[]{:S(2)}, u32[]{:S(2)}) collective-permute-start(bf16[256,128]{1,0:T(8,128)(2,1)S(1)} %add_convert_fusion.mine_hbm), channel_id=1, source_target_pairs={{0,1},{1,0},{2,3},{3,2},{4,5},{5,4},{6,7},{7,6},{8,9},{9,8},{10,11... | collective-permute-start | bytes 196616 | tf_op jit(solution)/shard_map/ppermute | solution.py:754
  117.8 4.0 %up_product.1 = (f32[512,640]{1,0:T(8,128)}, f32[512,128]{1,0:T(8,128)}, f32[512,128]{1,0:T(8,128)}) custom-call(s32[1]{0:T(128)} %bitcast.core_ref.par_ref, bf16[256,128]{1,0:T(8,128)(2,1)} %copy-done.10, bf16[256,128]{1,0:T(8,128)(2,1)} %copy-done.11, bf16[8,832,128]{2,1,0:T(8,128)(2,1)} %all-to-all-done.1.far_hbm, ...), custom_call_target="tpu_custom_call" | custom-call | tf_op jit(solution)/shard_map/up_product/pallas_call | solution.py:550
  122.6 10.5 %matmul4.3 = (f32[512,512]{1,0:T(8,128)}, f32[512,768]{1,0:T(8,128)}) custom-call(s32[4]{0:T(128)} %pad_add_fusion.js_ref, bf16[768,512]{1,0:T(8,128)(2,1)} %collective-permute-done.6.refs_0_, bf16[768,512]{1,0:T(8,128)(2,1)} %copy-done.2, bf16[256,512]{1,0:T(8,128)(2,1)} %copy-done.8, bf16[256,512]{1,0:T(8,128)(2,1)} %copy-done.9, ...), custom_call_target="tpu_custom_call" | custom-call | tf_op jit(solution)/shard_map/matmul4/pallas_call | solution.py:410
  133.7 3.2 %collective-permute-done.16.rx_hbm = f32[512,768]{1,0:T(8,128)S(1)} collective-permute-done((f32[512,768]{1,0:T(8,128)}, f32[512,768]{1,0:T(8,128)S(1)}, u32[]{:S(2)}, u32[]{:S(2)}) %collective-permute-start.16) | collective-permute-done | bytes 1572896 | tf_op jit(solution)/shard_map/ppermute | solution.py:754
  138.1 21.6 %attend.1 = (bf16[128,4,512]{2,1,0:T(4,128)(2,1)}, bf16[1024,16,128]{2,1,0:T(8,128)(2,1)}) custom-call(s32[1]{0:T(128)} %bitcast.core_ref.par_ref, s32[32,128]{1,0:T(8,128)} %get-tuple-element.24.meta_ref.meta_hbm, s32[24,128]{1,0:T(8,128)} %get-tuple-element.27.lens_ref, f32[512,512]{1,0:T(8,128)} %get-tuple-element.41.own_hbm, ...), custom_call_target="tpu_custom_call" | custom-call | tf_op jit(solution)/shard_map/attend/pallas_call | solution.py:716
  (51 shorter events, 9.2 us)
Async XLA Ops:
  0.6 57.6 %collective-permute-start.4 = (bf16[8192,512]{1,0:T(8,128)(2,1)}, bf16[8192,512]{1,0:T(8,128)(2,1)}, u32[]{:S(2)}, u32[]{:S(2)}) collective-permute-start(bf16[8192,512]{1,0:T(8,128)(2,1)} %refs_4_.3), channel_id=1, source_target_pairs={{0,1},{1,0},{2,3},{3,2},{4,5},{5,4},{6,7},{7,6},{8,9},{9,8},{10,11... | collective-permute-start | bytes 25165832 | tf_op jit(solution)/shard_map/ppermute | solution.py:754
  2.1 29.4 %collective-permute-start = (bf16[1024,16,128]{2,1,0:T(8,128)(2,1)}, bf16[1024,16,128]{2,1,0:T(8,128)(2,1)}, u32[]{:S(2)}, u32[]{:S(2)}) collective-permute-start(bf16[1024,16,128]{2,1,0:T(8,128)(2,1)} %pool_hbm.3), channel_id=1, source_target_pairs={{0,1},{1,0},{2,3},{3,2},{4,5},{5,4},{6,7},{7,6},{8,9},{9,8},{10,11... | collective-permute-start | bytes 12582920 | tf_op jit(solution)/shard_map/ppermute | solution.py:754
  2.2 36.7 %collective-permute-start.5 = (bf16[8192,128]{1,0:T(8,128)(2,1)}, bf16[8192,128]{1,0:T(8,128)(2,1)S(1)}, u32[]{:S(2)}, u32[]{:S(2)}) collective-permute-start(bf16[8192,128]{1,0:T(8,128)(2,1)} %refs_5_.3), channel_id=1, source_target_pairs={{0,1},{1,0},{2,3},{3,2},{4,5},{5,4},{6,7},{7,6},{8,9},{9,8},{10,11... | collective-permute-start | bytes 6291464 | tf_op jit(solution)/shard_map/ppermute | solution.py:754
  8.1 13.8 %all-to-all-start = ((bf16[8,32,640]{2,1,0:T(8,128)(2,1)}), bf16[8,32,640]{2,1,0:T(8,128)(2,1)S(1)}, u32[]{:S(2)}, u32[]{:S(2)}) async-start(bf16[8,32,640]{2,1,0:T(8,128)(2,1)} %bitcast.19), calls=%async_computation | async-start | bytes 655360 | tf_op jit(solution)/shard_map/all_to_all | solution.py:763
  21.9 9.6 %copy-start.7 = (bf16[8,32,640]{2,1,0:T(8,128)(2,1)}, bf16[8,32,640]{2,1,0:T(8,128)(2,1)S(1)}, u32[]{:S(2)}) copy-start(bf16[8,32,640]{2,1,0:T(8,128)(2,1)S(1)} %all-to-all-done) | copy-start | bytes 983044
  21.9 39.9 %all-to-all-start.1 = ((bf16[8,832,128]{2,1,0:T(8,128)(2,1)}), bf16[8,832,128]{2,1,0:T(8,128)(2,1)}, u32[]{:S(2)}, u32[]{:S(2)}) async-start(bf16[8,832,128]{2,1,0:T(8,128)(2,1)} %pack_adapters.1.after_ref), calls=%async_computation.1 | async-start | bytes 3407872 | tf_op jit(solution)/shard_map/all_to_all | solution.py:763
  33.7 13.1 %collective-permute-start.3 = (bf16[512,512]{1,0:T(8,128)(2,1)}, bf16[512,512]{1,0:T(8,128)(2,1)S(1)}, u32[]{:S(2)}, u32[]{:S(2)}) collective-permute-start(bf16[512,512]{1,0:T(8,128)(2,1)} %get-tuple-element.28.refs_0_.x_hbm), channel_id=1, source_target_pairs={{0,12},{1,13},{2,14},{3,15},{4,0},{5,1},{6,2},{7,3},{8,4},{9,5},{1... | collective-permute-start | bytes 1572872 | tf_op jit(solution)/shard_map/ppermute | solution.py:760
  36.5 13.5 %collective-permute-start.2 = (bf16[512,512]{1,0:T(8,128)(2,1)}, bf16[512,512]{1,0:T(8,128)(2,1)S(1)}, u32[]{:S(2)}, u32[]{:S(2)}) collective-permute-start(bf16[512,512]{1,0:T(8,128)(2,1)} %get-tuple-element.28.refs_0_.x_hbm), channel_id=1, source_target_pairs={{0,4},{1,5},{2,6},{3,7},{4,8},{5,9},{6,10},{7,11},{8,12},{9,13},{1... | collective-permute-start | bytes 1572872 | tf_op jit(solution)/shard_map/ppermute | solution.py:760
  36.5 21.8 %collective-permute-start.1 = (bf16[512,512]{1,0:T(8,128)(2,1)}, bf16[512,512]{1,0:T(8,128)(2,1)S(1)}, u32[]{:S(2)}, u32[]{:S(2)}) collective-permute-start(bf16[512,512]{1,0:T(8,128)(2,1)} %get-tuple-element.28.refs_0_.x_hbm), channel_id=1, source_target_pairs={{0,2},{1,3},{2,0},{3,1},{4,6},{5,7},{6,4},{7,5},{8,10},{9,11},{10,... | collective-permute-start | bytes 1572872 | tf_op jit(solution)/shard_map/ppermute | solution.py:757
  38.9 19.3 %copy-start = (bf16[8192,128]{1,0:T(8,128)(2,1)}, bf16[8192,128]{1,0:T(8,128)(2,1)S(1)}, u32[]{:S(2)}) copy-start(bf16[8192,128]{1,0:T(8,128)(2,1)S(1)} %collective-permute-done.5.refs_4_.refs_7_) | copy-start | bytes 6291460
  46.8 11.5 %copy-start.3 = (bf16[512,512]{1,0:T(8,128)(2,1)}, bf16[512,512]{1,0:T(8,128)(2,1)S(1)}, u32[]{:S(2)}) copy-start(bf16[512,512]{1,0:T(8,128)(2,1)S(1)} %collective-permute-done.3.refs_2_.refs_3_) | copy-start | bytes 1572868
  49.9 8.3 %copy-start.4 = (bf16[512,512]{1,0:T(8,128)(2,1)}, bf16[512,512]{1,0:T(8,128)(2,1)S(1)}, u32[]{:S(2)}) copy-start(bf16[512,512]{1,0:T(8,128)(2,1)S(1)} %collective-permute-done.2.refs_1_.refs_2_) | copy-start | bytes 1572868
  58.2 0.9 copy-start.5
  61.8 28.9 %all-to-all-start.2 = ((bf16[512,16,128]{2,1,0:T(8,128)(2,1)}), bf16[512,16,128]{2,1,0:T(8,128)(2,1)S(1)}, u32[]{:S(2)}, u32[]{:S(2)}) async-start(bf16[512,16,128]{2,1,0:T(8,128)(2,1)} %pack_cache.1.after2_ref), calls=%async_computation.2 | async-start | bytes 4194304 | tf_op jit(solution)/shard_map/all_to_all | solution.py:763
  66.3 32.1 %collective-permute-start.7 = (bf16[768,512]{1,0:T(8,128)(2,1)}, bf16[768,512]{1,0:T(8,128)(2,1)S(1)}, u32[]{:S(2)}, u32[]{:S(2)}) collective-permute-start(bf16[768,512]{1,0:T(8,128)(2,1)} %get-tuple-element.30), channel_id=1, source_target_pairs={{0,12},{1,13},{2,14},{3,15},{4,0},{5,1},{6,2},{7,3},{8,4},{9,5},{1... | collective-permute-start | bytes 2359304 | tf_op jit(solution)/shard_map/ppermute | solution.py:760
  69.1 40.9 %collective-permute-start.6 = (bf16[768,512]{1,0:T(8,128)(2,1)}, bf16[768,512]{1,0:T(8,128)(2,1)}, u32[]{:S(2)}, u32[]{:S(2)}) collective-permute-start(bf16[768,512]{1,0:T(8,128)(2,1)} %get-tuple-element.29), channel_id=1, source_target_pairs={{0,4},{1,5},{2,6},{3,7},{4,8},{5,9},{6,10},{7,11},{8,12},{9,13},{1... | collective-permute-start | bytes 2359304 | tf_op jit(solution)/shard_map/ppermute | solution.py:760
  72.6 4.0 %collective-permute-start.10 = (f32[256,128]{1,0:T(8,128)}, f32[256,128]{1,0:T(8,128)S(1)}, u32[]{:S(2)}, u32[]{:S(2)}) collective-permute-start(f32[256,128]{1,0:T(8,128)} %get-tuple-element.38), channel_id=1, source_target_pairs={{0,1},{1,0},{2,3},{3,2},{4,5},{5,4},{6,7},{7,6},{8,9},{9,8},{10,11... | collective-permute-start | bytes 393224 | tf_op jit(solution)/shard_map/ppermute | solution.py:754
  77.5 18.1 %collective-permute-start.11 = (f32[256,128]{1,0:T(8,128)S(1)}, f32[256,128]{1,0:T(8,128)S(1)}, u32[]{:S(2)}, u32[]{:S(2)}) collective-permute-start(f32[256,128]{1,0:T(8,128)S(1)} %add.125), channel_id=1, source_target_pairs={{0,2},{1,3},{2,0},{3,1},{4,6},{5,7},{6,4},{7,5},{8,10},{9,11},{10,... | collective-permute-start | bytes 393224 | tf_op jit(solution)/shard_map/ppermute | solution.py:757
  90.6 19.3 %copy-start.1 = (bf16[512,16,128]{2,1,0:T(8,128)(2,1)}, bf16[512,16,128]{2,1,0:T(8,128)(2,1)S(1)}, u32[]{:S(2)}) copy-start(bf16[512,16,128]{2,1,0:T(8,128)(2,1)S(1)} %all-to-all-done.2.got_hbm) | copy-start | bytes 6291460
  90.6 46.3 %collective-permute-start.17 = (bf16[512,16,128]{2,1,0:T(8,128)(2,1)S(1)}, bf16[512,16,128]{2,1,0:T(8,128)(2,1)}, u32[]{:S(2)}, u32[]{:S(2)}) collective-permute-start(bf16[512,16,128]{2,1,0:T(8,128)(2,1)S(1)} %all-to-all-done.2.got_hbm), channel_id=1, source_target_pairs={{0,1},{1,0},{2,3},{3,2},{4,5},{5,4},{6,7},{7,6},{8,9},{9,8},{10,11... | collective-permute-start | bytes 6291464 | tf_op jit(solution)/shard_map/ppermute | solution.py:754
  95.7 17.8 %collective-permute-start.14 = (f32[256,128]{1,0:T(8,128)S(1)}, f32[256,128]{1,0:T(8,128)S(1)}, u32[]{:S(2)}, u32[]{:S(2)}) collective-permute-start(f32[256,128]{1,0:T(8,128)S(1)} %add.126), channel_id=1, source_target_pairs={{0,12},{1,13},{2,14},{3,15},{4,0},{5,1},{6,2},{7,3},{8,4},{9,5},{1... | collective-permute-start | bytes 393224 | tf_op jit(solution)/shard_map/ppermute | solution.py:760
  98.4 16.1 %collective-permute-start.13 = (f32[256,128]{1,0:T(8,128)S(1)}, f32[256,128]{1,0:T(8,128)S(1)}, u32[]{:S(2)}, u32[]{:S(2)}) collective-permute-start(f32[256,128]{1,0:T(8,128)S(1)} %add.126), channel_id=1, source_target_pairs={{0,4},{1,5},{2,6},{3,7},{4,8},{5,9},{6,10},{7,11},{8,12},{9,13},{1... | collective-permute-start | bytes 393224 | tf_op jit(solution)/shard_map/ppermute | solution.py:760
  98.5 11.5 %copy-start.2 = (bf16[768,512]{1,0:T(8,128)(2,1)}, bf16[768,512]{1,0:T(8,128)(2,1)S(1)}, u32[]{:S(2)}) copy-start(bf16[768,512]{1,0:T(8,128)(2,1)S(1)} %collective-permute-done.7.refs_1_) | copy-start | bytes 2359300
  98.5 16.1 %collective-permute-start.12 = (f32[256,128]{1,0:T(8,128)S(1)}, f32[256,128]{1,0:T(8,128)S(1)}, u32[]{:S(2)}, u32[]{:S(2)}) collective-permute-start(f32[256,128]{1,0:T(8,128)S(1)} %add.126), channel_id=1, source_target_pairs={{0,8},{1,9},{2,10},{3,11},{4,12},{5,13},{6,14},{7,15},{8,0},{9,1},... | collective-permute-start | bytes 393224 | tf_op jit(solution)/shard_map/ppermute | solution.py:760
  111.8 10.0 %collective-permute-start.8 = (bf16[256,512]{1,0:T(8,128)(2,1)}, bf16[256,512]{1,0:T(8,128)(2,1)S(1)}, u32[]{:S(2)}, u32[]{:S(2)}) collective-permute-start(bf16[256,512]{1,0:T(8,128)(2,1)} %get-tuple-element.35), channel_id=1, source_target_pairs={{0,4},{1,5},{2,6},{3,7},{4,8},{5,9},{6,10},{7,11},{8,12},{9,13},{1... | collective-permute-start | bytes 786440 | tf_op jit(solution)/shard_map/ppermute | solution.py:760
  113.5 8.4 %collective-permute-start.9 = (bf16[256,512]{1,0:T(8,128)(2,1)}, bf16[256,512]{1,0:T(8,128)(2,1)S(1)}, u32[]{:S(2)}, u32[]{:S(2)}) collective-permute-start(bf16[256,512]{1,0:T(8,128)(2,1)} %get-tuple-element.36), channel_id=1, source_target_pairs={{0,12},{1,13},{2,14},{3,15},{4,0},{5,1},{6,2},{7,3},{8,4},{9,5},{1... | collective-permute-start | bytes 786440 | tf_op jit(solution)/shard_map/ppermute | solution.py:760
  114.6 2.6 %copy-start.10 = (bf16[256,128]{1,0:T(8,128)(2,1)}, bf16[256,128]{1,0:T(8,128)(2,1)S(1)}, u32[]{:S(2)}) copy-start(bf16[256,128]{1,0:T(8,128)(2,1)S(1)} %add_convert_fusion.mine_hbm) | copy-start | bytes 196612
  114.6 2.6 %collective-permute-start.15 = (bf16[256,128]{1,0:T(8,128)(2,1)S(1)}, bf16[256,128]{1,0:T(8,128)(2,1)S(1)}, u32[]{:S(2)}, u32[]{:S(2)}) collective-permute-start(bf16[256,128]{1,0:T(8,128)(2,1)S(1)} %add_convert_fusion.mine_hbm), channel_id=1, source_target_pairs={{0,1},{1,0},{2,3},{3,2},{4,5},{5,4},{6,7},{7,6},{8,9},{9,8},{10,11... | collective-permute-start | bytes 196616 | tf_op jit(solution)/shard_map/ppermute | solution.py:754
  121.8 0.7 copy-start.8
  121.9 0.8 copy-start.9
  133.1 3.8 %collective-permute-start.16 = (f32[512,768]{1,0:T(8,128)}, f32[512,768]{1,0:T(8,128)S(1)}, u32[]{:S(2)}, u32[]{:S(2)}) collective-permute-start(f32[512,768]{1,0:T(8,128)} %get-tuple-element.42.far_hbm), channel_id=1, source_target_pairs={{0,1},{1,0},{2,3},{3,2},{4,5},{5,4},{6,7},{7,6},{8,9},{9,8},{10,11... | collective-permute-start | bytes 4718600 | tf_op jit(solution)/shard_map/ppermute | solution.py:754
  136.9 1.2 copy-start.6
  (1 other events, 0.6 us)

commit v3 on v2

--- a/solution.py
+++ b/solution.py
@@ -208,71 +208,49 @@
     )(me, *ins)
 
 
-def pack_adapters_kernel(meta_ref, down_hbm, q_hbm, k_hbm, out_hbm, q_ref, out_ref, sem):
-    pairs = []
+def pack_kernel(
+    meta_ref, down_hbm, q_hbm, k_hbm, pool_hbm, down_out, rest_out,
+    down_ref, q_ref, k_ref, pool_ref, rest_ref, sem, pool_sem,
+):
+    pairs = [(down_hbm.at[meta_ref[PICK, d]], down_ref.at[d]) for d in range(8)]
+    loads = fetch(pairs, sem)
+    later = fetch(((pool_hbm, pool_ref), (q_hbm, q_ref), (k_hbm, k_ref)), pool_sem)
+    settle(loads)
+    stores = fetch(((down_ref, down_out),), sem)
+    settle(later)
     for d in range(8):
         i = meta_ref[PICK, d]
-        pairs.append((q_hbm.at[i], q_ref.at[d]))
-        pairs.append((k_hbm.at[i], out_ref.at[d, 768:]))
-        pairs.append((down_hbm.at[i], out_ref.at[d, :512]))
-    loads = fetch(pairs, sem)
-    for d in range(8):
-        loads[3 * d].wait()
-        q = q_ref[d]
+        q = q_ref[i]
         for h in range(4):
-            out_ref[d, 512 + 64 * h : 576 + 64 * h] = q[:, h * HEAD : (h + 1) * HEAD]
-        loads[3 * d + 1].wait()
-        loads[3 * d + 2].wait()
-    settle(fetch(((out_ref, out_hbm),), sem))
-
-
-def pack_adapters(meta, down, up_q, up_kv):
-    return pl.pallas_call(
-        pack_adapters_kernel,
-        out_shape=sds((8, 832, HEAD), BF16),
-        in_specs=[sspec()] + [hspec()] * 3,
-        out_specs=hspec(),
-        scratch_shapes=[
-            pltpu.VMEM(up_q.shape, BF16),
-            pltpu.VMEM((8, 832, HEAD), BF16),
-            pltpu.SemaphoreType.DMA((24,)),
-        ],
-        compiler_params=params(),
-        name="pack_adapters",
-    )(meta, down, up_q, up_kv)
-
-
-def pack_cache_kernel(meta_ref, pool_hbm, cache_hbm, pool_ref, cache_ref, sem):
-    settle(fetch(((pool_hbm, pool_ref),), sem))
+            rest_ref[d, 64 + 4 * h : 68 + 4 * h] = q[:, h * HEAD : (h + 1) * HEAD].reshape(4, 16, HEAD)
+        rest_ref[d, 80:84] = k_ref[i].reshape(4, 16, HEAD)
 
     def some(g, _):
         pages = [pool_ref[meta_ref[LEAVE + b, 4 * g + e]] for e in range(4) for b in range(8)]
         for n, page in enumerate(pages):
-            cache_ref[g * 32 + n] = page
+            rest_ref[g // 2, (g % 2) * 32 + n] = page
         return 0
 
     lax.fori_loop(0, 16, some, 0)
-    settle(fetch(((cache_ref, cache_hbm),), sem))
-
-
-def pack_cache(meta, pool):
+    settle(stores + fetch(((rest_ref, rest_out),), pool_sem))
+
+
+def pack(meta, down, up_q, up_kv, pool):
+    rest = sds((8, 84, 16, HEAD), BF16)
     return pl.pallas_call(
-        pack_cache_kernel,
-        out_shape=sds((512, 16, HEAD), BF16),
-        in_specs=[sspec(), hspec()],
-        out_specs=hspec(),
-        scratch_shapes=[
-            pltpu.VMEM(pool.shape, BF16),
-            pltpu.VMEM((512, 16, HEAD), BF16),
-            pltpu.SemaphoreType.DMA((1,)),
-        ],
+        pack_kernel,
+        out_shape=(sds(down.shape, BF16), rest),
+        in_specs=[sspec()] + [hspec()] * 4,
+        out_specs=(hspec(), hspec()),
+        scratch_shapes=[pltpu.VMEM(a.shape, BF16) for a in (down, up_q, up_kv, pool, rest)]
+        + [pltpu.SemaphoreType.DMA((8,)), pltpu.SemaphoreType.DMA((3,))],
         compiler_params=params(),
-        name="pack_cache",
-    )(meta, pool)
+        name="pack",
+    )(meta, down, up_q, up_kv, pool)
 
 
 def join_kernel(
-    own_hbm, got_hbm, meta_hbm, after_ref, after2_ref, after3_ref, x_hbm, len_hbm, lens_hbm,
+    own_hbm, got_hbm, meta_hbm, after_ref, after2_ref, x_hbm, len_hbm, lens_hbm,
     own_ref, got_ref, meta_ref, x_ref, len_ref, lens_ref, sem,
 ):
     settle(fetch(((own_hbm, own_ref), (got_hbm, got_ref), (meta_hbm, meta_ref)), sem))
@@ -301,7 +279,7 @@
     return pl.pallas_call(
         join_kernel,
         out_shape=(sds((rows, 512), BF16), sds((rows, HEAD), F32), sds((24, HEAD), I32)),
-        in_specs=[hspec()] * 6,
+        in_specs=[hspec()] * 5,
         out_specs=(hspec(),) * 3,
         scratch_shapes=[
             pltpu.VMEM(own.shape, BF16),
@@ -342,86 +320,91 @@
     )(*arrays, *after)
 
 
-def matmul_kernel(blocks, n, extra, js_ref, *refs):
+COLUMNS = {"far": ((2, 512, 0), (1, HEAD, 512), (3, HEAD, 640)), "own": ((0, 512, 0),)}
+WIDTH = {"far": 768, "own": 512}
+
+
+def matmul_kernel(blocks, offsets, chunk, n, parts, extra, after, at_ref, *refs):
+    np_, nb = len(parts), len(blocks)
     xs, refs = refs[:n], refs[n:]
     weights, refs = refs[:4], refs[4:]
-    accs, refs = refs[:extra], refs[extra:]
-    own_hbm, far_hbm, refs = refs[0], refs[1], refs[2:]
-    bufs, refs = refs[:4], refs[4:]
-    held, refs = refs[:n], refs[n:]
-    acc, refs = refs[:extra], refs[extra:]
-    own_ref, far_ref, x_sem, sem, acc_sem = refs
+    adds, refs = refs[: extra * np_], refs[extra * np_ + after :]
+    outs, refs = refs[:np_], refs[np_:]
+    bufs, refs = refs[:np_], refs[np_:]
+    add, refs = refs[: extra * np_], refs[extra * np_ :]
+    res, refs = refs[:np_], refs[np_:]
+    x_ref, x_sem, sem, add_sem, out_sem = refs
+    y, hi, core = at_ref[0] // 4, (at_ref[0] // 2) % 2, at_ref[0] % 2
+    place = [(((y + dy) % 4) * 2 + (hi + dx) % 2) * 2 + core for dy, dx in offsets]
+    x_loads, w_loads = [], {}
+    for k, cut in enumerate(blocks):
+        row = 0
+        for j, (i, lo, hi) in enumerate(cut):
+            to = x_ref.at[row : row + hi - lo, k * 512 : (k + 1) * 512]
+            x_loads.append((k, pltpu.make_async_copy(xs[i].at[lo:hi], to, x_sem.at[k, j])))
+            row += hi - lo
+    for o, part in enumerate(parts):
+        for k in range(nb):
+            at = pl.ds(pl.multiple_of(place[k] * 512, 512), 512)
+            w_loads[o, k] = [
+                pltpu.make_async_copy(
+                    weights[w].at[at],
+                    bufs[o].at[k * 512 : (k + 1) * 512, lo : lo + width],
+                    sem.at[k, w],
+                )
+                for w, width, lo in COLUMNS[part]
+            ]
+    for k in range(nb):
+        for c in [c for at, c in x_loads if at == k] + w_loads[0, k]:
+            c.start()
+    add_loads = fetch(list(zip(adds, add)), add_sem)
+    for o in range(1, np_):
+        for k in range(nb):
+            for c in w_loads[o, k]:
+                c.start()
+    stores = []
+    for o in range(np_):
+        for c in range(0, nb, chunk):
+            for k in range(c, c + chunk):
+                if o == 0:
+                    settle([copy for at, copy in x_loads if at == k])
+                settle(w_loads[o, k])
+            at = slice(c * 512, (c + chunk) * 512)
+            y = jnp.dot(x_ref[:, at], bufs[o][at], preferred_element_type=F32)
+            if c == 0:
+                settle(add_loads[o * extra : (o + 1) * extra])
+                for a in add[o * extra : (o + 1) * extra]:
+                    y = y + a[...]
+                res[o][...] = y
+            else:
+                res[o][...] += y
+        stores += fetch(((res[o], outs[o]),), out_sem, o)
+    settle(stores)
+
+
+def matmul(parts, at, offsets, blocks, xs, weights, adds=(), after=(), chunk=4):
     nb = len(blocks)
-    loads = fetch(list(zip(xs, held)), x_sem)
-    copies = []
-    for k in range(nb):
-        at = pl.ds(pl.multiple_of(js_ref[k] * 512, 512), 512)
-        copies.append(
-            [
-                pltpu.make_async_copy(
-                    weights[w].at[at], bufs[w].at[k * 512 : (k + 1) * 512], sem.at[k, w]
-                )
-                for w in range(4)
-            ]
-        )
-    for w in (2, 1, 3, 0):
-        for k in range(nb):
-            copies[k][w].start()
-    acc_loads = fetch(list(zip(accs, acc)), acc_sem)
-    settle(loads)
-    x = []
-    for parts in blocks:
-        pieces = [held[i][lo:hi] for i, lo, hi in parts]
-        x.append(pieces[0] if len(pieces) == 1 else jnp.concatenate(pieces, axis=0))
-    x = jnp.concatenate(x, axis=1) if nb > 1 else x[0]
-
-    def product(*which):
-        for k in range(nb):
-            for w in which:
-                copies[k][w].wait()
-        w = [bufs[w][...] for w in which]
-        w = w[0] if len(w) == 1 else jnp.concatenate(w, axis=1)
-        return jnp.dot(x, w, preferred_element_type=F32)
-
-    far_q = product(2)
-    settle(acc_loads)
-    if extra:
-        far_q = far_q + acc[1][:, :512]
-    far_ref[:, :512] = far_q
-    far_k = product(1, 3)
-    if extra:
-        far_k = far_k + acc[1][:, 512:]
-    if extra == 3:
-        far_k = far_k + jnp.concatenate([acc[2][:, 512:], jnp.zeros((512, HEAD), F32)], axis=1)
-    far_ref[:, 512:] = far_k
-    stores = fetch(((far_ref, far_hbm),), acc_sem, extra)
-    own = product(0)
-    if extra:
-        own = own + acc[0][...]
-    if extra == 3:
-        own = own + acc[2][:, :512]
-    own_ref[...] = own
-    settle(stores + fetch(((own_ref, own_hbm),), acc_sem, extra + 1))
-
-
-def matmul(js, blocks, xs, weights, accs=()):
-    nb = len(blocks)
-    outs = (sds((512, 512), F32), sds((512, 768), F32))
+    outs = tuple(sds((512, WIDTH[p]), F32) for p in parts)
+    flat = tuple(a[o] for o in range(len(parts)) for a in adds)
     return pl.pallas_call(
-        functools.partial(matmul_kernel, blocks, len(xs), len(accs)),
+        functools.partial(
+            matmul_kernel, blocks, offsets, min(chunk, nb), len(xs), parts, len(adds), len(after)
+        ),
         out_shape=outs,
-        in_specs=[sspec()] + [hspec()] * (len(xs) + 4 + len(accs)),
-        out_specs=(hspec(), hspec()),
-        scratch_shapes=[pltpu.VMEM((nb * 512, w.shape[1]), BF16) for w in weights]
-        + [pltpu.VMEM(a.shape, a.dtype) for a in (*xs, *accs, *outs)]
+        in_specs=[sspec()] + [hspec()] * (len(xs) + 4 + len(flat) + len(after)),
+        out_specs=(hspec(),) * len(parts),
+        scratch_shapes=[pltpu.VMEM((nb * 512, WIDTH[p]), BF16) for p in parts]
+        + [pltpu.VMEM(a.shape, a.dtype) for a in (*flat, *outs)]
         + [
-            pltpu.SemaphoreType.DMA((len(xs),)),
+            pltpu.VMEM((512, nb * 512), BF16),
+            pltpu.SemaphoreType.DMA((nb, 2)),
             pltpu.SemaphoreType.DMA((nb, 4)),
-            pltpu.SemaphoreType.DMA((len(accs) + 2,)),
+            pltpu.SemaphoreType.DMA((max(1, len(flat)),)),
+            pltpu.SemaphoreType.DMA((len(parts),)),
         ],
         compiler_params=params(),
-        name="matmul%d" % nb,
-    )(js, *xs, *weights, *accs)
+        name="matmul_" + "_".join(parts),
+    )(at, *xs, *weights, *flat, *after)
 
 
 def down_kernel(
@@ -429,7 +412,7 @@
     x_ref, here_ref, far_ref, cand_ref, out_ref, sem,
 ):
     loads = fetch(
-        ((x_hbm, x_ref), (here_hbm, here_ref), (cand_hbm, cand_ref), (far_hbm.at[:, :512], far_ref)),
+        ((x_hbm, x_ref), (here_hbm, here_ref), (cand_hbm, cand_ref), (far_hbm, far_ref)),
         sem,
     )
     settle(loads[:3])
@@ -485,9 +468,10 @@
 
 
 def up_kernel(
-    core_ref, mine_hbm, other_hbm, far_hbm, cand_hbm, q_hbm, k_hbm, len_hbm, table_hbm, after_ref,
-    out_hbm, cos_hbm, sin_hbm,
-    down_ref, far, cand_ref, q_here, k_here, len_ref, table_ref, out_ref, cos_ref, sin_ref, sem,
+    core_ref, mine_hbm, other_hbm, far_hbm, cand_hbm, q_hbm, k_hbm, len_hbm, table_hbm, acc_hbm,
+    out_hbm, kv_hbm, cos_hbm, sin_hbm,
+    down_ref, far, cand_ref, q_here, k_here, len_ref, table_ref, acc_ref,
+    out_ref, kv_ref, cos_ref, sin_ref, sem,
 ):
     half = mine_hbm.shape[0]
     mine = pl.ds(pl.multiple_of(core_ref[0] * half, half), half)
@@ -496,8 +480,8 @@
         fetch(
             (
                 (mine_hbm, down_ref.at[mine]), (other_hbm, down_ref.at[other]),
-                (far_hbm.at[:, 512:], far), (cand_hbm, cand_ref), (q_hbm, q_here),
-                (k_hbm, k_here), (len_hbm, len_ref), (table_hbm, table_ref),
+                (far_hbm.at[:, 64:], far), (cand_hbm, cand_ref), (q_hbm, q_here),
+                (k_hbm, k_here), (len_hbm, len_ref), (table_hbm, table_ref), (acc_hbm, acc_ref),
             ),
             sem,
         )
@@ -521,17 +505,20 @@
     q_all, k_all = q_here[...].reshape(512, 512), k_here[...].reshape(512, HEAD)
 
     def far_part(lo):
-        return jnp.concatenate([far[a, lo : lo + 64] for a in range(8)], axis=0)
+        return jnp.concatenate(
+            [far[a, lo // 16 : lo // 16 + 4].reshape(64, HEAD) for a in range(8)], axis=0
+        )
 
     w = [
         jnp.concatenate([q_all[:, h * HEAD : (h + 1) * HEAD], far_part(64 * h)], axis=0)
         for h in range(4)
     ]
     for h in (0, 2):
-        out_ref[:, h * HEAD : (h + 2) * HEAD] = jnp.dot(
+        at = slice(h * HEAD, (h + 2) * HEAD)
+        out_ref[:, at] = acc_ref[:, at] + jnp.dot(
             sq, jnp.concatenate([w[h], w[h + 1]], axis=1), preferred_element_type=F32
         )
-    out_ref[:, 512:] = jnp.dot(
+    kv_ref[...] = jnp.dot(
         sk, jnp.concatenate([k_all, far_part(256)], axis=0), preferred_element_type=F32
     )
     position = len_ref[...].astype(I32) + iota((rows, HEAD), 0) % 4
@@ -540,24 +527,28 @@
     turns = turns[:, :256] + turns[:, 256:512] + turns[:, 512:]
     cos_ref[...] = turns[:, :HEAD]
     sin_ref[...] = turns[:, HEAD:]
-    settle(fetch(((out_ref, out_hbm), (cos_ref, cos_hbm), (sin_ref, sin_hbm)), sem))
-
-
-def up_product(core, mine, other, far, cand, up_q, up_kv, length, after):
+    settle(
+        fetch(
+            ((out_ref, out_hbm), (kv_ref, kv_hbm), (cos_ref, cos_hbm), (sin_ref, sin_hbm)), sem
+        )
+    )
+
+
+def up_product(core, mine, other, far, cand, up_q, up_kv, length, acc):
     rows = cand.shape[0]
-    ins = (cand, up_q, up_kv, length, jnp.asarray(turn_table()))
-    outs = (sds((rows, 640), F32), sds((rows, HEAD), F32), sds((rows, HEAD), F32))
+    ins = (cand, up_q, up_kv, length, jnp.asarray(turn_table()), acc)
+    outs = (sds((rows, 512), F32),) + (sds((rows, HEAD), F32),) * 3
     return pl.pallas_call(
         up_kernel,
         out_shape=outs,
         in_specs=[sspec()] + [hspec()] * 9,
-        out_specs=(hspec(),) * 3,
-        scratch_shapes=[pltpu.VMEM((rows, HEAD), BF16), pltpu.VMEM((8, 320, HEAD), BF16)]
+        out_specs=(hspec(),) * 4,
+        scratch_shapes=[pltpu.VMEM((rows, HEAD), BF16), pltpu.VMEM((8, 20, 16, HEAD), BF16)]
         + [pltpu.VMEM(a.shape, a.dtype) for a in ins + outs]
-        + [pltpu.SemaphoreType.DMA((8,))],
+        + [pltpu.SemaphoreType.DMA((9,))],
         compiler_params=params(),
         name="up_product",
-    )(core, mine, other, far, *ins, after)
+    )(core, mine, other, far, *ins)
 
 
 GROUP = 4
@@ -570,25 +561,30 @@
 
 def attend_kernel(
     par_ref, meta_ref, lens_ref,
-    own_hbm, far_hbm, rx_hbm, cos_hbm, sin_hbm,
+    own_hbm, far_hbm, rx_hbm, kv_hbm, kv2_hbm, cos_hbm, sin_hbm,
     pool_hbm, pool2_hbm, got_hbm, got2_hbm,
     out_hbm, new_hbm,
-    own_ref, far_ref, rx_ref, cos_ref, sin_ref, out_ref, new_ref,
+    own_ref, far_ref, rx_ref, kv_ref, kv2_ref, cos_ref, sin_ref, out_ref, new_ref,
     q_scr, f_scr, page_scr, mask_scr, sem,
 ):
     odd = par_ref[0]
+    def pages_from(i, pool, got):
+        return [(pool, page_scr.at[i, :POOL])] + [
+            (got.at[g, :64], page_scr.at[i, POOL + 64 * g : POOL + 64 * g + 64]) for g in range(8)
+        ]
+
     copies = fetch(
         (
-            (pool_hbm, page_scr.at[0, :POOL]), (got_hbm, page_scr.at[0, POOL:ZERO_PAGE]),
-            (own_hbm, own_ref), (far_hbm, far_ref), (rx_hbm, rx_ref),
-            (cos_hbm, cos_ref), (sin_hbm, sin_ref),
-            (pool2_hbm, page_scr.at[1, :POOL]), (got2_hbm, page_scr.at[1, POOL:ZERO_PAGE]),
+            *pages_from(0, pool_hbm, got_hbm),
+            (far_hbm, far_ref), (rx_hbm, rx_ref), (kv_hbm, kv_ref), (kv2_hbm, kv2_ref),
+            (cos_hbm, cos_ref), (sin_hbm, sin_ref), (own_hbm, own_ref),
+            *pages_from(1, pool2_hbm, got2_hbm),
         ),
         sem,
     )
     page_masks(mask_scr)
     page_scr[0, ZERO_PAGE] = jnp.zeros((16, HEAD), BF16)
-    settle(copies[:2])
+    settle(copies[:9])
 
     def keep(g, _):
         kept = []
@@ -601,7 +597,7 @@
         return 0
 
     lax.fori_loop(0, 32, keep, 0)
-    settle(copies[2:7])
+    settle(copies[9:16])
     cos, sin = cos_ref[...], sin_ref[...]
 
     def turn(v):
@@ -610,8 +606,8 @@
     for h in range(4):
         at = slice(h * HEAD, (h + 1) * HEAD)
         q_scr[:, at] = turn(own_ref[:, at] + rx_ref[:, at])
-    kv_own = far_ref[:, 512:640] + rx_ref[:, 640:768]
-    kv_oth = far_ref[:, 640:768] + rx_ref[:, 512:640]
+    kv_own = far_ref[:, 512:640] + rx_ref[:, 640:768] + kv_ref[...]
+    kv_oth = far_ref[:, 640:768] + rx_ref[:, 512:640] + kv2_ref[...]
     key = turn(jnp.where(odd == 0, kv_own, kv_oth))
     value = jnp.where(odd == 0, kv_oth, kv_own)
     f_scr[:, :HEAD] = key
@@ -655,7 +651,7 @@
     col_new = iota((HEAD, HEAD), 1) - (row // 32) * 8 - (row % 8) // 4 * 4
     contract = (((1,), (1,)), ((), ()))
 
-    def mix(g, _):
+    def mixed_rows(g):
         q32 = q_scr[pl.ds(pl.multiple_of(32 * g, 32), 32), :]
         q = jnp.concatenate(
             [
@@ -696,39 +692,43 @@
                 jnp.dot(old[32 * k : 32 * k + 32], values, preferred_element_type=F32)
             )
         mixed = (mixed + jnp.concatenate(old_mixed, axis=0)).astype(BF16)
-        for k in range(GROUP):
-            for e in range(2):
-                slot = meta_ref[SLOT, 8 * g + 2 * k + e]
+        return mixed
+
+    def mix(i, _):
+        done = [mixed_rows(i * 4 + j) for j in range(4)]
+        for j, mixed in enumerate(done):
+            for n in range(2 * GROUP):
+                slot = meta_ref[SLOT, (i * 4 + j) * 2 * GROUP + n]
                 for h in range(4):
-                    lo = k * 32 + h * 8 + e * 4
+                    lo = n // 2 * 32 + h * 8 + n % 2 * 4
                     out_ref[slot, :, h * HEAD : (h + 1) * HEAD] = mixed[lo : lo + 4]
         return 0
 
     lax.fori_loop(0, 16, edge, 0)
     stores = fetch(((new_ref, new_hbm),), sem)
-    settle(copies[7:])
-    lax.fori_loop(0, 16, mix, 0)
+    settle(copies[16:])
+    lax.fori_loop(0, 4, mix, 0)
     settle(stores + fetch(((out_ref, out_hbm),), sem, 1))
 
 
-def attend(parity, meta, lens, own, far, rx, cos, sin, pool, pool2, got, got2):
+def attend(parity, meta, lens, own, far, rx, kv, kv2, cos, sin, pool, pool2, got, got2):
     outs = (sds((128, 4, 512), BF16), sds(pool.shape, BF16))
     return pl.pallas_call(
         attend_kernel,
         out_shape=outs,
-        in_specs=[sspec()] * 3 + [hspec()] * 9,
+        in_specs=[sspec()] * 3 + [hspec()] * 11,
         out_specs=(hspec(), hspec()),
-        scratch_shapes=[pltpu.VMEM(a.shape, a.dtype) for a in (own, far, rx, cos, sin, *outs)]
+        scratch_shapes=[pltpu.VMEM(a.shape, a.dtype) for a in (own, far, rx, kv, kv2, cos, sin, *outs)]
         + [
             pltpu.VMEM((512, 512), F32),
             pltpu.VMEM((512, 3 * HEAD), F32),
             pltpu.VMEM((2, ZERO_PAGE + 1, 16, HEAD), BF16),
             pltpu.VMEM((17, 16, HEAD), BF16),
-            pltpu.SemaphoreType.DMA((9,)),
+            pltpu.SemaphoreType.DMA((25,)),
         ],
         compiler_params=params(),
         name="attend",
-    )(parity, meta, lens, own, far, rx, cos, sin, pool, pool2, got, got2)
+    )(parity, meta, lens, own, far, rx, kv, kv2, cos, sin, pool, pool2, got, got2)
 
 
 def body(
@@ -767,19 +767,13 @@
         storage_slot_adapter.reshape(1, 64), lengths.reshape(1, 128),
         previous_block_table.T, moved_block_table.T, tokens.reshape(512, 512),
     )
-    packed = pack_adapters(meta, adapter_down_factors, adapter_up_query, adapter_up_key_value)
+    packed, leaving = pack(
+        meta, adapter_down_factors, adapter_up_query, adapter_up_key_value, paged_cache_pool
+    )
     pool2 = other_core(paged_cache_pool)
     vq, vk = other_core(query_weight_matrix), other_core(key_value_weight)
-    leaving = pack_cache(meta, paged_cache_pool)
-    x, length, lens = join(own, swap_rep(send), meta, packed, leaving, pool2)
-    far = swap_rep(packed)
-
-    hi = (t // 2) % 2
-    y = t // 4
-
-    def js(*blocks):
-        at = [(((y + dy) % 4) * 2 + (hi ^ dx)) * 2 + core for dy, dx in blocks]
-        return jnp.stack(at).astype(I32)
+    x, length, lens = join(own, swap_rep(send), meta, packed, pool2)
+    far_down = swap_rep(packed)
 
     weights = (query_weight_matrix, key_value_weight, vq, vk)
     one = core.reshape(1)
@@ -787,43 +781,42 @@
     yp = along_y(x, 1)
     ym = along_y(x, -1)
     full = (0, 512)
-    up, dn = slices(
-        ((0, (0, 512), 0, 0), (1, (0, 256), 0, 512), (0, (0, 512), 1, 0), (2, (256, 512), 1, 512)),
-        (768, 768), (xh, yp, ym), (vq, vk),
-    )
-    leaving, far, _ = lax.optimization_barrier((leaving, far, up))
-    got = swap_rep(leaving)
-    got2 = other_core(got)
-    up, dn = along_y(up, 1), along_y(dn, -1)
-    acc = matmul(
-        js((0, 0), (0, 1), (3, 0), (1, 0)),
-        tuple(((i, *full),) for i in range(4)),
-        (x, xh, yp, ym), weights,
-    )
-    keep, give = down_product(one, x, adapter_down_factors, far, cand)
-    up2, dn2 = slices(
-        ((0, (0, 256), 0, 0), (1, (256, 512), 1, 0)), (256, 256), (up, dn), (acc[0], keep)
-    )
-    last = (along_y(up2, 1), along_y(dn2, -1))
+    ends = ((0, (0, 256), 0, 0), (1, (256, 512), 1, 0))
+    yp2, ym2 = slices(ends, (256, 256), (yp, ym), (vq, vk))
+    y2 = (along_y(yp2, 1), along_y(ym2, -1))
+
+    keep, give = down_product(one, x, adapter_down_factors, far_down, cand)
     total = keep + other_core(give)
     total = total + other_x(total)
+    leaving, total, xh, y2 = lax.optimization_barrier((leaving, total, xh, y2))
+    got = swap_rep(leaving)
+
+    xyp, xym = along_y(xh, 1), along_y(xh, -1)
+    at = t.reshape(1)
+    acc = matmul(
+        ("far", "own"), at, ((0, 0), (3, 0), (1, 0), (2, 0)),
+        (((0, *full),), ((1, *full),), ((2, *full),), ((3, 0, 256), (4, 0, 256))),
+        (x, yp, ym, *y2), weights,
+    )
+    xyp2, xym2 = slices(ends, (256, 256), (xyp, xym), (acc[0],))
+    xy2 = (along_y(xyp2, 1), along_y(xym2, -1))
     total = (total + along_y(total, 2)) + (along_y(total, 1) + along_y(total, -1))
     total = total.astype(BF16)
-    delta, cos, sin = up_product(
-        one, total, other_core(total), far, cand, adapter_up_query, adapter_up_key_value, length,
-        acc[0],
-    )
-    acc_own, acc_far = matmul(
-        js((3, 1), (1, 1), (2, 0), (2, 1)),
-        (
-            ((0, *full),), ((1, *full),), ((0, 512, 768), (1, 512, 768)),
-            ((2, 0, 256), (3, 0, 256)),
-        ),
-        (up, dn, *last), weights, (*acc, delta),
+    other_total = other_core(total)
+    acc_far, acc_own = matmul(
+        ("far", "own"), at, ((0, 1), (3, 1), (1, 1), (2, 1)),
+        (((0, *full),), ((1, *full),), ((2, *full),), ((3, 0, 256), (4, 0, 256))),
+        (xh, xyp, xym, *xy2), weights, ((acc[0], acc[1]),), (other_total,),
     )
     rx = other_core(acc_far)
+    got, acc_own = lax.optimization_barrier((got, acc_own))
+    own, kv, cos, sin = up_product(
+        one, total, other_total, got, cand, adapter_up_query, adapter_up_key_value, length,
+        acc_own,
+    )
     return attend(
-        one, meta, lens, acc_own, acc_far, rx, cos, sin, paged_cache_pool, pool2, got, got2
+        one, meta, lens, own, acc_far, rx, kv, other_core(kv), cos, sin,
+        paged_cache_pool, pool2, got, other_core(got),
     )
 
 

time: 161 us -> 132 us (0.82)
  waiting for transfers between devices: 39.3 us -> 15.4 us
  Pallas kernels: 68.1 us -> 58.9 us
  starting transfers between devices: 43.9 us -> 50.1 us
    ppermute x9 -> x11, waiting for transfers between devices: 11 us -> 1.13 us  [along_y(): return lax.ppermute(a, 'tp', [(i, (i + 4 * d) % 16) for i in range(16)])]
    pallas_call x4 -> x3, Pallas kernels: 28.8 us -> 22.1 us  [the longest x2 15.8 us: matmul(): pl.pallas_call(functools.partial(matmul_kernel, blocks, offsets, min(chun...]
    all_to_all x3, waiting for transfers between devices: 15.2 us -> 8.51 us  [swap_rep(): return lax.all_to_all(a, 'rep', split_axis=0, concat_axis=0, tiled=True)]
    ppermute x2, waiting for transfers between devices: 8.31 us -> 2.88 us  [other_x(): return lax.ppermute(a, 'tp', [(i, i ^ 2) for i in range(16)])]
    ppermute x7 -> x8, starting transfers between devices: 12 us -> 16.8 us  [other_core(): return lax.ppermute(a, 'tp', [(i, i ^ 1) for i in range(16)])]
    ppermute x9 -> x11, starting transfers between devices: 12.7 us -> 14.9 us  [along_y(): return lax.ppermute(a, 'tp', [(i, (i + 4 * d) % 16) for i in range(16)])]
    ppermute x7 -> x8, waiting for transfers between devices: 4.77 us -> 2.86 us  [other_core(): return lax.ppermute(a, 'tp', [(i, i ^ 1) for i in range(16)])]
    pallas_call x1, Pallas kernels: 21.6 us -> 19.8 us  [attend(): pl.pallas_call(attend_kernel, out_shape=outs, in_specs=[sspec()] * 3 + [h...]
  transfers between devices with their start and end apart: 21 -> 24, of which waited for: 8 -> 7; matrix products, arithmetic and copies ran while one was open for 3% -> 2% of each run, Pallas kernels for 29% -> 30%
where the time goes in v3:
time: 132 us
  Pallas kernels  58.9 us (45%)
  starting transfers between devices  50.1 us (38%)
  waiting for transfers between devices  15.4 us (12%)
  local copies, waits for them, and re-layouts  5.27 us (4%)
    pallas_call x1, Pallas kernels, attend(): pl.pallas_call(attend_kernel, out_shape=outs, in_specs=[sspec()] * 3 + [h...  19.8 us
    ppermute x8, starting transfers between devices, other_core(): return lax.ppermute(a, 'tp', [(i, i ^ 1) for i in range(16)])  16.8 us
    pallas_call x2, Pallas kernels, matmul(): pl.pallas_call(functools.partial(matmul_kernel, blocks, offsets, min(chun...  15.8 us
    ppermute x11, starting transfers between devices, along_y(): return lax.ppermute(a, 'tp', [(i, (i + 4 * d) % 16) for i in range(16)])  14.9 us
    all_to_all x3, starting transfers between devices, swap_rep(): return lax.all_to_all(a, 'rep', split_axis=0, concat_axis=0, tiled=True)  13.4 us
    all_to_all x3, waiting for transfers between devices, swap_rep(): return lax.all_to_all(a, 'rep', split_axis=0, concat_axis=0, tiled=True)  8.51 us
    pallas_call x1, Pallas kernels, pack(): pl.pallas_call(pack_kernel, out_shape=(sds(down.shape, BF16), rest), in_s...  6.27 us
    ppermute x2, starting transfers between devices, other_x(): return lax.ppermute(a, 'tp', [(i, i ^ 2) for i in range(16)])  4.98 us
  transfers between devices with their start and end apart: 24, of which 7 were waited for; matrix products, arithmetic and copies ran while one was open for 2% of the time, Pallas kernels for 30%

profile of v3, /device:TPU:1, one launch (start us, length us, event | category | flops | bytes accessed | tf_op | source)
XLA Modules:
  0.0 131.7 jit_solution(17703906193695104773)
XLA Ops:
  0.6 1.5 %collective-permute-start.6 = (bf16[8192,512]{1,0:T(8,128)(2,1)}, bf16[8192,512]{1,0:T(8,128)(2,1)}, u32[]{:S(2)}, u32[]{:S(2)}) collective-permute-start(bf16[8192,512]{1,0:T(8,128)(2,1)} %refs_5_.3), channel_id=1, source_target_pairs={{0,1},{1,0},{2,3},{3,2},{4,5},{5,4},{6,7},{7,6},{8,9},{9,8},{10,11... | collective-permute-start | bytes 25165832 | tf_op jit(solution)/shard_map/ppermute | solution.py:754
  2.6 2.0 %reshape.36.tok_hbm = bf16[512,512]{1,0:T(8,128)(2,1)} reshape(bf16[128,4,512]{2,1,0:T(4,128)(2,1)} %param.14) | data formatting | bytes 1048576 | tf_op jit(solution)/shard_map/reshape | solution.py:768
  4.6 3.5 %plan.1 = (bf16[256,640]{1,0:T(8,128)(2,1)}, bf16[512,640]{1,0:T(8,128)(2,1)}, bf16[512,128]{1,0:T(8,128)(2,1)}, s32[32,128]{1,0:T(8,128)}) custom-call(s32[1]{0:T(128)} %bitcast.1.me_ref, s32[8,128]{1,0:T(8,128)} %bitcast.13, s32[8,128]{1,0:T(8,128)} %bitcast.14, s32[1,64]{1,0:T(1,128)} %bitcast.17, s32[1,128]{1,0:T(1,128)} %bitcast.18, s32[8,128]{1,0:T(8,128)} %bitcast.15, ...), custom_call_target="tpu_custom_call" | custom-call | tf_op jit(solution)/shard_map/plan/pallas_call | solution.py:199
  8.1 6.1 %all-to-all-start = ((bf16[8,32,640]{2,1,0:T(8,128)(2,1)}), bf16[8,32,640]{2,1,0:T(8,128)(2,1)S(1)}, u32[]{:S(2)}, u32[]{:S(2)}) async-start(bf16[8,32,640]{2,1,0:T(8,128)(2,1)} %bitcast.12), calls=%async_computation | async-start | bytes 655360 | tf_op jit(solution)/shard_map/all_to_all | solution.py:763
  14.2 6.3 %pack.1 = (bf16[8,512,128]{2,1,0:T(8,128)(2,1)}, bf16[8,84,16,128]{3,2,1,0:T(8,128)(2,1)}) custom-call(s32[32,128]{1,0:T(8,128)} %get-tuple-element.32.meta_ref.meta_hbm, bf16[8,512,128]{2,1,0:T(8,128)(2,1)} %here_hbm.1, bf16[8,64,512]{2,1,0:T(8,128)(2,1)} %q_hbm.3, bf16[8,64,128]{2,1,0:T(8,128)(2,1)} %k_hbm.3, bf16[1024,16,128]{2,1,0:T(8,128)(2,1)} %pool_hbm.3), custom_call_target="tpu_custom_call" | custom-call | tf_op jit(solution)/shard_map/pack/pallas_call | solution.py:240
  20.5 1.5 %all-to-all-done = bf16[8,32,640]{2,1,0:T(8,128)(2,1)S(1)} async-done(((bf16[8,32,640]{2,1,0:T(8,128)(2,1)}), bf16[8,32,640]{2,1,0:T(8,128)(2,1)S(1)}, u32[]{:S(2)}, u32[]{:S(2)}) %all-to-all-start) | async-done | bytes 327712 | tf_op jit(solution)/shard_map/all_to_all | solution.py:763
  22.0 3.7 %all-to-all-start.1 = ((bf16[8,512,128]{2,1,0:T(8,128)(2,1)}), bf16[8,512,128]{2,1,0:T(8,128)(2,1)S(1)}, u32[]{:S(2)}, u32[]{:S(2)}) async-start(bf16[8,512,128]{2,1,0:T(8,128)(2,1)} %get-tuple-element.35.after_ref), calls=%async_computation.1 | async-start | bytes 2097152 | tf_op jit(solution)/shard_map/all_to_all | solution.py:763
  25.7 2.1 %join.1 = (bf16[512,512]{1,0:T(8,128)(2,1)}, f32[512,128]{1,0:T(8,128)}, s32[24,128]{1,0:T(8,128)}) custom-call(bf16[512,640]{1,0:T(8,128)(2,1)} %get-tuple-element.33.own_hbm, bf16[256,640]{1,0:T(8,128)(2,1)} %bitcast.11, s32[32,128]{1,0:T(8,128)} %get-tuple-element.32.meta_ref.meta_hbm, bf16[8,512,128]{2,1,0:T(8,128)(2,1)} %get-tuple-element.35.after_ref, ...), custom_call_target="tpu_custom_call" | custom-call | tf_op jit(solution)/shard_map/join/pallas_call | solution.py:279
  27.8 2.8 %collective-permute-start.5 = (bf16[512,512]{1,0:T(8,128)(2,1)}, bf16[512,512]{1,0:T(8,128)(2,1)}, u32[]{:S(2)}, u32[]{:S(2)}) collective-permute-start(bf16[512,512]{1,0:T(8,128)(2,1)} %get-tuple-element.38.x_hbm.refs_0_), channel_id=1, source_target_pairs={{0,12},{1,13},{2,14},{3,15},{4,0},{5,1},{6,2},{7,3},{8,4},{9,5},{1... | collective-permute-start | bytes 1572872 | tf_op jit(solution)/shard_map/ppermute | solution.py:760
  30.6 2.5 %collective-permute-start.3 = (bf16[512,512]{1,0:T(8,128)(2,1)}, bf16[512,512]{1,0:T(8,128)(2,1)}, u32[]{:S(2)}, u32[]{:S(2)}) collective-permute-start(bf16[512,512]{1,0:T(8,128)(2,1)} %get-tuple-element.38.x_hbm.refs_0_), channel_id=1, source_target_pairs={{0,2},{1,3},{2,0},{3,1},{4,6},{5,7},{6,4},{7,5},{8,10},{9,11},{10,... | collective-permute-start | bytes 1572872 | tf_op jit(solution)/shard_map/ppermute | solution.py:757
  33.1 7.0 %all-to-all-done.1.far_hbm = bf16[8,512,128]{2,1,0:T(8,128)(2,1)S(1)} async-done(((bf16[8,512,128]{2,1,0:T(8,128)(2,1)}), bf16[8,512,128]{2,1,0:T(8,128)(2,1)S(1)}, u32[]{:S(2)}, u32[]{:S(2)}) %all-to-all-start.1) | async-done | bytes 1048608 | tf_op jit(solution)/shard_map/all_to_all | solution.py:763
  41.1 3.6 %down_product.1 = (f32[256,128]{1,0:T(8,128)}, f32[256,128]{1,0:T(8,128)}) custom-call(s32[1]{0:T(128)} %bitcast.core_ref.par_ref, bf16[512,512]{1,0:T(8,128)(2,1)} %get-tuple-element.38.x_hbm.refs_0_, bf16[8,512,128]{2,1,0:T(8,128)(2,1)} %here_hbm.1, bf16[8,512,128]{2,1,0:T(8,128)(2,1)} %copy-done.2, bf16[512,128]{1,0:T(8,128)(2,1)} %get-tuple-element.39.cand_hbm), custom_call_target="tpu_custom_call" | custom-call | tf_op jit(solution)/shard_map/down_product/pallas_call | solution.py:440
  44.7 3.8 %collective-permute-start.1 = (f32[256,128]{1,0:T(8,128)}, f32[256,128]{1,0:T(8,128)S(1)}, u32[]{:S(2)}, u32[]{:S(2)}) collective-permute-start(f32[256,128]{1,0:T(8,128)} %get-tuple-element.41), channel_id=1, source_target_pairs={{0,1},{1,0},{2,3},{3,2},{4,5},{5,4},{6,7},{7,6},{8,9},{9,8},{10,11... | collective-permute-start | bytes 393224 | tf_op jit(solution)/shard_map/ppermute | solution.py:754
  48.5 1.9 %slices.2 = (bf16[256,512]{1,0:T(8,128)(2,1)}, bf16[256,512]{1,0:T(8,128)(2,1)}) custom-call(bf16[512,512]{1,0:T(8,128)(2,1)} %collective-permute-done.4.refs_0_.refs_1_, bf16[512,512]{1,0:T(8,128)(2,1)} %collective-permute-done.5.refs_1_.refs_2_, bf16[8192,512]{1,0:T(8,128)(2,1)} %collective-permute-done.6.refs_2_.refs_7_, bf16[8192,128]{1,0:T(8,128)(2,1)} %copy-done.1), custom_call_target="tpu_custom_call" | custom-call | tf_op jit(solution)/shard_map/slices/pallas_call | solution.py:311
  50.4 1.4 %collective-permute-start.8 = (bf16[256,512]{1,0:T(8,128)(2,1)}, bf16[256,512]{1,0:T(8,128)(2,1)}, u32[]{:S(2)}, u32[]{:S(2)}) collective-permute-start(bf16[256,512]{1,0:T(8,128)(2,1)} %get-tuple-element.42), channel_id=1, source_target_pairs={{0,4},{1,5},{2,6},{3,7},{4,8},{5,9},{6,10},{7,11},{8,12},{9,13},{1... | collective-permute-start | bytes 786440 | tf_op jit(solution)/shard_map/ppermute | solution.py:760
  51.7 1.5 %collective-permute-start.9 = (bf16[256,512]{1,0:T(8,128)(2,1)}, bf16[256,512]{1,0:T(8,128)(2,1)}, u32[]{:S(2)}, u32[]{:S(2)}) collective-permute-start(bf16[256,512]{1,0:T(8,128)(2,1)} %get-tuple-element.43), channel_id=1, source_target_pairs={{0,12},{1,13},{2,14},{3,15},{4,0},{5,1},{6,2},{7,3},{8,4},{9,5},{1... | collective-permute-start | bytes 786440 | tf_op jit(solution)/shard_map/ppermute | solution.py:760
  53.3 2.5 %collective-permute-start.2 = (f32[256,128]{1,0:T(8,128)S(1)}, f32[256,128]{1,0:T(8,128)S(1)}, u32[]{:S(2)}, u32[]{:S(2)}) collective-permute-start(f32[256,128]{1,0:T(8,128)S(1)} %add.20), channel_id=1, source_target_pairs={{0,2},{1,3},{2,0},{3,1},{4,6},{5,7},{6,4},{7,5},{8,10},{9,11},{10,... | collective-permute-start | bytes 393224 | tf_op jit(solution)/shard_map/ppermute | solution.py:757
  55.8 2.9 %collective-permute-done.2 = f32[256,128]{1,0:T(8,128)S(1)} collective-permute-done((f32[256,128]{1,0:T(8,128)S(1)}, f32[256,128]{1,0:T(8,128)S(1)}, u32[]{:S(2)}, u32[]{:S(2)}) %collective-permute-start.2) | collective-permute-done | bytes 131104 | tf_op jit(solution)/shard_map/ppermute | solution.py:757
  58.7 3.6 %all-to-all-start.2 = ((bf16[8,84,16,128]{3,2,1,0:T(8,128)(2,1)}), bf16[8,84,16,128]{3,2,1,0:T(8,128)(2,1)S(1)}, u32[]{:S(2)}, u32[]{:S(2)}) async-start(bf16[8,84,16,128]{3,2,1,0:T(8,128)(2,1)} %get-tuple-element.45), calls=%async_computation.2 | async-start | bytes 5505024 | tf_op jit(solution)/shard_map/all_to_all | solution.py:763
  62.4 2.6 %collective-permute-start.15 = (bf16[512,512]{1,0:T(8,128)(2,1)}, bf16[512,512]{1,0:T(8,128)(2,1)S(1)}, u32[]{:S(2)}, u32[]{:S(2)}) collective-permute-start(bf16[512,512]{1,0:T(8,128)(2,1)} %collective-permute-done.3.refs_0_), channel_id=1, source_target_pairs={{0,12},{1,13},{2,14},{3,15},{4,0},{5,1},{6,2},{7,3},{8,4},{9,5},{1... | collective-permute-start | bytes 1572872 | tf_op jit(solution)/shard_map/ppermute | solution.py:760
  65.0 2.7 %collective-permute-start.12 = (f32[256,128]{1,0:T(8,128)S(1)}, f32[256,128]{1,0:T(8,128)S(1)}, u32[]{:S(2)}, u32[]{:S(2)}) collective-permute-start(f32[256,128]{1,0:T(8,128)S(1)} %add.21), channel_id=1, source_target_pairs={{0,12},{1,13},{2,14},{3,15},{4,0},{5,1},{6,2},{7,3},{8,4},{9,5},{1... | collective-permute-start | bytes 393224 | tf_op jit(solution)/shard_map/ppermute | solution.py:760
  68.8 7.3 %matmul_far_own.2 = (f32[512,768]{1,0:T(8,128)}, f32[512,512]{1,0:T(8,128)}) custom-call(s32[1]{0:T(128)} %bitcast.10.at_ref, bf16[512,512]{1,0:T(8,128)(2,1)} %get-tuple-element.38.x_hbm.refs_0_, bf16[512,512]{1,0:T(8,128)(2,1)} %collective-permute-done.4.refs_0_.refs_1_, bf16[512,512]{1,0:T(8,128)(2,1)} %collective-permute-done.5.refs_1_.refs_2_, ...), custom_call_target="tpu_custom_call" | custom-call | tf_op jit(solution)/shard_map/matmul_far_own/pallas_call | solution.py:389
  78.1 1.8 %slices.3 = (bf16[256,512]{1,0:T(8,128)(2,1)}, bf16[256,512]{1,0:T(8,128)(2,1)}) custom-call(bf16[512,512]{1,0:T(8,128)(2,1)} %copy-done.4, bf16[512,512]{1,0:T(8,128)(2,1)} %copy-done.3, f32[512,768]{1,0:T(8,128)} %get-tuple-element.49.refs_2_.refs_9_), custom_call_target="tpu_custom_call" | custom-call | tf_op jit(solution)/shard_map/slices/pallas_call | solution.py:311
  79.9 1.2 collective-permute-start.16
  81.1 1.5 %collective-permute-start.17 = (bf16[256,512]{1,0:T(8,128)(2,1)}, bf16[256,512]{1,0:T(8,128)(2,1)S(1)}, u32[]{:S(2)}, u32[]{:S(2)}) collective-permute-start(bf16[256,512]{1,0:T(8,128)(2,1)} %get-tuple-element.51), channel_id=1, source_target_pairs={{0,12},{1,13},{2,14},{3,15},{4,0},{5,1},{6,2},{7,3},{8,4},{9,5},{1... | collective-permute-start | bytes 786440 | tf_op jit(solution)/shard_map/ppermute | solution.py:760
  83.7 7.1 %collective-permute-start.13 = (bf16[256,128]{1,0:T(8,128)(2,1)S(1)}, bf16[256,128]{1,0:T(8,128)(2,1)S(1)}, u32[]{:S(2)}, u32[]{:S(2)}) collective-permute-start(bf16[256,128]{1,0:T(8,128)(2,1)S(1)} %add_convert_fusion.mine_hbm), channel_id=1, source_target_pairs={{0,1},{1,0},{2,3},{3,2},{4,5},{5,4},{6,7},{7,6},{8,9},{9,8},{10,11... | collective-permute-start | bytes 196616 | tf_op jit(solution)/shard_map/ppermute | solution.py:754
  92.5 8.5 %matmul_far_own.3 = (f32[512,768]{1,0:T(8,128)}, f32[512,512]{1,0:T(8,128)}) custom-call(s32[1]{0:T(128)} %bitcast.10.at_ref, bf16[512,512]{1,0:T(8,128)(2,1)} %collective-permute-done.3.refs_0_, bf16[512,512]{1,0:T(8,128)(2,1)} %copy-done.4, bf16[512,512]{1,0:T(8,128)(2,1)} %copy-done.3, bf16[256,512]{1,0:T(8,128)(2,1)} %copy-done.6, ...), custom_call_target="tpu_custom_call" | custom-call | tf_op jit(solution)/shard_map/matmul_far_own/pallas_call | solution.py:389
  101.0 2.4 %collective-permute-start.20 = (bf16[8,84,16,128]{3,2,1,0:T(8,128)(2,1)S(1)}, bf16[8,84,16,128]{3,2,1,0:T(8,128)(2,1)}, u32[]{:S(2)}, u32[]{:S(2)}) collective-permute-start(bf16[8,84,16,128]{3,2,1,0:T(8,128)(2,1)S(1)} %all-to-all-done.2.far_hbm.got_hbm), channel_id=1, source_target_pairs={{0,1},{1,0},{2,3},{3,2},{4,5},{5,4},{6,7},{7,6},{8,9},{9,8},{10,11... | collective-permute-start | bytes 8257544 | tf_op jit(solution)/shard_map/ppermute | solution.py:754
  103.5 4.1 %up_product.1 = (f32[512,512]{1,0:T(8,128)}, f32[512,128]{1,0:T(8,128)}, f32[512,128]{1,0:T(8,128)}, f32[512,128]{1,0:T(8,128)}) custom-call(s32[1]{0:T(128)} %bitcast.core_ref.par_ref, bf16[256,128]{1,0:T(8,128)(2,1)} %copy-done.10, bf16[256,128]{1,0:T(8,128)(2,1)} %copy-done.9, bf16[8,84,16,128]{3,2,1,0:T(8,128)(2,1)} %copy-done, ...), custom_call_target="tpu_custom_call" | custom-call | tf_op jit(solution)/shard_map/up_product/pallas_call | solution.py:541
  107.6 1.4 %collective-permute-start.19 = (f32[512,128]{1,0:T(8,128)}, f32[512,128]{1,0:T(8,128)S(1)}, u32[]{:S(2)}, u32[]{:S(2)}) collective-permute-start(f32[512,128]{1,0:T(8,128)} %get-tuple-element.59.kv_hbm), channel_id=1, source_target_pairs={{0,1},{1,0},{2,3},{3,2},{4,5},{5,4},{6,7},{7,6},{8,9},{9,8},{10,11... | collective-permute-start | bytes 786440 | tf_op jit(solution)/shard_map/ppermute | solution.py:754
  109.1 1.6 %collective-permute-done.18.rx_hbm = f32[512,768]{1,0:T(8,128)} collective-permute-done((f32[512,768]{1,0:T(8,128)}, f32[512,768]{1,0:T(8,128)}, u32[]{:S(2)}, u32[]{:S(2)}) %collective-permute-start.18) | collective-permute-done | bytes 1572896 | tf_op jit(solution)/shard_map/ppermute | solution.py:754
  111.7 19.8 %attend.1 = (bf16[128,4,512]{2,1,0:T(4,128)(2,1)}, bf16[1024,16,128]{2,1,0:T(8,128)(2,1)}) custom-call(s32[1]{0:T(128)} %bitcast.core_ref.par_ref, s32[32,128]{1,0:T(8,128)} %get-tuple-element.32.meta_ref.meta_hbm, s32[24,128]{1,0:T(8,128)} %get-tuple-element.36.lens_ref, f32[512,512]{1,0:T(8,128)} %get-tuple-element.57.own_hbm, ...), custom_call_target="tpu_custom_call" | custom-call | tf_op jit(solution)/shard_map/attend/pallas_call | solution.py:716
  (54 shorter events, 8.6 us)
Async XLA Ops:
  0.6 47.9 %collective-permute-start.6 = (bf16[8192,512]{1,0:T(8,128)(2,1)}, bf16[8192,512]{1,0:T(8,128)(2,1)}, u32[]{:S(2)}, u32[]{:S(2)}) collective-permute-start(bf16[8192,512]{1,0:T(8,128)(2,1)} %refs_5_.3), channel_id=1, source_target_pairs={{0,1},{1,0},{2,3},{3,2},{4,5},{5,4},{6,7},{7,6},{8,9},{9,8},{10,11... | collective-permute-start | bytes 25165832 | tf_op jit(solution)/shard_map/ppermute | solution.py:754
  2.1 23.5 %collective-permute-start = (bf16[1024,16,128]{2,1,0:T(8,128)(2,1)}, bf16[1024,16,128]{2,1,0:T(8,128)(2,1)}, u32[]{:S(2)}, u32[]{:S(2)}) collective-permute-start(bf16[1024,16,128]{2,1,0:T(8,128)(2,1)} %pool_hbm.3), channel_id=1, source_target_pairs={{0,1},{1,0},{2,3},{3,2},{4,5},{5,4},{6,7},{7,6},{8,9},{9,8},{10,11... | collective-permute-start | bytes 12582920 | tf_op jit(solution)/shard_map/ppermute | solution.py:754
  2.2 42.4 %collective-permute-start.7 = (bf16[8192,128]{1,0:T(8,128)(2,1)}, bf16[8192,128]{1,0:T(8,128)(2,1)S(1)}, u32[]{:S(2)}, u32[]{:S(2)}) collective-permute-start(bf16[8192,128]{1,0:T(8,128)(2,1)} %refs_6_.3), channel_id=1, source_target_pairs={{0,1},{1,0},{2,3},{3,2},{4,5},{5,4},{6,7},{7,6},{8,9},{9,8},{10,11... | collective-permute-start | bytes 6291464 | tf_op jit(solution)/shard_map/ppermute | solution.py:754
  8.1 13.8 %all-to-all-start = ((bf16[8,32,640]{2,1,0:T(8,128)(2,1)}), bf16[8,32,640]{2,1,0:T(8,128)(2,1)S(1)}, u32[]{:S(2)}, u32[]{:S(2)}) async-start(bf16[8,32,640]{2,1,0:T(8,128)(2,1)} %bitcast.12), calls=%async_computation | async-start | bytes 655360 | tf_op jit(solution)/shard_map/all_to_all | solution.py:763
  22.0 3.7 %copy-start.5 = (bf16[8,32,640]{2,1,0:T(8,128)(2,1)}, bf16[8,32,640]{2,1,0:T(8,128)(2,1)S(1)}, u32[]{:S(2)}) copy-start(bf16[8,32,640]{2,1,0:T(8,128)(2,1)S(1)} %all-to-all-done) | copy-start | bytes 983044
  22.0 18.2 %all-to-all-start.1 = ((bf16[8,512,128]{2,1,0:T(8,128)(2,1)}), bf16[8,512,128]{2,1,0:T(8,128)(2,1)S(1)}, u32[]{:S(2)}, u32[]{:S(2)}) async-start(bf16[8,512,128]{2,1,0:T(8,128)(2,1)} %get-tuple-element.35.after_ref), calls=%async_computation.1 | async-start | bytes 2097152 | tf_op jit(solution)/shard_map/all_to_all | solution.py:763
  27.8 20.6 %collective-permute-start.5 = (bf16[512,512]{1,0:T(8,128)(2,1)}, bf16[512,512]{1,0:T(8,128)(2,1)}, u32[]{:S(2)}, u32[]{:S(2)}) collective-permute-start(bf16[512,512]{1,0:T(8,128)(2,1)} %get-tuple-element.38.x_hbm.refs_0_), channel_id=1, source_target_pairs={{0,12},{1,13},{2,14},{3,15},{4,0},{5,1},{6,2},{7,3},{8,4},{9,5},{1... | collective-permute-start | bytes 1572872 | tf_op jit(solution)/shard_map/ppermute | solution.py:760
  30.6 17.8 %collective-permute-start.4 = (bf16[512,512]{1,0:T(8,128)(2,1)}, bf16[512,512]{1,0:T(8,128)(2,1)}, u32[]{:S(2)}, u32[]{:S(2)}) collective-permute-start(bf16[512,512]{1,0:T(8,128)(2,1)} %get-tuple-element.38.x_hbm.refs_0_), channel_id=1, source_target_pairs={{0,4},{1,5},{2,6},{3,7},{4,8},{5,9},{6,10},{7,11},{8,12},{9,13},{1... | collective-permute-start | bytes 1572872 | tf_op jit(solution)/shard_map/ppermute | solution.py:760
  30.6 28.1 %collective-permute-start.3 = (bf16[512,512]{1,0:T(8,128)(2,1)}, bf16[512,512]{1,0:T(8,128)(2,1)}, u32[]{:S(2)}, u32[]{:S(2)}) collective-permute-start(bf16[512,512]{1,0:T(8,128)(2,1)} %get-tuple-element.38.x_hbm.refs_0_), channel_id=1, source_target_pairs={{0,2},{1,3},{2,0},{3,1},{4,6},{5,7},{6,4},{7,5},{8,10},{9,11},{10,... | collective-permute-start | bytes 1572872 | tf_op jit(solution)/shard_map/ppermute | solution.py:757
  40.1 1.0 copy-start.2
  44.7 3.8 %copy-start.1 = (bf16[8192,128]{1,0:T(8,128)(2,1)}, bf16[8192,128]{1,0:T(8,128)(2,1)S(1)}, u32[]{:S(2)}) copy-start(bf16[8192,128]{1,0:T(8,128)(2,1)S(1)} %collective-permute-done.7.refs_3_.refs_8_) | copy-start | bytes 6291460
  44.7 8.6 %copy-start.11 = (f32[256,128]{1,0:T(8,128)S(1)}, f32[256,128]{1,0:T(8,128)}, u32[]{:S(2)}) copy-start(f32[256,128]{1,0:T(8,128)} %get-tuple-element.40) | copy-start | bytes 393220
  44.7 8.6 %collective-permute-start.1 = (f32[256,128]{1,0:T(8,128)}, f32[256,128]{1,0:T(8,128)S(1)}, u32[]{:S(2)}, u32[]{:S(2)}) collective-permute-start(f32[256,128]{1,0:T(8,128)} %get-tuple-element.41), channel_id=1, source_target_pairs={{0,1},{1,0},{2,3},{3,2},{4,5},{5,4},{6,7},{7,6},{8,9},{9,8},{10,11... | collective-permute-start | bytes 393224 | tf_op jit(solution)/shard_map/ppermute | solution.py:754
  50.4 8.4 %collective-permute-start.8 = (bf16[256,512]{1,0:T(8,128)(2,1)}, bf16[256,512]{1,0:T(8,128)(2,1)}, u32[]{:S(2)}, u32[]{:S(2)}) collective-permute-start(bf16[256,512]{1,0:T(8,128)(2,1)} %get-tuple-element.42), channel_id=1, source_target_pairs={{0,4},{1,5},{2,6},{3,7},{4,8},{5,9},{6,10},{7,11},{8,12},{9,13},{1... | collective-permute-start | bytes 786440 | tf_op jit(solution)/shard_map/ppermute | solution.py:760
  51.7 7.0 %collective-permute-start.9 = (bf16[256,512]{1,0:T(8,128)(2,1)}, bf16[256,512]{1,0:T(8,128)(2,1)}, u32[]{:S(2)}, u32[]{:S(2)}) collective-permute-start(bf16[256,512]{1,0:T(8,128)(2,1)} %get-tuple-element.43), channel_id=1, source_target_pairs={{0,12},{1,13},{2,14},{3,15},{4,0},{5,1},{6,2},{7,3},{8,4},{9,5},{1... | collective-permute-start | bytes 786440 | tf_op jit(solution)/shard_map/ppermute | solution.py:760
  53.3 5.4 %collective-permute-start.2 = (f32[256,128]{1,0:T(8,128)S(1)}, f32[256,128]{1,0:T(8,128)S(1)}, u32[]{:S(2)}, u32[]{:S(2)}) collective-permute-start(f32[256,128]{1,0:T(8,128)S(1)} %add.20), channel_id=1, source_target_pairs={{0,2},{1,3},{2,0},{3,1},{4,6},{5,7},{6,4},{7,5},{8,10},{9,11},{10,... | collective-permute-start | bytes 393224 | tf_op jit(solution)/shard_map/ppermute | solution.py:757
  58.7 42.3 %all-to-all-start.2 = ((bf16[8,84,16,128]{3,2,1,0:T(8,128)(2,1)}), bf16[8,84,16,128]{3,2,1,0:T(8,128)(2,1)S(1)}, u32[]{:S(2)}, u32[]{:S(2)}) async-start(bf16[8,84,16,128]{3,2,1,0:T(8,128)(2,1)} %get-tuple-element.45), calls=%async_computation.2 | async-start | bytes 5505024 | tf_op jit(solution)/shard_map/all_to_all | solution.py:763
  62.4 13.8 %collective-permute-start.15 = (bf16[512,512]{1,0:T(8,128)(2,1)}, bf16[512,512]{1,0:T(8,128)(2,1)S(1)}, u32[]{:S(2)}, u32[]{:S(2)}) collective-permute-start(bf16[512,512]{1,0:T(8,128)(2,1)} %collective-permute-done.3.refs_0_), channel_id=1, source_target_pairs={{0,12},{1,13},{2,14},{3,15},{4,0},{5,1},{6,2},{7,3},{8,4},{9,5},{1... | collective-permute-start | bytes 1572872 | tf_op jit(solution)/shard_map/ppermute | solution.py:760
  65.0 12.3 %collective-permute-start.14 = (bf16[512,512]{1,0:T(8,128)(2,1)}, bf16[512,512]{1,0:T(8,128)(2,1)S(1)}, u32[]{:S(2)}, u32[]{:S(2)}) collective-permute-start(bf16[512,512]{1,0:T(8,128)(2,1)} %collective-permute-done.3.refs_0_), channel_id=1, source_target_pairs={{0,4},{1,5},{2,6},{3,7},{4,8},{5,9},{6,10},{7,11},{8,12},{9,13},{1... | collective-permute-start | bytes 1572872 | tf_op jit(solution)/shard_map/ppermute | solution.py:760
  65.0 17.7 %collective-permute-start.12 = (f32[256,128]{1,0:T(8,128)S(1)}, f32[256,128]{1,0:T(8,128)S(1)}, u32[]{:S(2)}, u32[]{:S(2)}) collective-permute-start(f32[256,128]{1,0:T(8,128)S(1)} %add.21), channel_id=1, source_target_pairs={{0,12},{1,13},{2,14},{3,15},{4,0},{5,1},{6,2},{7,3},{8,4},{9,5},{1... | collective-permute-start | bytes 393224 | tf_op jit(solution)/shard_map/ppermute | solution.py:760
  67.7 15.0 %collective-permute-start.11 = (f32[256,128]{1,0:T(8,128)S(1)}, f32[256,128]{1,0:T(8,128)}, u32[]{:S(2)}, u32[]{:S(2)}) collective-permute-start(f32[256,128]{1,0:T(8,128)S(1)} %add.21), channel_id=1, source_target_pairs={{0,4},{1,5},{2,6},{3,7},{4,8},{5,9},{6,10},{7,11},{8,12},{9,13},{1... | collective-permute-start | bytes 393224 | tf_op jit(solution)/shard_map/ppermute | solution.py:760
  67.7 15.0 %collective-permute-start.10 = (f32[256,128]{1,0:T(8,128)S(1)}, f32[256,128]{1,0:T(8,128)}, u32[]{:S(2)}, u32[]{:S(2)}) collective-permute-start(f32[256,128]{1,0:T(8,128)S(1)} %add.21), channel_id=1, source_target_pairs={{0,8},{1,9},{2,10},{3,11},{4,12},{5,13},{6,14},{7,15},{8,0},{9,1},... | collective-permute-start | bytes 393224 | tf_op jit(solution)/shard_map/ppermute | solution.py:760
  76.2 1.1 copy-start.3
  79.9 11.8 %collective-permute-start.16 = (bf16[256,512]{1,0:T(8,128)(2,1)}, bf16[256,512]{1,0:T(8,128)(2,1)S(1)}, u32[]{:S(2)}, u32[]{:S(2)}) collective-permute-start(bf16[256,512]{1,0:T(8,128)(2,1)} %get-tuple-element.50), channel_id=1, source_target_pairs={{0,4},{1,5},{2,6},{3,7},{4,8},{5,9},{6,10},{7,11},{8,12},{9,13},{1... | collective-permute-start | bytes 786440 | tf_op jit(solution)/shard_map/ppermute | solution.py:760
  81.1 10.6 %collective-permute-start.17 = (bf16[256,512]{1,0:T(8,128)(2,1)}, bf16[256,512]{1,0:T(8,128)(2,1)S(1)}, u32[]{:S(2)}, u32[]{:S(2)}) collective-permute-start(bf16[256,512]{1,0:T(8,128)(2,1)} %get-tuple-element.51), channel_id=1, source_target_pairs={{0,12},{1,13},{2,14},{3,15},{4,0},{5,1},{6,2},{7,3},{8,4},{9,5},{1... | collective-permute-start | bytes 786440 | tf_op jit(solution)/shard_map/ppermute | solution.py:760
  83.7 17.3 %copy-start.10 = (bf16[256,128]{1,0:T(8,128)(2,1)}, bf16[256,128]{1,0:T(8,128)(2,1)S(1)}, u32[]{:S(2)}) copy-start(bf16[256,128]{1,0:T(8,128)(2,1)S(1)} %add_convert_fusion.mine_hbm) | copy-start | bytes 196612
  83.7 8.0 %collective-permute-start.13 = (bf16[256,128]{1,0:T(8,128)(2,1)S(1)}, bf16[256,128]{1,0:T(8,128)(2,1)S(1)}, u32[]{:S(2)}, u32[]{:S(2)}) collective-permute-start(bf16[256,128]{1,0:T(8,128)(2,1)S(1)} %add_convert_fusion.mine_hbm), channel_id=1, source_target_pairs={{0,1},{1,0},{2,3},{3,2},{4,5},{5,4},{6,7},{7,6},{8,9},{9,8},{10,11... | collective-permute-start | bytes 196616 | tf_op jit(solution)/shard_map/ppermute | solution.py:754
  91.7 0.8 copy-start.7
  101.0 2.5 %copy-start = (bf16[8,84,16,128]{3,2,1,0:T(8,128)(2,1)}, bf16[8,84,16,128]{3,2,1,0:T(8,128)(2,1)S(1)}, u32[]{:S(2)}) copy-start(bf16[8,84,16,128]{3,2,1,0:T(8,128)(2,1)S(1)} %all-to-all-done.2.far_hbm.got_hbm) | copy-start | bytes 8257540
  101.0 10.0 %collective-permute-start.20 = (bf16[8,84,16,128]{3,2,1,0:T(8,128)(2,1)S(1)}, bf16[8,84,16,128]{3,2,1,0:T(8,128)(2,1)}, u32[]{:S(2)}, u32[]{:S(2)}) collective-permute-start(bf16[8,84,16,128]{3,2,1,0:T(8,128)(2,1)S(1)} %all-to-all-done.2.far_hbm.got_hbm), channel_id=1, source_target_pairs={{0,1},{1,0},{2,3},{3,2},{4,5},{5,4},{6,7},{7,6},{8,9},{9,8},{10,11... | collective-permute-start | bytes 8257544 | tf_op jit(solution)/shard_map/ppermute | solution.py:754
  103.5 7.2 %collective-permute-start.18 = (f32[512,768]{1,0:T(8,128)}, f32[512,768]{1,0:T(8,128)}, u32[]{:S(2)}, u32[]{:S(2)}) collective-permute-start(f32[512,768]{1,0:T(8,128)} %get-tuple-element.58.far_hbm), channel_id=1, source_target_pairs={{0,1},{1,0},{2,3},{3,2},{4,5},{5,4},{6,7},{7,6},{8,9},{9,8},{10,11... | collective-permute-start | bytes 4718600 | tf_op jit(solution)/shard_map/ppermute | solution.py:754
  107.6 3.4 %collective-permute-start.19 = (f32[512,128]{1,0:T(8,128)}, f32[512,128]{1,0:T(8,128)S(1)}, u32[]{:S(2)}, u32[]{:S(2)}) collective-permute-start(f32[512,128]{1,0:T(8,128)} %get-tuple-element.59.kv_hbm), channel_id=1, source_target_pairs={{0,1},{1,0},{2,3},{3,2},{4,5},{5,4},{6,7},{7,6},{8,9},{9,8},{10,11... | collective-permute-start | bytes 786440 | tf_op jit(solution)/shard_map/ppermute | solution.py:754
  (4 other events, 2.9 us)

commit v4 on v3

--- a/solution.py
+++ b/solution.py
@@ -48,7 +48,7 @@
 
 
 def plan_kernel(
-    me_ref, mig_hbm, sra_hbm, ssa_hbm, len_hbm, prev_hbm, moved_hbm, tok_hbm,
+    mig_hbm, sra_hbm, ssa_hbm, len_hbm, prev_hbm, moved_hbm, tok_hbm,
     send_hbm, own_hbm, cand_hbm, meta_hbm,
     mig_ref, sra_ref, ssa_ref, len_ref, prev_ref, moved_ref, tok_ref, send_ref, own_ref, cand_ref, meta_ref, sem,
 ):
@@ -60,7 +60,7 @@
         sem,
     )
     settle(loads[:6])
-    r = me_ref[0]
+    r = lax.axis_index("rep").astype(I32)
     groups, per = mig_ref.shape
     half = per // 2
     mig = mig_ref[...]
@@ -187,7 +187,7 @@
     return jax.ShapeDtypeStruct(shape, dtype)
 
 
-def plan(me, mig, sra, ssa, lengths, prev, moved, tok):
+def plan(mig, sra, ssa, lengths, prev, moved, tok):
     rows = tok.shape[0]
     ins = (mig, sra, ssa, lengths, prev, moved, tok)
     outs = (
@@ -199,13 +199,13 @@
     return pl.pallas_call(
         plan_kernel,
         out_shape=outs,
-        in_specs=[sspec()] + [hspec()] * 7,
+        in_specs=[hspec()] * 7,
         out_specs=(hspec(),) * 4,
         scratch_shapes=[pltpu.VMEM(a.shape, a.dtype) for a in ins + outs]
         + [pltpu.SemaphoreType.DMA((7,))],
         compiler_params=params(),
         name="plan",
-    )(me, *ins)
+    )(*ins)
 
 
 def pack_kernel(
@@ -324,7 +324,7 @@
 WIDTH = {"far": 768, "own": 512}
 
 
-def matmul_kernel(blocks, offsets, chunk, n, parts, extra, after, at_ref, *refs):
+def matmul_kernel(blocks, offsets, chunk, n, parts, extra, after, *refs):
     np_, nb = len(parts), len(blocks)
     xs, refs = refs[:n], refs[n:]
     weights, refs = refs[:4], refs[4:]
@@ -334,7 +334,8 @@
     add, refs = refs[: extra * np_], refs[extra * np_ :]
     res, refs = refs[:np_], refs[np_:]
     x_ref, x_sem, sem, add_sem, out_sem = refs
-    y, hi, core = at_ref[0] // 4, (at_ref[0] // 2) % 2, at_ref[0] % 2
+    at = lax.axis_index("tp").astype(I32)
+    y, hi, core = at // 4, (at // 2) % 2, at % 2
     place = [(((y + dy) % 4) * 2 + (hi + dx) % 2) * 2 + core for dy, dx in offsets]
     x_loads, w_loads = [], {}
     for k, cut in enumerate(blocks):
@@ -382,7 +383,7 @@
     settle(stores)
 
 
-def matmul(parts, at, offsets, blocks, xs, weights, adds=(), after=(), chunk=4):
+def matmul(parts, offsets, blocks, xs, weights, adds=(), after=(), chunk=4):
     nb = len(blocks)
     outs = tuple(sds((512, WIDTH[p]), F32) for p in parts)
     flat = tuple(a[o] for o in range(len(parts)) for a in adds)
@@ -391,7 +392,7 @@
             matmul_kernel, blocks, offsets, min(chunk, nb), len(xs), parts, len(adds), len(after)
         ),
         out_shape=outs,
-        in_specs=[sspec()] + [hspec()] * (len(xs) + 4 + len(flat) + len(after)),
+        in_specs=[hspec()] * (len(xs) + 4 + len(flat) + len(after)),
         out_specs=(hspec(),) * len(parts),
         scratch_shapes=[pltpu.VMEM((nb * 512, WIDTH[p]), BF16) for p in parts]
         + [pltpu.VMEM(a.shape, a.dtype) for a in (*flat, *outs)]
@@ -404,11 +405,11 @@
         ],
         compiler_params=params(),
         name="matmul_" + "_".join(parts),
-    )(at, *xs, *weights, *flat, *after)
+    )(*xs, *weights, *flat, *after)
 
 
 def down_kernel(
-    core_ref, x_hbm, here_hbm, far_hbm, cand_hbm, keep_hbm, give_hbm,
+    x_hbm, here_hbm, far_hbm, cand_hbm, keep_hbm, give_hbm,
     x_ref, here_ref, far_ref, cand_ref, out_ref, sem,
 ):
     loads = fetch(
@@ -430,17 +431,18 @@
         acc = y if acc is None else acc + y
     out_ref[...] = acc
     half = out_ref.shape[0] // 2
-    mine = pl.ds(pl.multiple_of(core_ref[0] * half, half), half)
-    other = pl.ds(pl.multiple_of((1 - core_ref[0]) * half, half), half)
+    core = lax.axis_index("tp").astype(I32) % 2
+    mine = pl.ds(pl.multiple_of(core * half, half), half)
+    other = pl.ds(pl.multiple_of((1 - core) * half, half), half)
     settle(fetch(((out_ref.at[mine], keep_hbm), (out_ref.at[other], give_hbm)), sem))
 
 
-def down_product(core, x, here, far, cand):
+def down_product(x, here, far, cand):
     rows = x.shape[0]
     return pl.pallas_call(
         down_kernel,
         out_shape=(sds((rows // 2, HEAD), F32),) * 2,
-        in_specs=[sspec()] + [hspec()] * 4,
+        in_specs=[hspec()] * 4,
         out_specs=(hspec(), hspec()),
         scratch_shapes=[
             pltpu.VMEM(x.shape, BF16),
@@ -452,7 +454,7 @@
         ],
         compiler_params=params(),
         name="down_product",
-    )(core, x, here, far, cand)
+    )(x, here, far, cand)
 
 
 def turn_table():
@@ -468,14 +470,15 @@
 
 
 def up_kernel(
-    core_ref, mine_hbm, other_hbm, far_hbm, cand_hbm, q_hbm, k_hbm, len_hbm, table_hbm, acc_hbm,
+    mine_hbm, other_hbm, far_hbm, cand_hbm, q_hbm, k_hbm, len_hbm, table_hbm, acc_hbm,
     out_hbm, kv_hbm, cos_hbm, sin_hbm,
     down_ref, far, cand_ref, q_here, k_here, len_ref, table_ref, acc_ref,
     out_ref, kv_ref, cos_ref, sin_ref, sem,
 ):
     half = mine_hbm.shape[0]
-    mine = pl.ds(pl.multiple_of(core_ref[0] * half, half), half)
-    other = pl.ds(pl.multiple_of((1 - core_ref[0]) * half, half), half)
+    core = lax.axis_index("tp").astype(I32) % 2
+    mine = pl.ds(pl.multiple_of(core * half, half), half)
+    other = pl.ds(pl.multiple_of((1 - core) * half, half), half)
     settle(
         fetch(
             (
@@ -534,21 +537,21 @@
     )
 
 
-def up_product(core, mine, other, far, cand, up_q, up_kv, length, acc):
+def up_product(mine, other, far, cand, up_q, up_kv, length, acc):
     rows = cand.shape[0]
     ins = (cand, up_q, up_kv, length, jnp.asarray(turn_table()), acc)
     outs = (sds((rows, 512), F32),) + (sds((rows, HEAD), F32),) * 3
     return pl.pallas_call(
         up_kernel,
         out_shape=outs,
-        in_specs=[sspec()] + [hspec()] * 9,
+        in_specs=[hspec()] * 9,
         out_specs=(hspec(),) * 4,
         scratch_shapes=[pltpu.VMEM((rows, HEAD), BF16), pltpu.VMEM((8, 20, 16, HEAD), BF16)]
         + [pltpu.VMEM(a.shape, a.dtype) for a in ins + outs]
         + [pltpu.SemaphoreType.DMA((9,))],
         compiler_params=params(),
         name="up_product",
-    )(core, mine, other, far, *ins)
+    )(mine, other, far, *ins)
 
 
 GROUP = 4
@@ -560,14 +563,13 @@
 
 
 def attend_kernel(
-    par_ref, meta_ref, lens_ref,
-    own_hbm, far_hbm, rx_hbm, kv_hbm, kv2_hbm, cos_hbm, sin_hbm,
+    meta_hbm, lens_hbm, own_hbm, far_hbm, rx_hbm, kv_hbm, kv2_hbm, cos_hbm, sin_hbm,
     pool_hbm, pool2_hbm, got_hbm, got2_hbm,
     out_hbm, new_hbm,
-    own_ref, far_ref, rx_ref, kv_ref, kv2_ref, cos_ref, sin_ref, out_ref, new_ref,
+    meta_ref, lens_ref, own_ref, far_ref, rx_ref, kv_ref, kv2_ref, cos_ref, sin_ref, out_ref, new_ref,
     q_scr, f_scr, page_scr, mask_scr, sem,
 ):
-    odd = par_ref[0]
+    odd = lax.axis_index("tp").astype(I32) % 2
     def pages_from(i, pool, got):
         return [(pool, page_scr.at[i, :POOL])] + [
             (got.at[g, :64], page_scr.at[i, POOL + 64 * g : POOL + 64 * g + 64]) for g in range(8)
@@ -575,8 +577,8 @@
 
     copies = fetch(
         (
-            *pages_from(0, pool_hbm, got_hbm),
-            (far_hbm, far_ref), (rx_hbm, rx_ref), (kv_hbm, kv_ref), (kv2_hbm, kv2_ref),
+            (meta_hbm, meta_ref), (lens_hbm, lens_ref), *pages_from(0, pool_hbm, got_hbm),
+            (far_hbm.at[:, 512:], far_ref), (rx_hbm, rx_ref), (kv_hbm, kv_ref), (kv2_hbm, kv2_ref),
             (cos_hbm, cos_ref), (sin_hbm, sin_ref), (own_hbm, own_ref),
             *pages_from(1, pool2_hbm, got2_hbm),
         ),
@@ -584,7 +586,7 @@
     )
     page_masks(mask_scr)
     page_scr[0, ZERO_PAGE] = jnp.zeros((16, HEAD), BF16)
-    settle(copies[:9])
+    settle(copies[:3])
 
     def keep(g, _):
         kept = []
@@ -596,8 +598,10 @@
             new_ref[at] = page
         return 0
 
-    lax.fori_loop(0, 32, keep, 0)
-    settle(copies[9:16])
+    lax.fori_loop(0, 16, keep, 0)
+    settle(copies[3:11])
+    lax.fori_loop(16, 32, keep, 0)
+    settle(copies[11:18])
     cos, sin = cos_ref[...], sin_ref[...]
 
     def turn(v):
@@ -606,8 +610,8 @@
     for h in range(4):
         at = slice(h * HEAD, (h + 1) * HEAD)
         q_scr[:, at] = turn(own_ref[:, at] + rx_ref[:, at])
-    kv_own = far_ref[:, 512:640] + rx_ref[:, 640:768] + kv_ref[...]
-    kv_oth = far_ref[:, 640:768] + rx_ref[:, 512:640] + kv2_ref[...]
+    kv_own = far_ref[:, :HEAD] + rx_ref[:, 640:768] + kv_ref[...]
+    kv_oth = far_ref[:, HEAD:] + rx_ref[:, 512:640] + kv2_ref[...]
     key = turn(jnp.where(odd == 0, kv_own, kv_oth))
     value = jnp.where(odd == 0, kv_oth, kv_own)
     f_scr[:, :HEAD] = key
@@ -621,7 +625,7 @@
     )
     c32 = iota((1, 32), 1) // 4
 
-    def edge(g, _):
+    def edge_pages(g):
         at = [8 * g + e for e in range(8)]
         lengths = [lens_ref[LENGTH, p] for p in at]
         first = [jnp.minimum(n // 16, 6) for n in lengths]
@@ -638,6 +642,10 @@
                 lo = e * 32 + k * 16
                 page = page_scr[0, meta_ref[SOURCE + b, p]] * mask_scr[lens_ref[KEPT + b, p]]
                 done.append((meta_ref[TARGET + b, p], page + placed[lo : lo + 16]))
+        return done
+
+    def edge(i, _):
+        done = [pair for j in range(2) for pair in edge_pages(2 * i + j)]
         for to, page in done:
             new_ref[to] = page
         return 0
@@ -704,31 +712,35 @@
                     out_ref[slot, :, h * HEAD : (h + 1) * HEAD] = mixed[lo : lo + 4]
         return 0
 
-    lax.fori_loop(0, 16, edge, 0)
+    lax.fori_loop(0, 8, edge, 0)
     stores = fetch(((new_ref, new_hbm),), sem)
-    settle(copies[16:])
+    settle(copies[18:])
     lax.fori_loop(0, 4, mix, 0)
     settle(stores + fetch(((out_ref, out_hbm),), sem, 1))
 
 
-def attend(parity, meta, lens, own, far, rx, kv, kv2, cos, sin, pool, pool2, got, got2):
+def attend(meta, lens, own, far, rx, kv, kv2, cos, sin, pool, pool2, got, got2):
     outs = (sds((128, 4, 512), BF16), sds(pool.shape, BF16))
     return pl.pallas_call(
         attend_kernel,
         out_shape=outs,
-        in_specs=[sspec()] * 3 + [hspec()] * 11,
+        in_specs=[hspec()] * 13,
         out_specs=(hspec(), hspec()),
-        scratch_shapes=[pltpu.VMEM(a.shape, a.dtype) for a in (own, far, rx, kv, kv2, cos, sin, *outs)]
+        scratch_shapes=[pltpu.SMEM(meta.shape, I32), pltpu.SMEM(lens.shape, I32)]
+        + [
+            pltpu.VMEM(a.shape, a.dtype)
+            for a in (own, sds((512, 256), F32), rx, kv, kv2, cos, sin, *outs)
+        ]
         + [
             pltpu.VMEM((512, 512), F32),
             pltpu.VMEM((512, 3 * HEAD), F32),
             pltpu.VMEM((2, ZERO_PAGE + 1, 16, HEAD), BF16),
             pltpu.VMEM((17, 16, HEAD), BF16),
-            pltpu.SemaphoreType.DMA((25,)),
+            pltpu.SemaphoreType.DMA((27,)),
         ],
         compiler_params=params(),
         name="attend",
-    )(parity, meta, lens, own, far, rx, kv, kv2, cos, sin, pool, pool2, got, got2)
+    )(meta, lens, own, far, rx, kv, kv2, cos, sin, pool, pool2, got, got2)
 
 
 def body(
@@ -746,10 +758,6 @@
     moved_block_table,
     paged_cache_pool,
 ):
-    r = lax.axis_index("rep").astype(I32)
-    t = lax.axis_index("tp").astype(I32)
-    core = t % 2
-
     def other_core(a):
         return lax.ppermute(a, "tp", [(i, i ^ 1) for i in range(16)])
 
@@ -763,7 +771,7 @@
         return lax.all_to_all(a, "rep", split_axis=0, concat_axis=0, tiled=True)
 
     send, own, cand, meta = plan(
-        r.reshape(1), migration.reshape(8, 128), slot_request_adapter.reshape(8, 128),
+        migration.reshape(8, 128), slot_request_adapter.reshape(8, 128),
         storage_slot_adapter.reshape(1, 64), lengths.reshape(1, 128),
         previous_block_table.T, moved_block_table.T, tokens.reshape(512, 512),
     )
@@ -776,7 +784,6 @@
     far_down = swap_rep(packed)
 
     weights = (query_weight_matrix, key_value_weight, vq, vk)
-    one = core.reshape(1)
     xh = other_x(x)
     yp = along_y(x, 1)
     ym = along_y(x, -1)
@@ -785,16 +792,15 @@
     yp2, ym2 = slices(ends, (256, 256), (yp, ym), (vq, vk))
     y2 = (along_y(yp2, 1), along_y(ym2, -1))
 
-    keep, give = down_product(one, x, adapter_down_factors, far_down, cand)
+    keep, give = down_product(x, adapter_down_factors, far_down, cand)
     total = keep + other_core(give)
     total = total + other_x(total)
-    leaving, total, xh, y2 = lax.optimization_barrier((leaving, total, xh, y2))
+    leaving, total, _, _ = lax.optimization_barrier((leaving, total, xh, y2))
     got = swap_rep(leaving)
 
     xyp, xym = along_y(xh, 1), along_y(xh, -1)
-    at = t.reshape(1)
     acc = matmul(
-        ("far", "own"), at, ((0, 0), (3, 0), (1, 0), (2, 0)),
+        ("far", "own"), ((0, 0), (3, 0), (1, 0), (2, 0)),
         (((0, *full),), ((1, *full),), ((2, *full),), ((3, 0, 256), (4, 0, 256))),
         (x, yp, ym, *y2), weights,
     )
@@ -804,18 +810,17 @@
     total = total.astype(BF16)
     other_total = other_core(total)
     acc_far, acc_own = matmul(
-        ("far", "own"), at, ((0, 1), (3, 1), (1, 1), (2, 1)),
+        ("far", "own"), ((0, 1), (3, 1), (1, 1), (2, 1)),
         (((0, *full),), ((1, *full),), ((2, *full),), ((3, 0, 256), (4, 0, 256))),
         (xh, xyp, xym, *xy2), weights, ((acc[0], acc[1]),), (other_total,),
     )
     rx = other_core(acc_far)
     got, acc_own = lax.optimization_barrier((got, acc_own))
     own, kv, cos, sin = up_product(
-        one, total, other_total, got, cand, adapter_up_query, adapter_up_key_value, length,
-        acc_own,
+        total, other_total, got, cand, adapter_up_query, adapter_up_key_value, length, acc_own
     )
     return attend(
-        one, meta, lens, own, acc_far, rx, kv, other_core(kv), cos, sin,
+        meta, lens, own, acc_far, rx, kv, other_core(kv), cos, sin,
         paged_cache_pool, pool2, got, other_core(got),
     )
 

time: 132 us -> 130 us (0.985)
  Pallas kernels: 58.9 us -> 56.4 us
    pallas_call x3, Pallas kernels: 27.4 us -> 25 us  [the longest x1 17.4 us: attend(): pl.pallas_call(attend_kernel, out_shape=outs, in_specs=[hspec()] * 13, ou...]
where the time goes in v4:
time: 130 us; the launch traced here: 129 us
  Pallas kernels  56.4 us (43%)
  starting transfers between devices  50.1 us (39%)
  waiting for transfers between devices  15.4 us (12%)
  local copies, waits for them, and re-layouts  5.27 us (4%)
    pallas_call x1, Pallas kernels, attend(): pl.pallas_call(attend_kernel, out_shape=outs, in_specs=[hspec()] * 13, ou...  17.4 us
    ppermute x8, starting transfers between devices, other_core(): return lax.ppermute(a, 'tp', [(i, i ^ 1) for i in range(16)])  16.8 us
    pallas_call x2, Pallas kernels, matmul(): pl.pallas_call(functools.partial(matmul_kernel, blocks, offsets, min(chun...  15.8 us
    ppermute x11, starting transfers between devices, along_y(): return lax.ppermute(a, 'tp', [(i, (i + 4 * d) % 16) for i in range(16)])  14.9 us
    all_to_all x3, starting transfers between devices, swap_rep(): return lax.all_to_all(a, 'rep', split_axis=0, concat_axis=0, tiled=True)  13.4 us
    all_to_all x3, waiting for transfers between devices, swap_rep(): return lax.all_to_all(a, 'rep', split_axis=0, concat_axis=0, tiled=True)  8.51 us
    pallas_call x1, Pallas kernels, pack(): pl.pallas_call(pack_kernel, out_shape=(sds(down.shape, BF16), rest), in_s...  6.27 us
    ppermute x2, starting transfers between devices, other_x(): return lax.ppermute(a, 'tp', [(i, i ^ 2) for i in range(16)])  4.98 us
  transfers between devices with their start and end apart: 24, of which 7 were waited for; matrix products, arithmetic and copies ran while one was open for 2% of the time, Pallas kernels for 30%

profile of v4, /device:TPU:1, one launch (start us, length us, event | category | flops | bytes accessed | tf_op | source)
XLA Modules:
  0.0 129.2 jit_solution(11510078582665130758)
XLA Ops:
  0.6 1.5 %collective-permute-start.6 = (bf16[8192,512]{1,0:T(8,128)(2,1)}, bf16[8192,512]{1,0:T(8,128)(2,1)}, u32[]{:S(2)}, u32[]{:S(2)}) collective-permute-start(bf16[8192,512]{1,0:T(8,128)(2,1)} %refs_5_.3), channel_id=1, source_target_pairs={{0,1},{1,0},{2,3},{3,2},{4,5},{5,4},{6,7},{7,6},{8,9},{9,8},{10,11... | collective-permute-start | bytes 25165832 | tf_op jit(solution)/shard_map/ppermute | solution.py:762
  2.6 2.0 %reshape.25.tok_hbm = bf16[512,512]{1,0:T(8,128)(2,1)} reshape(bf16[128,4,512]{2,1,0:T(4,128)(2,1)} %param.14) | data formatting | bytes 1048576 | tf_op jit(solution)/shard_map/reshape | solution.py:776
  4.6 3.5 %plan.1 = (bf16[256,640]{1,0:T(8,128)(2,1)}, bf16[512,640]{1,0:T(8,128)(2,1)}, bf16[512,128]{1,0:T(8,128)(2,1)}, s32[32,128]{1,0:T(8,128)}) custom-call(s32[8,128]{1,0:T(8,128)} %bitcast.10, s32[8,128]{1,0:T(8,128)} %bitcast.11, s32[1,64]{1,0:T(1,128)} %bitcast.14, s32[1,128]{1,0:T(1,128)} %bitcast.15, s32[8,128]{1,0:T(8,128)} %bitcast.12, ...), custom_call_target="tpu_custom_call" | custom-call | tf_op jit(solution)/shard_map/plan/pallas_call | solution.py:199
  8.1 6.1 %all-to-all-start = ((bf16[8,32,640]{2,1,0:T(8,128)(2,1)}), bf16[8,32,640]{2,1,0:T(8,128)(2,1)S(1)}, u32[]{:S(2)}, u32[]{:S(2)}) async-start(bf16[8,32,640]{2,1,0:T(8,128)(2,1)} %bitcast.9), calls=%async_computation | async-start | bytes 655360 | tf_op jit(solution)/shard_map/all_to_all | solution.py:771
  14.2 6.3 %pack.1 = (bf16[8,512,128]{2,1,0:T(8,128)(2,1)}, bf16[8,84,16,128]{3,2,1,0:T(8,128)(2,1)}) custom-call(s32[32,128]{1,0:T(8,128)} %get-tuple-element.29.meta_ref.meta_hbm, bf16[8,512,128]{2,1,0:T(8,128)(2,1)} %here_hbm.1, bf16[8,64,512]{2,1,0:T(8,128)(2,1)} %q_hbm.3, bf16[8,64,128]{2,1,0:T(8,128)(2,1)} %k_hbm.3, bf16[1024,16,128]{2,1,0:T(8,128)(2,1)} %pool_hbm.3), custom_call_target="tpu_custom_call" | custom-call | tf_op jit(solution)/shard_map/pack/pallas_call | solution.py:240
  20.5 1.5 %all-to-all-done = bf16[8,32,640]{2,1,0:T(8,128)(2,1)S(1)} async-done(((bf16[8,32,640]{2,1,0:T(8,128)(2,1)}), bf16[8,32,640]{2,1,0:T(8,128)(2,1)S(1)}, u32[]{:S(2)}, u32[]{:S(2)}) %all-to-all-start) | async-done | bytes 327712 | tf_op jit(solution)/shard_map/all_to_all | solution.py:771
  21.9 3.7 %all-to-all-start.1 = ((bf16[8,512,128]{2,1,0:T(8,128)(2,1)}), bf16[8,512,128]{2,1,0:T(8,128)(2,1)S(1)}, u32[]{:S(2)}, u32[]{:S(2)}) async-start(bf16[8,512,128]{2,1,0:T(8,128)(2,1)} %get-tuple-element.32.after_ref), calls=%async_computation.1 | async-start | bytes 2097152 | tf_op jit(solution)/shard_map/all_to_all | solution.py:771
  25.7 2.1 %join.1 = (bf16[512,512]{1,0:T(8,128)(2,1)}, f32[512,128]{1,0:T(8,128)}, s32[24,128]{1,0:T(8,128)}) custom-call(bf16[512,640]{1,0:T(8,128)(2,1)} %get-tuple-element.30.own_hbm, bf16[256,640]{1,0:T(8,128)(2,1)} %bitcast.8, s32[32,128]{1,0:T(8,128)} %get-tuple-element.29.meta_ref.meta_hbm, bf16[8,512,128]{2,1,0:T(8,128)(2,1)} %get-tuple-element.32.after_ref, ...), custom_call_target="tpu_custom_call" | custom-call | tf_op jit(solution)/shard_map/join/pallas_call | solution.py:279
  27.8 2.8 %collective-permute-start.5 = (bf16[512,512]{1,0:T(8,128)(2,1)}, bf16[512,512]{1,0:T(8,128)(2,1)}, u32[]{:S(2)}, u32[]{:S(2)}) collective-permute-start(bf16[512,512]{1,0:T(8,128)(2,1)} %get-tuple-element.35.x_hbm.refs_0_), channel_id=1, source_target_pairs={{0,12},{1,13},{2,14},{3,15},{4,0},{5,1},{6,2},{7,3},{8,4},{9,5},{1... | collective-permute-start | bytes 1572872 | tf_op jit(solution)/shard_map/ppermute | solution.py:768
  30.6 2.4 %collective-permute-start.3 = (bf16[512,512]{1,0:T(8,128)(2,1)}, bf16[512,512]{1,0:T(8,128)(2,1)}, u32[]{:S(2)}, u32[]{:S(2)}) collective-permute-start(bf16[512,512]{1,0:T(8,128)(2,1)} %get-tuple-element.35.x_hbm.refs_0_), channel_id=1, source_target_pairs={{0,2},{1,3},{2,0},{3,1},{4,6},{5,7},{6,4},{7,5},{8,10},{9,11},{10,... | collective-permute-start | bytes 1572872 | tf_op jit(solution)/shard_map/ppermute | solution.py:765
  33.1 7.0 %all-to-all-done.1.far_hbm = bf16[8,512,128]{2,1,0:T(8,128)(2,1)S(1)} async-done(((bf16[8,512,128]{2,1,0:T(8,128)(2,1)}), bf16[8,512,128]{2,1,0:T(8,128)(2,1)S(1)}, u32[]{:S(2)}, u32[]{:S(2)}) %all-to-all-start.1) | async-done | bytes 1048608 | tf_op jit(solution)/shard_map/all_to_all | solution.py:771
  41.1 3.6 %down_product.1 = (f32[256,128]{1,0:T(8,128)}, f32[256,128]{1,0:T(8,128)}) custom-call(bf16[512,512]{1,0:T(8,128)(2,1)} %get-tuple-element.35.x_hbm.refs_0_, bf16[8,512,128]{2,1,0:T(8,128)(2,1)} %here_hbm.1, bf16[8,512,128]{2,1,0:T(8,128)(2,1)} %copy-done.2, bf16[512,128]{1,0:T(8,128)(2,1)} %get-tuple-element.36.cand_hbm), custom_call_target="tpu_custom_call" | custom-call | tf_op jit(solution)/shard_map/down_product/pallas_call | solution.py:442
  44.7 3.8 %collective-permute-start.1 = (f32[256,128]{1,0:T(8,128)}, f32[256,128]{1,0:T(8,128)S(1)}, u32[]{:S(2)}, u32[]{:S(2)}) collective-permute-start(f32[256,128]{1,0:T(8,128)} %get-tuple-element.38), channel_id=1, source_target_pairs={{0,1},{1,0},{2,3},{3,2},{4,5},{5,4},{6,7},{7,6},{8,9},{9,8},{10,11... | collective-permute-start | bytes 393224 | tf_op jit(solution)/shard_map/ppermute | solution.py:762
  48.5 1.9 %slices.2 = (bf16[256,512]{1,0:T(8,128)(2,1)}, bf16[256,512]{1,0:T(8,128)(2,1)}) custom-call(bf16[512,512]{1,0:T(8,128)(2,1)} %collective-permute-done.4.refs_0_.refs_1_, bf16[512,512]{1,0:T(8,128)(2,1)} %collective-permute-done.5.refs_1_.refs_2_, bf16[8192,512]{1,0:T(8,128)(2,1)} %collective-permute-done.6.refs_2_.refs_7_, bf16[8192,128]{1,0:T(8,128)(2,1)} %copy-done.1), custom_call_target="tpu_custom_call" | custom-call | tf_op jit(solution)/shard_map/slices/pallas_call | solution.py:311
  50.4 1.4 %collective-permute-start.8 = (bf16[256,512]{1,0:T(8,128)(2,1)}, bf16[256,512]{1,0:T(8,128)(2,1)}, u32[]{:S(2)}, u32[]{:S(2)}) collective-permute-start(bf16[256,512]{1,0:T(8,128)(2,1)} %get-tuple-element.39), channel_id=1, source_target_pairs={{0,4},{1,5},{2,6},{3,7},{4,8},{5,9},{6,10},{7,11},{8,12},{9,13},{1... | collective-permute-start | bytes 786440 | tf_op jit(solution)/shard_map/ppermute | solution.py:768
  51.7 1.5 %collective-permute-start.9 = (bf16[256,512]{1,0:T(8,128)(2,1)}, bf16[256,512]{1,0:T(8,128)(2,1)}, u32[]{:S(2)}, u32[]{:S(2)}) collective-permute-start(bf16[256,512]{1,0:T(8,128)(2,1)} %get-tuple-element.40), channel_id=1, source_target_pairs={{0,12},{1,13},{2,14},{3,15},{4,0},{5,1},{6,2},{7,3},{8,4},{9,5},{1... | collective-permute-start | bytes 786440 | tf_op jit(solution)/shard_map/ppermute | solution.py:768
  53.3 2.5 %collective-permute-start.2 = (f32[256,128]{1,0:T(8,128)S(1)}, f32[256,128]{1,0:T(8,128)S(1)}, u32[]{:S(2)}, u32[]{:S(2)}) collective-permute-start(f32[256,128]{1,0:T(8,128)S(1)} %add.15), channel_id=1, source_target_pairs={{0,2},{1,3},{2,0},{3,1},{4,6},{5,7},{6,4},{7,5},{8,10},{9,11},{10,... | collective-permute-start | bytes 393224 | tf_op jit(solution)/shard_map/ppermute | solution.py:765
  55.8 2.9 %collective-permute-done.2 = f32[256,128]{1,0:T(8,128)S(1)} collective-permute-done((f32[256,128]{1,0:T(8,128)S(1)}, f32[256,128]{1,0:T(8,128)S(1)}, u32[]{:S(2)}, u32[]{:S(2)}) %collective-permute-start.2) | collective-permute-done | bytes 131104 | tf_op jit(solution)/shard_map/ppermute | solution.py:765
  58.7 3.6 %all-to-all-start.2 = ((bf16[8,84,16,128]{3,2,1,0:T(8,128)(2,1)}), bf16[8,84,16,128]{3,2,1,0:T(8,128)(2,1)S(1)}, u32[]{:S(2)}, u32[]{:S(2)}) async-start(bf16[8,84,16,128]{3,2,1,0:T(8,128)(2,1)} %get-tuple-element.42), calls=%async_computation.2 | async-start | bytes 5505024 | tf_op jit(solution)/shard_map/all_to_all | solution.py:771
  62.4 2.6 %collective-permute-start.15 = (bf16[512,512]{1,0:T(8,128)(2,1)}, bf16[512,512]{1,0:T(8,128)(2,1)S(1)}, u32[]{:S(2)}, u32[]{:S(2)}) collective-permute-start(bf16[512,512]{1,0:T(8,128)(2,1)} %collective-permute-done.3.refs_0_), channel_id=1, source_target_pairs={{0,12},{1,13},{2,14},{3,15},{4,0},{5,1},{6,2},{7,3},{8,4},{9,5},{1... | collective-permute-start | bytes 1572872 | tf_op jit(solution)/shard_map/ppermute | solution.py:768
  65.0 2.7 %collective-permute-start.12 = (f32[256,128]{1,0:T(8,128)S(1)}, f32[256,128]{1,0:T(8,128)S(1)}, u32[]{:S(2)}, u32[]{:S(2)}) collective-permute-start(f32[256,128]{1,0:T(8,128)S(1)} %add.16), channel_id=1, source_target_pairs={{0,12},{1,13},{2,14},{3,15},{4,0},{5,1},{6,2},{7,3},{8,4},{9,5},{1... | collective-permute-start | bytes 393224 | tf_op jit(solution)/shard_map/ppermute | solution.py:768
  68.8 7.3 %matmul_far_own.2 = (f32[512,768]{1,0:T(8,128)}, f32[512,512]{1,0:T(8,128)}) custom-call(bf16[512,512]{1,0:T(8,128)(2,1)} %get-tuple-element.35.x_hbm.refs_0_, bf16[512,512]{1,0:T(8,128)(2,1)} %collective-permute-done.4.refs_0_.refs_1_, bf16[512,512]{1,0:T(8,128)(2,1)} %collective-permute-done.5.refs_1_.refs_2_, ...), custom_call_target="tpu_custom_call" | custom-call | tf_op jit(solution)/shard_map/matmul_far_own/pallas_call | solution.py:390
  78.1 1.8 %slices.3 = (bf16[256,512]{1,0:T(8,128)(2,1)}, bf16[256,512]{1,0:T(8,128)(2,1)}) custom-call(bf16[512,512]{1,0:T(8,128)(2,1)} %copy-done.4, bf16[512,512]{1,0:T(8,128)(2,1)} %copy-done.3, f32[512,768]{1,0:T(8,128)} %get-tuple-element.43.refs_2_.refs_9_), custom_call_target="tpu_custom_call" | custom-call | tf_op jit(solution)/shard_map/slices/pallas_call | solution.py:311
  79.9 1.2 collective-permute-start.16
  81.1 1.5 %collective-permute-start.17 = (bf16[256,512]{1,0:T(8,128)(2,1)}, bf16[256,512]{1,0:T(8,128)(2,1)S(1)}, u32[]{:S(2)}, u32[]{:S(2)}) collective-permute-start(bf16[256,512]{1,0:T(8,128)(2,1)} %get-tuple-element.45), channel_id=1, source_target_pairs={{0,12},{1,13},{2,14},{3,15},{4,0},{5,1},{6,2},{7,3},{8,4},{9,5},{1... | collective-permute-start | bytes 786440 | tf_op jit(solution)/shard_map/ppermute | solution.py:768
  83.7 7.1 %collective-permute-start.13 = (bf16[256,128]{1,0:T(8,128)(2,1)S(1)}, bf16[256,128]{1,0:T(8,128)(2,1)S(1)}, u32[]{:S(2)}, u32[]{:S(2)}) collective-permute-start(bf16[256,128]{1,0:T(8,128)(2,1)S(1)} %add_convert_fusion.mine_hbm), channel_id=1, source_target_pairs={{0,1},{1,0},{2,3},{3,2},{4,5},{5,4},{6,7},{7,6},{8,9},{9,8},{10,11... | collective-permute-start | bytes 196616 | tf_op jit(solution)/shard_map/ppermute | solution.py:762
  92.5 8.5 %matmul_far_own.3 = (f32[512,768]{1,0:T(8,128)}, f32[512,512]{1,0:T(8,128)}) custom-call(bf16[512,512]{1,0:T(8,128)(2,1)} %collective-permute-done.3.refs_0_, bf16[512,512]{1,0:T(8,128)(2,1)} %copy-done.4, bf16[512,512]{1,0:T(8,128)(2,1)} %copy-done.3, bf16[256,512]{1,0:T(8,128)(2,1)} %copy-done.6, bf16[256,512]{1,0:T(8,128)(2,1)} %copy-done.7, ...), custom_call_target="tpu_custom_call" | custom-call | tf_op jit(solution)/shard_map/matmul_far_own/pallas_call | solution.py:390
  101.0 2.4 %collective-permute-start.20 = (bf16[8,84,16,128]{3,2,1,0:T(8,128)(2,1)S(1)}, bf16[8,84,16,128]{3,2,1,0:T(8,128)(2,1)}, u32[]{:S(2)}, u32[]{:S(2)}) collective-permute-start(bf16[8,84,16,128]{3,2,1,0:T(8,128)(2,1)S(1)} %all-to-all-done.2.far_hbm.got_hbm), channel_id=1, source_target_pairs={{0,1},{1,0},{2,3},{3,2},{4,5},{5,4},{6,7},{7,6},{8,9},{9,8},{10,11... | collective-permute-start | bytes 8257544 | tf_op jit(solution)/shard_map/ppermute | solution.py:762
  103.5 4.1 %up_product.1 = (f32[512,512]{1,0:T(8,128)}, f32[512,128]{1,0:T(8,128)}, f32[512,128]{1,0:T(8,128)}, f32[512,128]{1,0:T(8,128)}) custom-call(bf16[256,128]{1,0:T(8,128)(2,1)} %copy-done.10, bf16[256,128]{1,0:T(8,128)(2,1)} %copy-done.9, bf16[8,84,16,128]{3,2,1,0:T(8,128)(2,1)} %copy-done, bf16[512,128]{1,0:T(8,128)(2,1)} %get-tuple-element.36.cand_hbm, ...), custom_call_target="tpu_custom_call" | custom-call | tf_op jit(solution)/shard_map/up_product/pallas_call | solution.py:544
  107.6 1.4 %collective-permute-start.19 = (f32[512,128]{1,0:T(8,128)}, f32[512,128]{1,0:T(8,128)S(1)}, u32[]{:S(2)}, u32[]{:S(2)}) collective-permute-start(f32[512,128]{1,0:T(8,128)} %get-tuple-element.53.kv_hbm), channel_id=1, source_target_pairs={{0,1},{1,0},{2,3},{3,2},{4,5},{5,4},{6,7},{7,6},{8,9},{9,8},{10,11... | collective-permute-start | bytes 786440 | tf_op jit(solution)/shard_map/ppermute | solution.py:762
  109.1 1.6 %collective-permute-done.18.rx_hbm = f32[512,768]{1,0:T(8,128)} collective-permute-done((f32[512,768]{1,0:T(8,128)}, f32[512,768]{1,0:T(8,128)}, u32[]{:S(2)}, u32[]{:S(2)}) %collective-permute-start.18) | collective-permute-done | bytes 1572896 | tf_op jit(solution)/shard_map/ppermute | solution.py:762
  111.7 17.4 %attend.1 = (bf16[128,4,512]{2,1,0:T(4,128)(2,1)}, bf16[1024,16,128]{2,1,0:T(8,128)(2,1)}) custom-call(s32[32,128]{1,0:T(8,128)} %get-tuple-element.29.meta_ref.meta_hbm, s32[24,128]{1,0:T(8,128)} %get-tuple-element.33.lens_hbm, f32[512,512]{1,0:T(8,128)} %get-tuple-element.51.own_hbm, f32[512,768]{1,0:T(8,128)} %get-tuple-element.52.far_hbm, ...), custom_call_target="tpu_custom_call" | custom-call | tf_op jit(solution)/shard_map/attend/pallas_call | solution.py:724
  (54 shorter events, 8.6 us)
Async XLA Ops:
  0.6 47.8 %collective-permute-start.6 = (bf16[8192,512]{1,0:T(8,128)(2,1)}, bf16[8192,512]{1,0:T(8,128)(2,1)}, u32[]{:S(2)}, u32[]{:S(2)}) collective-permute-start(bf16[8192,512]{1,0:T(8,128)(2,1)} %refs_5_.3), channel_id=1, source_target_pairs={{0,1},{1,0},{2,3},{3,2},{4,5},{5,4},{6,7},{7,6},{8,9},{9,8},{10,11... | collective-permute-start | bytes 25165832 | tf_op jit(solution)/shard_map/ppermute | solution.py:762
  2.1 23.5 %collective-permute-start = (bf16[1024,16,128]{2,1,0:T(8,128)(2,1)}, bf16[1024,16,128]{2,1,0:T(8,128)(2,1)}, u32[]{:S(2)}, u32[]{:S(2)}) collective-permute-start(bf16[1024,16,128]{2,1,0:T(8,128)(2,1)} %pool_hbm.3), channel_id=1, source_target_pairs={{0,1},{1,0},{2,3},{3,2},{4,5},{5,4},{6,7},{7,6},{8,9},{9,8},{10,11... | collective-permute-start | bytes 12582920 | tf_op jit(solution)/shard_map/ppermute | solution.py:762
  2.2 42.4 %collective-permute-start.7 = (bf16[8192,128]{1,0:T(8,128)(2,1)}, bf16[8192,128]{1,0:T(8,128)(2,1)S(1)}, u32[]{:S(2)}, u32[]{:S(2)}) collective-permute-start(bf16[8192,128]{1,0:T(8,128)(2,1)} %refs_6_.3), channel_id=1, source_target_pairs={{0,1},{1,0},{2,3},{3,2},{4,5},{5,4},{6,7},{7,6},{8,9},{9,8},{10,11... | collective-permute-start | bytes 6291464 | tf_op jit(solution)/shard_map/ppermute | solution.py:762
  8.1 13.8 %all-to-all-start = ((bf16[8,32,640]{2,1,0:T(8,128)(2,1)}), bf16[8,32,640]{2,1,0:T(8,128)(2,1)S(1)}, u32[]{:S(2)}, u32[]{:S(2)}) async-start(bf16[8,32,640]{2,1,0:T(8,128)(2,1)} %bitcast.9), calls=%async_computation | async-start | bytes 655360 | tf_op jit(solution)/shard_map/all_to_all | solution.py:771
  21.9 3.7 %copy-start.5 = (bf16[8,32,640]{2,1,0:T(8,128)(2,1)}, bf16[8,32,640]{2,1,0:T(8,128)(2,1)S(1)}, u32[]{:S(2)}) copy-start(bf16[8,32,640]{2,1,0:T(8,128)(2,1)S(1)} %all-to-all-done) | copy-start | bytes 983044
  21.9 18.2 %all-to-all-start.1 = ((bf16[8,512,128]{2,1,0:T(8,128)(2,1)}), bf16[8,512,128]{2,1,0:T(8,128)(2,1)S(1)}, u32[]{:S(2)}, u32[]{:S(2)}) async-start(bf16[8,512,128]{2,1,0:T(8,128)(2,1)} %get-tuple-element.32.after_ref), calls=%async_computation.1 | async-start | bytes 2097152 | tf_op jit(solution)/shard_map/all_to_all | solution.py:771
  27.8 20.6 %collective-permute-start.5 = (bf16[512,512]{1,0:T(8,128)(2,1)}, bf16[512,512]{1,0:T(8,128)(2,1)}, u32[]{:S(2)}, u32[]{:S(2)}) collective-permute-start(bf16[512,512]{1,0:T(8,128)(2,1)} %get-tuple-element.35.x_hbm.refs_0_), channel_id=1, source_target_pairs={{0,12},{1,13},{2,14},{3,15},{4,0},{5,1},{6,2},{7,3},{8,4},{9,5},{1... | collective-permute-start | bytes 1572872 | tf_op jit(solution)/shard_map/ppermute | solution.py:768
  30.6 17.8 %collective-permute-start.4 = (bf16[512,512]{1,0:T(8,128)(2,1)}, bf16[512,512]{1,0:T(8,128)(2,1)}, u32[]{:S(2)}, u32[]{:S(2)}) collective-permute-start(bf16[512,512]{1,0:T(8,128)(2,1)} %get-tuple-element.35.x_hbm.refs_0_), channel_id=1, source_target_pairs={{0,4},{1,5},{2,6},{3,7},{4,8},{5,9},{6,10},{7,11},{8,12},{9,13},{1... | collective-permute-start | bytes 1572872 | tf_op jit(solution)/shard_map/ppermute | solution.py:768
  30.6 28.1 %collective-permute-start.3 = (bf16[512,512]{1,0:T(8,128)(2,1)}, bf16[512,512]{1,0:T(8,128)(2,1)}, u32[]{:S(2)}, u32[]{:S(2)}) collective-permute-start(bf16[512,512]{1,0:T(8,128)(2,1)} %get-tuple-element.35.x_hbm.refs_0_), channel_id=1, source_target_pairs={{0,2},{1,3},{2,0},{3,1},{4,6},{5,7},{6,4},{7,5},{8,10},{9,11},{10,... | collective-permute-start | bytes 1572872 | tf_op jit(solution)/shard_map/ppermute | solution.py:765
  40.1 1.0 copy-start.2
  44.7 3.8 %copy-start.1 = (bf16[8192,128]{1,0:T(8,128)(2,1)}, bf16[8192,128]{1,0:T(8,128)(2,1)S(1)}, u32[]{:S(2)}) copy-start(bf16[8192,128]{1,0:T(8,128)(2,1)S(1)} %collective-permute-done.7.refs_3_.refs_8_) | copy-start | bytes 6291460
  44.7 8.6 %copy-start.11 = (f32[256,128]{1,0:T(8,128)S(1)}, f32[256,128]{1,0:T(8,128)}, u32[]{:S(2)}) copy-start(f32[256,128]{1,0:T(8,128)} %get-tuple-element.37) | copy-start | bytes 393220
  44.7 8.6 %collective-permute-start.1 = (f32[256,128]{1,0:T(8,128)}, f32[256,128]{1,0:T(8,128)S(1)}, u32[]{:S(2)}, u32[]{:S(2)}) collective-permute-start(f32[256,128]{1,0:T(8,128)} %get-tuple-element.38), channel_id=1, source_target_pairs={{0,1},{1,0},{2,3},{3,2},{4,5},{5,4},{6,7},{7,6},{8,9},{9,8},{10,11... | collective-permute-start | bytes 393224 | tf_op jit(solution)/shard_map/ppermute | solution.py:762
  50.4 8.3 %collective-permute-start.8 = (bf16[256,512]{1,0:T(8,128)(2,1)}, bf16[256,512]{1,0:T(8,128)(2,1)}, u32[]{:S(2)}, u32[]{:S(2)}) collective-permute-start(bf16[256,512]{1,0:T(8,128)(2,1)} %get-tuple-element.39), channel_id=1, source_target_pairs={{0,4},{1,5},{2,6},{3,7},{4,8},{5,9},{6,10},{7,11},{8,12},{9,13},{1... | collective-permute-start | bytes 786440 | tf_op jit(solution)/shard_map/ppermute | solution.py:768
  51.7 7.0 %collective-permute-start.9 = (bf16[256,512]{1,0:T(8,128)(2,1)}, bf16[256,512]{1,0:T(8,128)(2,1)}, u32[]{:S(2)}, u32[]{:S(2)}) collective-permute-start(bf16[256,512]{1,0:T(8,128)(2,1)} %get-tuple-element.40), channel_id=1, source_target_pairs={{0,12},{1,13},{2,14},{3,15},{4,0},{5,1},{6,2},{7,3},{8,4},{9,5},{1... | collective-permute-start | bytes 786440 | tf_op jit(solution)/shard_map/ppermute | solution.py:768
  53.3 5.4 %collective-permute-start.2 = (f32[256,128]{1,0:T(8,128)S(1)}, f32[256,128]{1,0:T(8,128)S(1)}, u32[]{:S(2)}, u32[]{:S(2)}) collective-permute-start(f32[256,128]{1,0:T(8,128)S(1)} %add.15), channel_id=1, source_target_pairs={{0,2},{1,3},{2,0},{3,1},{4,6},{5,7},{6,4},{7,5},{8,10},{9,11},{10,... | collective-permute-start | bytes 393224 | tf_op jit(solution)/shard_map/ppermute | solution.py:765
  58.7 42.3 %all-to-all-start.2 = ((bf16[8,84,16,128]{3,2,1,0:T(8,128)(2,1)}), bf16[8,84,16,128]{3,2,1,0:T(8,128)(2,1)S(1)}, u32[]{:S(2)}, u32[]{:S(2)}) async-start(bf16[8,84,16,128]{3,2,1,0:T(8,128)(2,1)} %get-tuple-element.42), calls=%async_computation.2 | async-start | bytes 5505024 | tf_op jit(solution)/shard_map/all_to_all | solution.py:771
  62.4 13.8 %collective-permute-start.15 = (bf16[512,512]{1,0:T(8,128)(2,1)}, bf16[512,512]{1,0:T(8,128)(2,1)S(1)}, u32[]{:S(2)}, u32[]{:S(2)}) collective-permute-start(bf16[512,512]{1,0:T(8,128)(2,1)} %collective-permute-done.3.refs_0_), channel_id=1, source_target_pairs={{0,12},{1,13},{2,14},{3,15},{4,0},{5,1},{6,2},{7,3},{8,4},{9,5},{1... | collective-permute-start | bytes 1572872 | tf_op jit(solution)/shard_map/ppermute | solution.py:768
  65.0 12.3 %collective-permute-start.14 = (bf16[512,512]{1,0:T(8,128)(2,1)}, bf16[512,512]{1,0:T(8,128)(2,1)S(1)}, u32[]{:S(2)}, u32[]{:S(2)}) collective-permute-start(bf16[512,512]{1,0:T(8,128)(2,1)} %collective-permute-done.3.refs_0_), channel_id=1, source_target_pairs={{0,4},{1,5},{2,6},{3,7},{4,8},{5,9},{6,10},{7,11},{8,12},{9,13},{1... | collective-permute-start | bytes 1572872 | tf_op jit(solution)/shard_map/ppermute | solution.py:768
  65.0 17.7 %collective-permute-start.12 = (f32[256,128]{1,0:T(8,128)S(1)}, f32[256,128]{1,0:T(8,128)S(1)}, u32[]{:S(2)}, u32[]{:S(2)}) collective-permute-start(f32[256,128]{1,0:T(8,128)S(1)} %add.16), channel_id=1, source_target_pairs={{0,12},{1,13},{2,14},{3,15},{4,0},{5,1},{6,2},{7,3},{8,4},{9,5},{1... | collective-permute-start | bytes 393224 | tf_op jit(solution)/shard_map/ppermute | solution.py:768
  67.6 15.0 %collective-permute-start.11 = (f32[256,128]{1,0:T(8,128)S(1)}, f32[256,128]{1,0:T(8,128)}, u32[]{:S(2)}, u32[]{:S(2)}) collective-permute-start(f32[256,128]{1,0:T(8,128)S(1)} %add.16), channel_id=1, source_target_pairs={{0,4},{1,5},{2,6},{3,7},{4,8},{5,9},{6,10},{7,11},{8,12},{9,13},{1... | collective-permute-start | bytes 393224 | tf_op jit(solution)/shard_map/ppermute | solution.py:768
  67.6 15.0 %collective-permute-start.10 = (f32[256,128]{1,0:T(8,128)S(1)}, f32[256,128]{1,0:T(8,128)}, u32[]{:S(2)}, u32[]{:S(2)}) collective-permute-start(f32[256,128]{1,0:T(8,128)S(1)} %add.16), channel_id=1, source_target_pairs={{0,8},{1,9},{2,10},{3,11},{4,12},{5,13},{6,14},{7,15},{8,0},{9,1},... | collective-permute-start | bytes 393224 | tf_op jit(solution)/shard_map/ppermute | solution.py:768
  76.2 1.1 copy-start.3
  79.9 11.8 %collective-permute-start.16 = (bf16[256,512]{1,0:T(8,128)(2,1)}, bf16[256,512]{1,0:T(8,128)(2,1)S(1)}, u32[]{:S(2)}, u32[]{:S(2)}) collective-permute-start(bf16[256,512]{1,0:T(8,128)(2,1)} %get-tuple-element.44), channel_id=1, source_target_pairs={{0,4},{1,5},{2,6},{3,7},{4,8},{5,9},{6,10},{7,11},{8,12},{9,13},{1... | collective-permute-start | bytes 786440 | tf_op jit(solution)/shard_map/ppermute | solution.py:768
  81.1 10.6 %collective-permute-start.17 = (bf16[256,512]{1,0:T(8,128)(2,1)}, bf16[256,512]{1,0:T(8,128)(2,1)S(1)}, u32[]{:S(2)}, u32[]{:S(2)}) collective-permute-start(bf16[256,512]{1,0:T(8,128)(2,1)} %get-tuple-element.45), channel_id=1, source_target_pairs={{0,12},{1,13},{2,14},{3,15},{4,0},{5,1},{6,2},{7,3},{8,4},{9,5},{1... | collective-permute-start | bytes 786440 | tf_op jit(solution)/shard_map/ppermute | solution.py:768
  83.7 17.3 %copy-start.10 = (bf16[256,128]{1,0:T(8,128)(2,1)}, bf16[256,128]{1,0:T(8,128)(2,1)S(1)}, u32[]{:S(2)}) copy-start(bf16[256,128]{1,0:T(8,128)(2,1)S(1)} %add_convert_fusion.mine_hbm) | copy-start | bytes 196612
  83.7 8.0 %collective-permute-start.13 = (bf16[256,128]{1,0:T(8,128)(2,1)S(1)}, bf16[256,128]{1,0:T(8,128)(2,1)S(1)}, u32[]{:S(2)}, u32[]{:S(2)}) collective-permute-start(bf16[256,128]{1,0:T(8,128)(2,1)S(1)} %add_convert_fusion.mine_hbm), channel_id=1, source_target_pairs={{0,1},{1,0},{2,3},{3,2},{4,5},{5,4},{6,7},{7,6},{8,9},{9,8},{10,11... | collective-permute-start | bytes 196616 | tf_op jit(solution)/shard_map/ppermute | solution.py:762
  91.7 0.8 copy-start.7
  101.0 2.5 %copy-start = (bf16[8,84,16,128]{3,2,1,0:T(8,128)(2,1)}, bf16[8,84,16,128]{3,2,1,0:T(8,128)(2,1)S(1)}, u32[]{:S(2)}) copy-start(bf16[8,84,16,128]{3,2,1,0:T(8,128)(2,1)S(1)} %all-to-all-done.2.far_hbm.got_hbm) | copy-start | bytes 8257540
  101.0 10.0 %collective-permute-start.20 = (bf16[8,84,16,128]{3,2,1,0:T(8,128)(2,1)S(1)}, bf16[8,84,16,128]{3,2,1,0:T(8,128)(2,1)}, u32[]{:S(2)}, u32[]{:S(2)}) collective-permute-start(bf16[8,84,16,128]{3,2,1,0:T(8,128)(2,1)S(1)} %all-to-all-done.2.far_hbm.got_hbm), channel_id=1, source_target_pairs={{0,1},{1,0},{2,3},{3,2},{4,5},{5,4},{6,7},{7,6},{8,9},{9,8},{10,11... | collective-permute-start | bytes 8257544 | tf_op jit(solution)/shard_map/ppermute | solution.py:762
  103.4 7.2 %collective-permute-start.18 = (f32[512,768]{1,0:T(8,128)}, f32[512,768]{1,0:T(8,128)}, u32[]{:S(2)}, u32[]{:S(2)}) collective-permute-start(f32[512,768]{1,0:T(8,128)} %get-tuple-element.52.far_hbm), channel_id=1, source_target_pairs={{0,1},{1,0},{2,3},{3,2},{4,5},{5,4},{6,7},{7,6},{8,9},{9,8},{10,11... | collective-permute-start | bytes 4718600 | tf_op jit(solution)/shard_map/ppermute | solution.py:762
  107.6 3.4 %collective-permute-start.19 = (f32[512,128]{1,0:T(8,128)}, f32[512,128]{1,0:T(8,128)S(1)}, u32[]{:S(2)}, u32[]{:S(2)}) collective-permute-start(f32[512,128]{1,0:T(8,128)} %get-tuple-element.53.kv_hbm), channel_id=1, source_target_pairs={{0,1},{1,0},{2,3},{3,2},{4,5},{5,4},{6,7},{7,6},{8,9},{9,8},{10,11... | collective-permute-start | bytes 786440 | tf_op jit(solution)/shard_map/ppermute | solution.py:762
  (4 other events, 2.9 us)

commit v5 on v4

--- a/solution.py
+++ b/solution.py
@@ -123,7 +123,8 @@
 
     len_col = jnp.broadcast_to(row_to_col(len_ref[...], rows, 4), (rows, HEAD))
     settle(loads[6:])
-    tok = jnp.concatenate([tok_ref[...], len_col.astype(F32).astype(BF16)], axis=1)
+    tok3 = tok_ref[...]
+    tok = jnp.concatenate([tok3.reshape(rows, tok3.shape[2]), len_col.astype(F32).astype(BF16)], axis=1)
 
     def rows_of(row, n):
         base = row_to_col(row, n, 4)
@@ -188,7 +189,7 @@
 
 
 def plan(mig, sra, ssa, lengths, prev, moved, tok):
-    rows = tok.shape[0]
+    rows = tok.shape[0] * tok.shape[1]
     ins = (mig, sra, ssa, lengths, prev, moved, tok)
     outs = (
         sds((rows // 2, 640), BF16),
@@ -773,7 +774,7 @@
     send, own, cand, meta = plan(
         migration.reshape(8, 128), slot_request_adapter.reshape(8, 128),
         storage_slot_adapter.reshape(1, 64), lengths.reshape(1, 128),
-        previous_block_table.T, moved_block_table.T, tokens.reshape(512, 512),
+        previous_block_table.T, moved_block_table.T, tokens,
     )
     packed, leaving = pack(
         meta, adapter_down_factors, adapter_up_query, adapter_up_key_value, paged_cache_pool

time: 130 us -> 128 us (0.985)
  local copies, waits for them, and re-layouts: 5.27 us -> 3.32 us
    reshape x1 -> x0, local copies, waits for them, and re-layouts: 1.96 us -> none  [body(): tokens.reshape(512, 512)]
  transfers between devices with their start and end apart: 24 -> 24, of which waited for: 7 -> 8; matrix products, arithmetic and copies ran while one was open for 2% -> 1% of each run, Pallas kernels for 30% -> 31%
where the time goes in v5:
time: 128 us; the launch traced here: 127 us
  Pallas kernels  56.4 us (44%)
  starting transfers between devices  50.5 us (39%)
  waiting for transfers between devices  15 us (12%)
  local copies, waits for them, and re-layouts  3.32 us (3%)
    pallas_call x1, Pallas kernels, attend(): pl.pallas_call(attend_kernel, out_shape=outs, in_specs=[hspec()] * 13, ou...  17.4 us
    ppermute x8, starting transfers between devices, other_core(): return lax.ppermute(a, 'tp', [(i, i ^ 1) for i in range(16)])  16.8 us
    pallas_call x2, Pallas kernels, matmul(): pl.pallas_call(functools.partial(matmul_kernel, blocks, offsets, min(chun...  15.8 us
    ppermute x11, starting transfers between devices, along_y(): return lax.ppermute(a, 'tp', [(i, (i + 4 * d) % 16) for i in range(16)])  15 us
    all_to_all x3, starting transfers between devices, swap_rep(): return lax.all_to_all(a, 'rep', split_axis=0, concat_axis=0, tiled=True)  13.4 us
    all_to_all x3, waiting for transfers between devices, swap_rep(): return lax.all_to_all(a, 'rep', split_axis=0, concat_axis=0, tiled=True)  7.55 us
    pallas_call x1, Pallas kernels, pack(): pl.pallas_call(pack_kernel, out_shape=(sds(down.shape, BF16), rest), in_s...  6.27 us
    ppermute x2, starting transfers between devices, other_x(): return lax.ppermute(a, 'tp', [(i, i ^ 2) for i in range(16)])  5.27 us
  transfers between devices with their start and end apart: 24, of which 8 were waited for; matrix products, arithmetic and copies ran while one was open for 1% of the time, Pallas kernels for 31%

profile of v5, /device:TPU:1, one launch (start us, length us, event | category | flops | bytes accessed | tf_op | source)
XLA Modules:
  0.0 127.2 jit_solution(3375096366568876948)
XLA Ops:
  0.6 1.5 %collective-permute-start.6 = (bf16[8192,512]{1,0:T(8,128)(2,1)}, bf16[8192,512]{1,0:T(8,128)(2,1)}, u32[]{:S(2)}, u32[]{:S(2)}) collective-permute-start(bf16[8192,512]{1,0:T(8,128)(2,1)} %refs_5_.3), channel_id=1, source_target_pairs={{0,1},{1,0},{2,3},{3,2},{4,5},{5,4},{6,7},{7,6},{8,9},{9,8},{10,11... | collective-permute-start | bytes 25165832 | tf_op jit(solution)/shard_map/ppermute | solution.py:763
  2.6 3.5 %plan.1 = (bf16[256,640]{1,0:T(8,128)(2,1)}, bf16[512,640]{1,0:T(8,128)(2,1)}, bf16[512,128]{1,0:T(8,128)(2,1)}, s32[32,128]{1,0:T(8,128)}) custom-call(s32[8,128]{1,0:T(8,128)} %bitcast.10, s32[8,128]{1,0:T(8,128)} %bitcast.11, s32[1,64]{1,0:T(1,128)} %bitcast.14, s32[1,128]{1,0:T(1,128)} %bitcast.15, s32[8,128]{1,0:T(8,128)} %bitcast.12, ...), custom_call_target="tpu_custom_call" | custom-call | tf_op jit(solution)/shard_map/plan/pallas_call | solution.py:200
  6.1 6.1 %all-to-all-start = ((bf16[8,32,640]{2,1,0:T(8,128)(2,1)}), bf16[8,32,640]{2,1,0:T(8,128)(2,1)S(1)}, u32[]{:S(2)}, u32[]{:S(2)}) async-start(bf16[8,32,640]{2,1,0:T(8,128)(2,1)} %bitcast.9), calls=%async_computation | async-start | bytes 655360 | tf_op jit(solution)/shard_map/all_to_all | solution.py:772
  12.2 6.3 %pack.1 = (bf16[8,512,128]{2,1,0:T(8,128)(2,1)}, bf16[8,84,16,128]{3,2,1,0:T(8,128)(2,1)}) custom-call(s32[32,128]{1,0:T(8,128)} %get-tuple-element.29.meta_ref.meta_hbm, bf16[8,512,128]{2,1,0:T(8,128)(2,1)} %here_hbm.1, bf16[8,64,512]{2,1,0:T(8,128)(2,1)} %q_hbm.3, bf16[8,64,128]{2,1,0:T(8,128)(2,1)} %k_hbm.3, bf16[1024,16,128]{2,1,0:T(8,128)(2,1)} %pool_hbm.3), custom_call_target="tpu_custom_call" | custom-call | tf_op jit(solution)/shard_map/pack/pallas_call | solution.py:241
  18.5 1.5 %all-to-all-done = bf16[8,32,640]{2,1,0:T(8,128)(2,1)S(1)} async-done(((bf16[8,32,640]{2,1,0:T(8,128)(2,1)}), bf16[8,32,640]{2,1,0:T(8,128)(2,1)S(1)}, u32[]{:S(2)}, u32[]{:S(2)}) %all-to-all-start) | async-done | bytes 327712 | tf_op jit(solution)/shard_map/all_to_all | solution.py:772
  19.9 3.7 %all-to-all-start.1 = ((bf16[8,512,128]{2,1,0:T(8,128)(2,1)}), bf16[8,512,128]{2,1,0:T(8,128)(2,1)S(1)}, u32[]{:S(2)}, u32[]{:S(2)}) async-start(bf16[8,512,128]{2,1,0:T(8,128)(2,1)} %get-tuple-element.32.after_ref), calls=%async_computation.1 | async-start | bytes 2097152 | tf_op jit(solution)/shard_map/all_to_all | solution.py:772
  24.3 2.1 %join.1 = (bf16[512,512]{1,0:T(8,128)(2,1)}, f32[512,128]{1,0:T(8,128)}, s32[24,128]{1,0:T(8,128)}) custom-call(bf16[512,640]{1,0:T(8,128)(2,1)} %get-tuple-element.30.own_hbm, bf16[256,640]{1,0:T(8,128)(2,1)} %bitcast.8, s32[32,128]{1,0:T(8,128)} %get-tuple-element.29.meta_ref.meta_hbm, bf16[8,512,128]{2,1,0:T(8,128)(2,1)} %get-tuple-element.32.after_ref, ...), custom_call_target="tpu_custom_call" | custom-call | tf_op jit(solution)/shard_map/join/pallas_call | solution.py:280
  26.4 2.9 %collective-permute-start.5 = (bf16[512,512]{1,0:T(8,128)(2,1)}, bf16[512,512]{1,0:T(8,128)(2,1)}, u32[]{:S(2)}, u32[]{:S(2)}) collective-permute-start(bf16[512,512]{1,0:T(8,128)(2,1)} %get-tuple-element.35.x_hbm.refs_0_), channel_id=1, source_target_pairs={{0,12},{1,13},{2,14},{3,15},{4,0},{5,1},{6,2},{7,3},{8,4},{9,5},{1... | collective-permute-start | bytes 1572872 | tf_op jit(solution)/shard_map/ppermute | solution.py:769
  29.3 2.7 %collective-permute-start.3 = (bf16[512,512]{1,0:T(8,128)(2,1)}, bf16[512,512]{1,0:T(8,128)(2,1)}, u32[]{:S(2)}, u32[]{:S(2)}) collective-permute-start(bf16[512,512]{1,0:T(8,128)(2,1)} %get-tuple-element.35.x_hbm.refs_0_), channel_id=1, source_target_pairs={{0,2},{1,3},{2,0},{3,1},{4,6},{5,7},{6,4},{7,5},{8,10},{9,11},{10,... | collective-permute-start | bytes 1572872 | tf_op jit(solution)/shard_map/ppermute | solution.py:766
  32.0 6.1 %all-to-all-done.1.far_hbm = bf16[8,512,128]{2,1,0:T(8,128)(2,1)S(1)} async-done(((bf16[8,512,128]{2,1,0:T(8,128)(2,1)}), bf16[8,512,128]{2,1,0:T(8,128)(2,1)S(1)}, u32[]{:S(2)}, u32[]{:S(2)}) %all-to-all-start.1) | async-done | bytes 1048608 | tf_op jit(solution)/shard_map/all_to_all | solution.py:772
  39.1 3.6 %down_product.1 = (f32[256,128]{1,0:T(8,128)}, f32[256,128]{1,0:T(8,128)}) custom-call(bf16[512,512]{1,0:T(8,128)(2,1)} %get-tuple-element.35.x_hbm.refs_0_, bf16[8,512,128]{2,1,0:T(8,128)(2,1)} %here_hbm.1, bf16[8,512,128]{2,1,0:T(8,128)(2,1)} %copy-done.2, bf16[512,128]{1,0:T(8,128)(2,1)} %get-tuple-element.36.cand_hbm), custom_call_target="tpu_custom_call" | custom-call | tf_op jit(solution)/shard_map/down_product/pallas_call | solution.py:443
  42.7 3.8 %collective-permute-start.1 = (f32[256,128]{1,0:T(8,128)}, f32[256,128]{1,0:T(8,128)S(1)}, u32[]{:S(2)}, u32[]{:S(2)}) collective-permute-start(f32[256,128]{1,0:T(8,128)} %get-tuple-element.38), channel_id=1, source_target_pairs={{0,1},{1,0},{2,3},{3,2},{4,5},{5,4},{6,7},{7,6},{8,9},{9,8},{10,11... | collective-permute-start | bytes 393224 | tf_op jit(solution)/shard_map/ppermute | solution.py:763
  46.5 1.9 %slices.2 = (bf16[256,512]{1,0:T(8,128)(2,1)}, bf16[256,512]{1,0:T(8,128)(2,1)}) custom-call(bf16[512,512]{1,0:T(8,128)(2,1)} %collective-permute-done.4.refs_0_.refs_1_, bf16[512,512]{1,0:T(8,128)(2,1)} %collective-permute-done.5.refs_1_.refs_2_, bf16[8192,512]{1,0:T(8,128)(2,1)} %collective-permute-done.6.refs_2_.refs_7_, bf16[8192,128]{1,0:T(8,128)(2,1)} %copy-done.1), custom_call_target="tpu_custom_call" | custom-call | tf_op jit(solution)/shard_map/slices/pallas_call | solution.py:312
  48.4 1.4 %collective-permute-start.8 = (bf16[256,512]{1,0:T(8,128)(2,1)}, bf16[256,512]{1,0:T(8,128)(2,1)}, u32[]{:S(2)}, u32[]{:S(2)}) collective-permute-start(bf16[256,512]{1,0:T(8,128)(2,1)} %get-tuple-element.39), channel_id=1, source_target_pairs={{0,4},{1,5},{2,6},{3,7},{4,8},{5,9},{6,10},{7,11},{8,12},{9,13},{1... | collective-permute-start | bytes 786440 | tf_op jit(solution)/shard_map/ppermute | solution.py:769
  49.7 1.5 %collective-permute-start.9 = (bf16[256,512]{1,0:T(8,128)(2,1)}, bf16[256,512]{1,0:T(8,128)(2,1)}, u32[]{:S(2)}, u32[]{:S(2)}) collective-permute-start(bf16[256,512]{1,0:T(8,128)(2,1)} %get-tuple-element.40), channel_id=1, source_target_pairs={{0,12},{1,13},{2,14},{3,15},{4,0},{5,1},{6,2},{7,3},{8,4},{9,5},{1... | collective-permute-start | bytes 786440 | tf_op jit(solution)/shard_map/ppermute | solution.py:769
  51.3 2.5 %collective-permute-start.2 = (f32[256,128]{1,0:T(8,128)S(1)}, f32[256,128]{1,0:T(8,128)S(1)}, u32[]{:S(2)}, u32[]{:S(2)}) collective-permute-start(f32[256,128]{1,0:T(8,128)S(1)} %add.15), channel_id=1, source_target_pairs={{0,2},{1,3},{2,0},{3,1},{4,6},{5,7},{6,4},{7,5},{8,10},{9,11},{10,... | collective-permute-start | bytes 393224 | tf_op jit(solution)/shard_map/ppermute | solution.py:766
  53.8 2.9 %collective-permute-done.2 = f32[256,128]{1,0:T(8,128)S(1)} collective-permute-done((f32[256,128]{1,0:T(8,128)S(1)}, f32[256,128]{1,0:T(8,128)S(1)}, u32[]{:S(2)}, u32[]{:S(2)}) %collective-permute-start.2) | collective-permute-done | bytes 131104 | tf_op jit(solution)/shard_map/ppermute | solution.py:766
  56.7 3.6 %all-to-all-start.2 = ((bf16[8,84,16,128]{3,2,1,0:T(8,128)(2,1)}), bf16[8,84,16,128]{3,2,1,0:T(8,128)(2,1)S(1)}, u32[]{:S(2)}, u32[]{:S(2)}) async-start(bf16[8,84,16,128]{3,2,1,0:T(8,128)(2,1)} %get-tuple-element.42), calls=%async_computation.2 | async-start | bytes 5505024 | tf_op jit(solution)/shard_map/all_to_all | solution.py:772
  60.4 2.6 %collective-permute-start.15 = (bf16[512,512]{1,0:T(8,128)(2,1)}, bf16[512,512]{1,0:T(8,128)(2,1)S(1)}, u32[]{:S(2)}, u32[]{:S(2)}) collective-permute-start(bf16[512,512]{1,0:T(8,128)(2,1)} %collective-permute-done.3.refs_0_), channel_id=1, source_target_pairs={{0,12},{1,13},{2,14},{3,15},{4,0},{5,1},{6,2},{7,3},{8,4},{9,5},{1... | collective-permute-start | bytes 1572872 | tf_op jit(solution)/shard_map/ppermute | solution.py:769
  63.0 2.7 %collective-permute-start.12 = (f32[256,128]{1,0:T(8,128)S(1)}, f32[256,128]{1,0:T(8,128)S(1)}, u32[]{:S(2)}, u32[]{:S(2)}) collective-permute-start(f32[256,128]{1,0:T(8,128)S(1)} %add.16), channel_id=1, source_target_pairs={{0,12},{1,13},{2,14},{3,15},{4,0},{5,1},{6,2},{7,3},{8,4},{9,5},{1... | collective-permute-start | bytes 393224 | tf_op jit(solution)/shard_map/ppermute | solution.py:769
  65.6 1.2 collective-permute-start.10
  66.8 7.3 %matmul_far_own.2 = (f32[512,768]{1,0:T(8,128)}, f32[512,512]{1,0:T(8,128)}) custom-call(bf16[512,512]{1,0:T(8,128)(2,1)} %get-tuple-element.35.x_hbm.refs_0_, bf16[512,512]{1,0:T(8,128)(2,1)} %collective-permute-done.4.refs_0_.refs_1_, bf16[512,512]{1,0:T(8,128)(2,1)} %collective-permute-done.5.refs_1_.refs_2_, ...), custom_call_target="tpu_custom_call" | custom-call | tf_op jit(solution)/shard_map/matmul_far_own/pallas_call | solution.py:391
  76.1 1.8 %slices.3 = (bf16[256,512]{1,0:T(8,128)(2,1)}, bf16[256,512]{1,0:T(8,128)(2,1)}) custom-call(bf16[512,512]{1,0:T(8,128)(2,1)} %copy-done.4, bf16[512,512]{1,0:T(8,128)(2,1)} %copy-done.3, f32[512,768]{1,0:T(8,128)} %get-tuple-element.43.refs_2_.refs_9_), custom_call_target="tpu_custom_call" | custom-call | tf_op jit(solution)/shard_map/slices/pallas_call | solution.py:312
  77.9 1.2 collective-permute-start.16
  79.1 1.5 %collective-permute-start.17 = (bf16[256,512]{1,0:T(8,128)(2,1)}, bf16[256,512]{1,0:T(8,128)(2,1)S(1)}, u32[]{:S(2)}, u32[]{:S(2)}) collective-permute-start(bf16[256,512]{1,0:T(8,128)(2,1)} %get-tuple-element.45), channel_id=1, source_target_pairs={{0,12},{1,13},{2,14},{3,15},{4,0},{5,1},{6,2},{7,3},{8,4},{9,5},{1... | collective-permute-start | bytes 786440 | tf_op jit(solution)/shard_map/ppermute | solution.py:769
  81.7 7.1 %collective-permute-start.13 = (bf16[256,128]{1,0:T(8,128)(2,1)S(1)}, bf16[256,128]{1,0:T(8,128)(2,1)S(1)}, u32[]{:S(2)}, u32[]{:S(2)}) collective-permute-start(bf16[256,128]{1,0:T(8,128)(2,1)S(1)} %add_convert_fusion.mine_hbm), channel_id=1, source_target_pairs={{0,1},{1,0},{2,3},{3,2},{4,5},{5,4},{6,7},{7,6},{8,9},{9,8},{10,11... | collective-permute-start | bytes 196616 | tf_op jit(solution)/shard_map/ppermute | solution.py:763
  90.5 8.5 %matmul_far_own.3 = (f32[512,768]{1,0:T(8,128)}, f32[512,512]{1,0:T(8,128)}) custom-call(bf16[512,512]{1,0:T(8,128)(2,1)} %collective-permute-done.3.refs_0_, bf16[512,512]{1,0:T(8,128)(2,1)} %copy-done.4, bf16[512,512]{1,0:T(8,128)(2,1)} %copy-done.3, bf16[256,512]{1,0:T(8,128)(2,1)} %copy-done.6, bf16[256,512]{1,0:T(8,128)(2,1)} %copy-done.7, ...), custom_call_target="tpu_custom_call" | custom-call | tf_op jit(solution)/shard_map/matmul_far_own/pallas_call | solution.py:391
  99.0 2.4 %collective-permute-start.20 = (bf16[8,84,16,128]{3,2,1,0:T(8,128)(2,1)S(1)}, bf16[8,84,16,128]{3,2,1,0:T(8,128)(2,1)}, u32[]{:S(2)}, u32[]{:S(2)}) collective-permute-start(bf16[8,84,16,128]{3,2,1,0:T(8,128)(2,1)S(1)} %all-to-all-done.2.far_hbm.got_hbm), channel_id=1, source_target_pairs={{0,1},{1,0},{2,3},{3,2},{4,5},{5,4},{6,7},{7,6},{8,9},{9,8},{10,11... | collective-permute-start | bytes 8257544 | tf_op jit(solution)/shard_map/ppermute | solution.py:763
  101.5 4.1 %up_product.1 = (f32[512,512]{1,0:T(8,128)}, f32[512,128]{1,0:T(8,128)}, f32[512,128]{1,0:T(8,128)}, f32[512,128]{1,0:T(8,128)}) custom-call(bf16[256,128]{1,0:T(8,128)(2,1)} %copy-done.10, bf16[256,128]{1,0:T(8,128)(2,1)} %copy-done.9, bf16[8,84,16,128]{3,2,1,0:T(8,128)(2,1)} %copy-done, bf16[512,128]{1,0:T(8,128)(2,1)} %get-tuple-element.36.cand_hbm, ...), custom_call_target="tpu_custom_call" | custom-call | tf_op jit(solution)/shard_map/up_product/pallas_call | solution.py:545
  105.6 1.4 %collective-permute-start.19 = (f32[512,128]{1,0:T(8,128)}, f32[512,128]{1,0:T(8,128)S(1)}, u32[]{:S(2)}, u32[]{:S(2)}) collective-permute-start(f32[512,128]{1,0:T(8,128)} %get-tuple-element.53.kv_hbm), channel_id=1, source_target_pairs={{0,1},{1,0},{2,3},{3,2},{4,5},{5,4},{6,7},{7,6},{8,9},{9,8},{10,11... | collective-permute-start | bytes 786440 | tf_op jit(solution)/shard_map/ppermute | solution.py:763
  107.1 1.6 %collective-permute-done.18.rx_hbm = f32[512,768]{1,0:T(8,128)} collective-permute-done((f32[512,768]{1,0:T(8,128)}, f32[512,768]{1,0:T(8,128)}, u32[]{:S(2)}, u32[]{:S(2)}) %collective-permute-start.18) | collective-permute-done | bytes 1572896 | tf_op jit(solution)/shard_map/ppermute | solution.py:763
  109.7 17.4 %attend.1 = (bf16[128,4,512]{2,1,0:T(4,128)(2,1)}, bf16[1024,16,128]{2,1,0:T(8,128)(2,1)}) custom-call(s32[32,128]{1,0:T(8,128)} %get-tuple-element.29.meta_ref.meta_hbm, s32[24,128]{1,0:T(8,128)} %get-tuple-element.33.lens_hbm, f32[512,512]{1,0:T(8,128)} %get-tuple-element.51.own_hbm, f32[512,768]{1,0:T(8,128)} %get-tuple-element.52.far_hbm, ...), custom_call_target="tpu_custom_call" | custom-call | tf_op jit(solution)/shard_map/attend/pallas_call | solution.py:725
  (53 shorter events, 8.0 us)
Async XLA Ops:
  0.6 45.8 %collective-permute-start.6 = (bf16[8192,512]{1,0:T(8,128)(2,1)}, bf16[8192,512]{1,0:T(8,128)(2,1)}, u32[]{:S(2)}, u32[]{:S(2)}) collective-permute-start(bf16[8192,512]{1,0:T(8,128)(2,1)} %refs_5_.3), channel_id=1, source_target_pairs={{0,1},{1,0},{2,3},{3,2},{4,5},{5,4},{6,7},{7,6},{8,9},{9,8},{10,11... | collective-permute-start | bytes 25165832 | tf_op jit(solution)/shard_map/ppermute | solution.py:763
  2.1 22.1 %collective-permute-start = (bf16[1024,16,128]{2,1,0:T(8,128)(2,1)}, bf16[1024,16,128]{2,1,0:T(8,128)(2,1)}, u32[]{:S(2)}, u32[]{:S(2)}) collective-permute-start(bf16[1024,16,128]{2,1,0:T(8,128)(2,1)} %pool_hbm.3), channel_id=1, source_target_pairs={{0,1},{1,0},{2,3},{3,2},{4,5},{5,4},{6,7},{7,6},{8,9},{9,8},{10,11... | collective-permute-start | bytes 12582920 | tf_op jit(solution)/shard_map/ppermute | solution.py:763
  2.2 40.4 %collective-permute-start.7 = (bf16[8192,128]{1,0:T(8,128)(2,1)}, bf16[8192,128]{1,0:T(8,128)(2,1)S(1)}, u32[]{:S(2)}, u32[]{:S(2)}) collective-permute-start(bf16[8192,128]{1,0:T(8,128)(2,1)} %refs_6_.3), channel_id=1, source_target_pairs={{0,1},{1,0},{2,3},{3,2},{4,5},{5,4},{6,7},{7,6},{8,9},{9,8},{10,11... | collective-permute-start | bytes 6291464 | tf_op jit(solution)/shard_map/ppermute | solution.py:763
  6.1 13.8 %all-to-all-start = ((bf16[8,32,640]{2,1,0:T(8,128)(2,1)}), bf16[8,32,640]{2,1,0:T(8,128)(2,1)S(1)}, u32[]{:S(2)}, u32[]{:S(2)}) async-start(bf16[8,32,640]{2,1,0:T(8,128)(2,1)} %bitcast.9), calls=%async_computation | async-start | bytes 655360 | tf_op jit(solution)/shard_map/all_to_all | solution.py:772
  19.9 4.3 %copy-start.5 = (bf16[8,32,640]{2,1,0:T(8,128)(2,1)}, bf16[8,32,640]{2,1,0:T(8,128)(2,1)S(1)}, u32[]{:S(2)}) copy-start(bf16[8,32,640]{2,1,0:T(8,128)(2,1)S(1)} %all-to-all-done) | copy-start | bytes 983044
  19.9 18.2 %all-to-all-start.1 = ((bf16[8,512,128]{2,1,0:T(8,128)(2,1)}), bf16[8,512,128]{2,1,0:T(8,128)(2,1)S(1)}, u32[]{:S(2)}, u32[]{:S(2)}) async-start(bf16[8,512,128]{2,1,0:T(8,128)(2,1)} %get-tuple-element.32.after_ref), calls=%async_computation.1 | async-start | bytes 2097152 | tf_op jit(solution)/shard_map/all_to_all | solution.py:772
  26.4 20.1 %collective-permute-start.5 = (bf16[512,512]{1,0:T(8,128)(2,1)}, bf16[512,512]{1,0:T(8,128)(2,1)}, u32[]{:S(2)}, u32[]{:S(2)}) collective-permute-start(bf16[512,512]{1,0:T(8,128)(2,1)} %get-tuple-element.35.x_hbm.refs_0_), channel_id=1, source_target_pairs={{0,12},{1,13},{2,14},{3,15},{4,0},{5,1},{6,2},{7,3},{8,4},{9,5},{1... | collective-permute-start | bytes 1572872 | tf_op jit(solution)/shard_map/ppermute | solution.py:769
  29.3 17.2 %collective-permute-start.4 = (bf16[512,512]{1,0:T(8,128)(2,1)}, bf16[512,512]{1,0:T(8,128)(2,1)}, u32[]{:S(2)}, u32[]{:S(2)}) collective-permute-start(bf16[512,512]{1,0:T(8,128)(2,1)} %get-tuple-element.35.x_hbm.refs_0_), channel_id=1, source_target_pairs={{0,4},{1,5},{2,6},{3,7},{4,8},{5,9},{6,10},{7,11},{8,12},{9,13},{1... | collective-permute-start | bytes 1572872 | tf_op jit(solution)/shard_map/ppermute | solution.py:769
  29.3 27.4 %collective-permute-start.3 = (bf16[512,512]{1,0:T(8,128)(2,1)}, bf16[512,512]{1,0:T(8,128)(2,1)}, u32[]{:S(2)}, u32[]{:S(2)}) collective-permute-start(bf16[512,512]{1,0:T(8,128)(2,1)} %get-tuple-element.35.x_hbm.refs_0_), channel_id=1, source_target_pairs={{0,2},{1,3},{2,0},{3,1},{4,6},{5,7},{6,4},{7,5},{8,10},{9,11},{10,... | collective-permute-start | bytes 1572872 | tf_op jit(solution)/shard_map/ppermute | solution.py:766
  38.1 1.0 copy-start.2
  42.7 3.8 %copy-start.1 = (bf16[8192,128]{1,0:T(8,128)(2,1)}, bf16[8192,128]{1,0:T(8,128)(2,1)S(1)}, u32[]{:S(2)}) copy-start(bf16[8192,128]{1,0:T(8,128)(2,1)S(1)} %collective-permute-done.7.refs_3_.refs_8_) | copy-start | bytes 6291460
  42.7 8.6 %copy-start.11 = (f32[256,128]{1,0:T(8,128)S(1)}, f32[256,128]{1,0:T(8,128)}, u32[]{:S(2)}) copy-start(f32[256,128]{1,0:T(8,128)} %get-tuple-element.37) | copy-start | bytes 393220
  42.7 8.6 %collective-permute-start.1 = (f32[256,128]{1,0:T(8,128)}, f32[256,128]{1,0:T(8,128)S(1)}, u32[]{:S(2)}, u32[]{:S(2)}) collective-permute-start(f32[256,128]{1,0:T(8,128)} %get-tuple-element.38), channel_id=1, source_target_pairs={{0,1},{1,0},{2,3},{3,2},{4,5},{5,4},{6,7},{7,6},{8,9},{9,8},{10,11... | collective-permute-start | bytes 393224 | tf_op jit(solution)/shard_map/ppermute | solution.py:763
  48.4 8.3 %collective-permute-start.8 = (bf16[256,512]{1,0:T(8,128)(2,1)}, bf16[256,512]{1,0:T(8,128)(2,1)}, u32[]{:S(2)}, u32[]{:S(2)}) collective-permute-start(bf16[256,512]{1,0:T(8,128)(2,1)} %get-tuple-element.39), channel_id=1, source_target_pairs={{0,4},{1,5},{2,6},{3,7},{4,8},{5,9},{6,10},{7,11},{8,12},{9,13},{1... | collective-permute-start | bytes 786440 | tf_op jit(solution)/shard_map/ppermute | solution.py:769
  49.7 7.0 %collective-permute-start.9 = (bf16[256,512]{1,0:T(8,128)(2,1)}, bf16[256,512]{1,0:T(8,128)(2,1)}, u32[]{:S(2)}, u32[]{:S(2)}) collective-permute-start(bf16[256,512]{1,0:T(8,128)(2,1)} %get-tuple-element.40), channel_id=1, source_target_pairs={{0,12},{1,13},{2,14},{3,15},{4,0},{5,1},{6,2},{7,3},{8,4},{9,5},{1... | collective-permute-start | bytes 786440 | tf_op jit(solution)/shard_map/ppermute | solution.py:769
  51.3 5.4 %collective-permute-start.2 = (f32[256,128]{1,0:T(8,128)S(1)}, f32[256,128]{1,0:T(8,128)S(1)}, u32[]{:S(2)}, u32[]{:S(2)}) collective-permute-start(f32[256,128]{1,0:T(8,128)S(1)} %add.15), channel_id=1, source_target_pairs={{0,2},{1,3},{2,0},{3,1},{4,6},{5,7},{6,4},{7,5},{8,10},{9,11},{10,... | collective-permute-start | bytes 393224 | tf_op jit(solution)/shard_map/ppermute | solution.py:766
  56.7 42.3 %all-to-all-start.2 = ((bf16[8,84,16,128]{3,2,1,0:T(8,128)(2,1)}), bf16[8,84,16,128]{3,2,1,0:T(8,128)(2,1)S(1)}, u32[]{:S(2)}, u32[]{:S(2)}) async-start(bf16[8,84,16,128]{3,2,1,0:T(8,128)(2,1)} %get-tuple-element.42), calls=%async_computation.2 | async-start | bytes 5505024 | tf_op jit(solution)/shard_map/all_to_all | solution.py:772
  60.4 13.8 %collective-permute-start.15 = (bf16[512,512]{1,0:T(8,128)(2,1)}, bf16[512,512]{1,0:T(8,128)(2,1)S(1)}, u32[]{:S(2)}, u32[]{:S(2)}) collective-permute-start(bf16[512,512]{1,0:T(8,128)(2,1)} %collective-permute-done.3.refs_0_), channel_id=1, source_target_pairs={{0,12},{1,13},{2,14},{3,15},{4,0},{5,1},{6,2},{7,3},{8,4},{9,5},{1... | collective-permute-start | bytes 1572872 | tf_op jit(solution)/shard_map/ppermute | solution.py:769
  63.0 12.3 %collective-permute-start.14 = (bf16[512,512]{1,0:T(8,128)(2,1)}, bf16[512,512]{1,0:T(8,128)(2,1)S(1)}, u32[]{:S(2)}, u32[]{:S(2)}) collective-permute-start(bf16[512,512]{1,0:T(8,128)(2,1)} %collective-permute-done.3.refs_0_), channel_id=1, source_target_pairs={{0,4},{1,5},{2,6},{3,7},{4,8},{5,9},{6,10},{7,11},{8,12},{9,13},{1... | collective-permute-start | bytes 1572872 | tf_op jit(solution)/shard_map/ppermute | solution.py:769
  63.0 17.7 %collective-permute-start.12 = (f32[256,128]{1,0:T(8,128)S(1)}, f32[256,128]{1,0:T(8,128)S(1)}, u32[]{:S(2)}, u32[]{:S(2)}) collective-permute-start(f32[256,128]{1,0:T(8,128)S(1)} %add.16), channel_id=1, source_target_pairs={{0,12},{1,13},{2,14},{3,15},{4,0},{5,1},{6,2},{7,3},{8,4},{9,5},{1... | collective-permute-start | bytes 393224 | tf_op jit(solution)/shard_map/ppermute | solution.py:769
  65.6 15.0 %collective-permute-start.11 = (f32[256,128]{1,0:T(8,128)S(1)}, f32[256,128]{1,0:T(8,128)}, u32[]{:S(2)}, u32[]{:S(2)}) collective-permute-start(f32[256,128]{1,0:T(8,128)S(1)} %add.16), channel_id=1, source_target_pairs={{0,4},{1,5},{2,6},{3,7},{4,8},{5,9},{6,10},{7,11},{8,12},{9,13},{1... | collective-permute-start | bytes 393224 | tf_op jit(solution)/shard_map/ppermute | solution.py:769
  65.6 15.0 %collective-permute-start.10 = (f32[256,128]{1,0:T(8,128)S(1)}, f32[256,128]{1,0:T(8,128)}, u32[]{:S(2)}, u32[]{:S(2)}) collective-permute-start(f32[256,128]{1,0:T(8,128)S(1)} %add.16), channel_id=1, source_target_pairs={{0,8},{1,9},{2,10},{3,11},{4,12},{5,13},{6,14},{7,15},{8,0},{9,1},... | collective-permute-start | bytes 393224 | tf_op jit(solution)/shard_map/ppermute | solution.py:769
  74.2 1.1 copy-start.3
  77.9 11.8 %collective-permute-start.16 = (bf16[256,512]{1,0:T(8,128)(2,1)}, bf16[256,512]{1,0:T(8,128)(2,1)S(1)}, u32[]{:S(2)}, u32[]{:S(2)}) collective-permute-start(bf16[256,512]{1,0:T(8,128)(2,1)} %get-tuple-element.44), channel_id=1, source_target_pairs={{0,4},{1,5},{2,6},{3,7},{4,8},{5,9},{6,10},{7,11},{8,12},{9,13},{1... | collective-permute-start | bytes 786440 | tf_op jit(solution)/shard_map/ppermute | solution.py:769
  79.1 10.6 %collective-permute-start.17 = (bf16[256,512]{1,0:T(8,128)(2,1)}, bf16[256,512]{1,0:T(8,128)(2,1)S(1)}, u32[]{:S(2)}, u32[]{:S(2)}) collective-permute-start(bf16[256,512]{1,0:T(8,128)(2,1)} %get-tuple-element.45), channel_id=1, source_target_pairs={{0,12},{1,13},{2,14},{3,15},{4,0},{5,1},{6,2},{7,3},{8,4},{9,5},{1... | collective-permute-start | bytes 786440 | tf_op jit(solution)/shard_map/ppermute | solution.py:769
  81.7 17.3 %copy-start.10 = (bf16[256,128]{1,0:T(8,128)(2,1)}, bf16[256,128]{1,0:T(8,128)(2,1)S(1)}, u32[]{:S(2)}) copy-start(bf16[256,128]{1,0:T(8,128)(2,1)S(1)} %add_convert_fusion.mine_hbm) | copy-start | bytes 196612
  81.7 8.0 %collective-permute-start.13 = (bf16[256,128]{1,0:T(8,128)(2,1)S(1)}, bf16[256,128]{1,0:T(8,128)(2,1)S(1)}, u32[]{:S(2)}, u32[]{:S(2)}) collective-permute-start(bf16[256,128]{1,0:T(8,128)(2,1)S(1)} %add_convert_fusion.mine_hbm), channel_id=1, source_target_pairs={{0,1},{1,0},{2,3},{3,2},{4,5},{5,4},{6,7},{7,6},{8,9},{9,8},{10,11... | collective-permute-start | bytes 196616 | tf_op jit(solution)/shard_map/ppermute | solution.py:763
  89.7 0.8 copy-start.7
  99.0 2.5 %copy-start = (bf16[8,84,16,128]{3,2,1,0:T(8,128)(2,1)}, bf16[8,84,16,128]{3,2,1,0:T(8,128)(2,1)S(1)}, u32[]{:S(2)}) copy-start(bf16[8,84,16,128]{3,2,1,0:T(8,128)(2,1)S(1)} %all-to-all-done.2.far_hbm.got_hbm) | copy-start | bytes 8257540
  99.0 10.0 %collective-permute-start.20 = (bf16[8,84,16,128]{3,2,1,0:T(8,128)(2,1)S(1)}, bf16[8,84,16,128]{3,2,1,0:T(8,128)(2,1)}, u32[]{:S(2)}, u32[]{:S(2)}) collective-permute-start(bf16[8,84,16,128]{3,2,1,0:T(8,128)(2,1)S(1)} %all-to-all-done.2.far_hbm.got_hbm), channel_id=1, source_target_pairs={{0,1},{1,0},{2,3},{3,2},{4,5},{5,4},{6,7},{7,6},{8,9},{9,8},{10,11... | collective-permute-start | bytes 8257544 | tf_op jit(solution)/shard_map/ppermute | solution.py:763
  101.4 7.2 %collective-permute-start.18 = (f32[512,768]{1,0:T(8,128)}, f32[512,768]{1,0:T(8,128)}, u32[]{:S(2)}, u32[]{:S(2)}) collective-permute-start(f32[512,768]{1,0:T(8,128)} %get-tuple-element.52.far_hbm), channel_id=1, source_target_pairs={{0,1},{1,0},{2,3},{3,2},{4,5},{5,4},{6,7},{7,6},{8,9},{9,8},{10,11... | collective-permute-start | bytes 4718600 | tf_op jit(solution)/shard_map/ppermute | solution.py:763
  105.6 3.4 %collective-permute-start.19 = (f32[512,128]{1,0:T(8,128)}, f32[512,128]{1,0:T(8,128)S(1)}, u32[]{:S(2)}, u32[]{:S(2)}) collective-permute-start(f32[512,128]{1,0:T(8,128)} %get-tuple-element.53.kv_hbm), channel_id=1, source_target_pairs={{0,1},{1,0},{2,3},{3,2},{4,5},{5,4},{6,7},{7,6},{8,9},{9,8},{10,11... | collective-permute-start | bytes 786440 | tf_op jit(solution)/shard_map/ppermute | solution.py:763
  (4 other events, 2.9 us)
